TPU v7x, 32 devices: a whole 2x2x4 slice. The times are simulated.
32 devices in a mesh: rows: 8 (over y, x, core), seq: 4 (over z).
Axes of the slice: x: 2, y: 2, z: 4, core: 2. Of those that a mesh axis runs over, the one named last changes fastest.
Arguments:
- tokens: bfloat16 [96, 512, 384], P('rows', 'seq'), may hold values from -6 to 6
- lengths: int32 [96, 8], P('rows'), may hold values from 1 to 505, as said below
- w_query: bfloat16 [384, 384], replicated, may hold values from -0.3125 to 0.3125
- b_query: float32 [384], replicated, may hold values from -3 to 3
- w_key: bfloat16 [384, 384], replicated, may hold values from -0.3125 to 0.3125
- w_value: bfloat16 [384, 384], replicated, may hold values from -0.3125 to 0.3125
- b_value: float32 [384], replicated, may hold values from -3 to 3
- w_out: bfloat16 [384, 384], replicated, may hold values from -3.5 to 3.5
- b_out: float32 [384], replicated, may hold values from -3 to 3
- gain_attn: float32 [384], replicated, may hold values from 0.5 to 1.5
- shift_attn: float32 [384], replicated, may hold values from -3 to 3
- w_up: bfloat16 [384, 1536], replicated, may hold values from -0.3125 to 0.3125
- b_up: float32 [1536], replicated, may hold values from -3 to 3
- w_down: bfloat16 [1536, 384], replicated, may hold values from -0.15625 to 0.15625
- b_down: float32 [384], replicated, may hold values from -3 to 3
- gain_ffn: float32 [384], replicated, may hold values from 0.5 to 1.5
- shift_ffn: float32 [384], replicated, may hold values from -3 to 3
- cotangent: bfloat16 [96, 512, 384], P('rows', 'seq'), may hold values from -6 to 6
Outputs:
- layer_out: bfloat16 [96, 512, 384], P('rows', 'seq')
- grad_tokens: float32 [96, 512, 384], P('rows', 'seq')
- grad_query: float32 [384, 384], replicated
- grad_qbias: float32 [384], replicated
- grad_key: float32 [384, 384], replicated
- grad_value: float32 [384, 384], replicated
- grad_vbias: float32 [384], replicated
- grad_output: float32 [384, 384], replicated
- grad_obias: float32 [384], replicated
- grad_gain1: float32 [384], replicated
- grad_shift1: float32 [384], replicated
- grad_up: float32 [384, 1536], replicated
- grad_upbias: float32 [1536], replicated
- grad_down: float32 [1536, 384], replicated
- grad_dnbias: float32 [384], replicated
- grad_gain2: float32 [384], replicated
- grad_shift2: float32 [384], replicated
Inputs may be any that keep to these rules, and one draw needn't show every extreme that they name: Each row's 8 lengths sum to 512; in every row one pair starts within the first 128 positions and ends within the last 128.
All inputs are finite; a program needn't handle non-finite values.
Results may differ from a plain program's by a relative error of at most 0.014.
Values may be sent and summed in bfloat16 or wider, within the bound.
No kernel may reach another device: no remote copies, remote signals or barrier semaphores. Data moves between devices by JAX's collectives and lax.ppermute only.
A program may use at most 192 MiB of HBM per device.

v0:
```python
import jax
import jax.numpy as jnp
from jax import lax
from jax.sharding import PartitionSpec as P

HEADS = 12
HD = 32


MASKED = -1e30
EPSILON = 1e-05


def project(operand, weight):
    return jnp.einsum("rsd,de->rse", operand, weight, preferred_element_type=jnp.float32)


def project_back(operand, weight):
    return jnp.einsum("rse,de->rsd", operand, weight, preferred_element_type=jnp.float32)


def weight_grad(operand, upstream):
    return jnp.einsum("rsd,rse->de", operand, upstream, preferred_element_type=jnp.float32)


def column_sum(values):
    return jnp.sum(values.astype(jnp.float32), axis=(0, 1))


def normalize(hidden):
    centre = hidden - jnp.mean(hidden, axis=-1, keepdims=True)
    inverse = lax.rsqrt(jnp.mean(centre * centre, axis=-1, keepdims=True) + EPSILON)
    return (centre * inverse, inverse)


def normalize_back(upstream, scaled, inverse):
    spread = jnp.mean(upstream * scaled, axis=-1, keepdims=True)
    return inverse * (upstream - jnp.mean(upstream, axis=-1, keepdims=True) - scaled * spread)


def exact_gelu(values):
    return jax.nn.gelu(values, approximate=False)


def segment_ids(bounds, offset, extent):
    places = offset + jnp.arange(extent, dtype=jnp.int32)
    return jnp.sum((places[None, :, None] >= bounds[:, None, :]).astype(jnp.int32), axis=-1)


def row_scores(query_row, key_row, query_seg, key_seg):
    query_len = query_row.shape[0]
    key_len = key_row.shape[0]
    logits = jnp.einsum(
        "shd,nhd->hsn",
        query_row.reshape(query_len, HEADS, HD),
        key_row.reshape(key_len, HEADS, HD),
        preferred_element_type=jnp.float32,
    ) * HD ** (-0.5)
    matching = query_seg[:, None] == key_seg[None, :]
    return jnp.where(matching[None], logits, MASKED)


def stats_row(packed):
    query_row, key_row, query_seg, key_seg, running_max, running_sum = packed
    logits = row_scores(query_row, key_row, query_seg, key_seg)
    new_max = jnp.maximum(running_max, jnp.max(logits, axis=-1))
    new_sum = running_sum * jnp.exp(running_max - new_max) + jnp.sum(
        jnp.exp(logits - new_max[:, :, None]), axis=-1
    )
    return (new_max, new_sum)


def output_row(packed):
    query_row, key_row, value_row, query_seg, key_seg, log_total = packed
    key_len = key_row.shape[0]
    logits = row_scores(query_row, key_row, query_seg, key_seg)
    probs = jnp.exp(logits - log_total.T[:, :, None])
    value_heads = value_row.reshape(key_len, HEADS, HD)
    mixed = jnp.einsum(
        "hsn,nhd->shd", probs.astype(jnp.bfloat16), value_heads, preferred_element_type=jnp.float32
    )
    exact = jnp.einsum(
        "hsn,nhd->shd", probs, value_heads.astype(jnp.float32), precision=lax.Precision.HIGHEST
    )
    return (mixed.reshape(query_row.shape[0], -1), exact.reshape(query_row.shape[0], -1))


def backward_row(packed):
    query_row, key_row, value_row, query_seg, key_seg, log_total, row_delta, out_grad = packed
    query_len = query_row.shape[0]
    key_len = key_row.shape[0]
    logits = row_scores(query_row, key_row, query_seg, key_seg)
    probs = jnp.exp(logits - log_total.T[:, :, None])
    query_heads = query_row.reshape(query_len, HEADS, HD)
    key_heads = key_row.reshape(key_len, HEADS, HD)
    value_heads = value_row.reshape(key_len, HEADS, HD)
    grad_heads = out_grad.reshape(query_len, HEADS, HD)
    grad_probs = jnp.einsum(
        "shd,nhd->hsn", grad_heads, value_heads, preferred_element_type=jnp.float32
    )
    grad_logits = (probs * (grad_probs - row_delta.T[:, :, None])).astype(jnp.bfloat16)
    factor = HD ** (-0.5)
    part_query = (
        jnp.einsum("hsn,nhd->shd", grad_logits, key_heads, preferred_element_type=jnp.float32)
        * factor
    )
    part_key = (
        jnp.einsum("hsn,shd->nhd", grad_logits, query_heads, preferred_element_type=jnp.float32)
        * factor
    )
    part_value = jnp.einsum(
        "hsn,shd->nhd", probs.astype(jnp.bfloat16), grad_heads, preferred_element_type=jnp.float32
    )
    return (
        part_query.reshape(query_len, -1),
        part_key.reshape(key_len, -1),
        part_value.reshape(key_len, -1),
    )


def projections(tokens, w_query, b_query, w_key, w_value, b_value):
    query_b = (project(tokens, w_query) + b_query).astype(jnp.bfloat16)
    key_b = project(tokens, w_key).astype(jnp.bfloat16)
    value_b = (project(tokens, w_value) + b_value).astype(jnp.bfloat16)
    return (query_b, key_b, value_b)


def start_stats(row_count, span):
    return (
        jnp.full((row_count, HEADS, span), MASKED, jnp.float32),
        jnp.zeros((row_count, HEADS, span), jnp.float32),
    )


def dense_part(
    tokens,
    attended,
    exact_mix,
    cotangent,
    w_out,
    b_out,
    gain_attn,
    shift_attn,
    w_up,
    b_up,
    w_down,
    b_down,
    gain_ffn,
    shift_ffn,
):
    row_count, span, width = tokens.shape
    attended_b = attended.astype(jnp.bfloat16)
    residual_one = tokens.astype(jnp.float32) + project(attended_b, w_out) + b_out
    scaled_one, inverse_one = normalize(residual_one)
    normed = scaled_one * gain_attn + shift_attn
    normed_b = normed.astype(jnp.bfloat16)
    upward = project(normed_b, w_up) + b_up
    activated, gelu_pull = jax.vjp(exact_gelu, upward)
    activated_b = activated.astype(jnp.bfloat16)
    residual_two = normed + project(activated_b, w_down) + b_down
    scaled_two, inverse_two = normalize(residual_two)
    layer_out = (scaled_two * gain_ffn + shift_ffn).astype(jnp.bfloat16)
    grad_layer = cotangent.astype(jnp.float32)
    grad_gain2 = jnp.sum(grad_layer * scaled_two, axis=(0, 1))
    grad_shift2 = jnp.sum(grad_layer, axis=(0, 1))
    grad_res2 = normalize_back(grad_layer * gain_ffn, scaled_two, inverse_two)
    down_b = grad_res2.astype(jnp.bfloat16)
    grad_down = weight_grad(activated_b, down_b)
    grad_dnbias = column_sum(down_b)
    (grad_upward,) = gelu_pull(project_back(down_b, w_down))
    up_b = grad_upward.astype(jnp.bfloat16)
    grad_up = weight_grad(normed_b, up_b)
    grad_upbias = column_sum(up_b)
    grad_normed = grad_res2 + project_back(up_b, w_up)
    grad_gain1 = jnp.sum(grad_normed * scaled_one, axis=(0, 1))
    grad_shift1 = jnp.sum(grad_normed, axis=(0, 1))
    grad_res1 = normalize_back(grad_normed * gain_attn, scaled_one, inverse_one)
    branch_b = grad_res1.astype(jnp.bfloat16)
    grad_output = weight_grad(attended_b, branch_b)
    grad_obias = column_sum(branch_b)
    out_grad_b = project_back(branch_b, w_out).astype(jnp.bfloat16)
    row_delta = jnp.sum(
        (out_grad_b.astype(jnp.float32) * exact_mix).reshape(row_count, span, HEADS, HD), axis=-1
    )
    later_grads = (
        grad_output,
        grad_obias,
        grad_gain1,
        grad_shift1,
        grad_up,
        grad_upbias,
        grad_down,
        grad_dnbias,
        grad_gain2,
        grad_shift2,
    )
    return (layer_out, grad_res1, out_grad_b, row_delta, later_grads)


def input_part(tokens, grad_res1, query_sum, key_sum, value_sum, w_query, w_key, w_value):
    query_gb = query_sum.astype(jnp.bfloat16)
    key_gb = key_sum.astype(jnp.bfloat16)
    value_gb = value_sum.astype(jnp.bfloat16)
    grad_tokens = (
        grad_res1
        + project_back(query_gb, w_query)
        + project_back(key_gb, w_key)
        + project_back(value_gb, w_value)
    )
    first_grads = (
        weight_grad(tokens, query_gb),
        column_sum(query_gb),
        weight_grad(tokens, key_gb),
        weight_grad(tokens, value_gb),
        column_sum(value_gb),
    )
    return (grad_tokens, first_grads)


def body(
    tokens,
    lengths,
    w_query,
    b_query,
    w_key,
    w_value,
    b_value,
    w_out,
    b_out,
    gain_attn,
    shift_attn,
    w_up,
    b_up,
    w_down,
    b_down,
    gain_ffn,
    shift_ffn,
    cotangent,
):
    dense_weights = (
        w_out,
        b_out,
        gain_attn,
        shift_attn,
        w_up,
        b_up,
        w_down,
        b_down,
        gain_ffn,
        shift_ffn,
    )
    row_count, seq_span, width = tokens.shape
    offset = lax.axis_index("seq") * seq_span
    bounds = jnp.cumsum(lengths, axis=1)
    query_seg = segment_ids(bounds, offset, seq_span)
    query_b, key_b, value_b = projections(tokens, w_query, b_query, w_key, w_value, b_value)
    pieces = lax.all_gather(key_b, "seq", axis=1, tiled=True)
    running_max, running_sum = start_stats(row_count, seq_span)
    piece_seg = segment_ids(bounds, jnp.int32(0), pieces.shape[1])
    running_max, running_sum = lax.map(
        stats_row, (query_b, pieces, query_seg, piece_seg, running_max, running_sum)
    )
    log_total = (running_max + jnp.log(running_sum)).transpose(0, 2, 1)
    key_piece = lax.all_gather(key_b, "seq", axis=1, tiled=True)
    value_piece = lax.all_gather(value_b, "seq", axis=1, tiled=True)
    piece_seg = segment_ids(bounds, jnp.int32(0), key_piece.shape[1])
    mixed, exact = lax.map(
        output_row, (query_b, key_piece, value_piece, query_seg, piece_seg, log_total)
    )
    layer_out, grad_res1, out_grad_b, row_delta, later_grads = dense_part(
        tokens, mixed, exact, cotangent, *dense_weights
    )
    key_piece = lax.all_gather(key_b, "seq", axis=1, tiled=True)
    value_piece = lax.all_gather(value_b, "seq", axis=1, tiled=True)
    piece_seg = segment_ids(bounds, jnp.int32(0), key_piece.shape[1])
    part_query, part_key, part_value = lax.map(
        backward_row,
        (query_b, key_piece, value_piece, query_seg, piece_seg, log_total, row_delta, out_grad_b),
    )
    key_sum, value_sum = (
        lax.psum_scatter(part_key, "seq", scatter_dimension=1, tiled=True),
        lax.psum_scatter(part_value, "seq", scatter_dimension=1, tiled=True),
    )
    grad_tokens, first_grads = input_part(
        tokens, grad_res1, part_query, key_sum, value_sum, w_query, w_key, w_value
    )
    partial_grads = first_grads + later_grads
    summed = lax.psum(partial_grads, ("rows", "seq"))
    return (layer_out, grad_tokens) + tuple(summed)


def solution(mesh):
    in_specs = (
        P("rows", "seq", None),
        P("rows", None),
        P(),
        P(),
        P(),
        P(),
        P(),
        P(),
        P(),
        P(),
        P(),
        P(),
        P(),
        P(),
        P(),
        P(),
        P(),
        P("rows", "seq", None),
    )
    out_specs = (
        P("rows", "seq", None),
        P("rows", "seq", None),
        P(),
        P(),
        P(),
        P(),
        P(),
        P(),
        P(),
        P(),
        P(),
        P(),
        P(),
        P(),
        P(),
        P(),
        P(),
    )
    return jax.shard_map(body, mesh=mesh, in_specs=in_specs, out_specs=out_specs, check_vma=False)
```

profile of v0, /device:TPU:0, one launch (start us, length us, event | category | flops | bytes accessed | tf_op | source)
XLA Modules:
  0.0 1008.9 jit_solution(3096809662367498733)
XLA Ops:
  7.3 3.3 convolution_convert_fusion.1
  16.8 86.2 %all-gather.5.cloned.1.call-done = bf16[12,512,384]{2,1,0:T(8,128)(2,1)} async-done(((bf16[12,128,384]{2,1,0:T(8,128)(2,1)}), bf16[12,512,384]{2,1,0:T(8,128)(2,1)}) %all-gather.5.cloned.1.call-update) | async-done | bytes 4718608 | tf_op jit(solution)/shard_map/all_gather | solution.py:264
  102.9 6.7 copy.84
  109.6 35.5 %while.38 = (s32[]{:T(128)}, f32[12,12,128]{2,1,0:T(8,128)S(1)}, f32[12,12,128]{2,1,0:T(8,128)S(1)}, s32[12,128]{1,0:T(8,128)S(1)}, s32[12,512]{1,0:T(8,128)S(1)...) while((s32[]{:T(128)}, f32[12,12,128]{2,1,0:T(8,128)S(1)}, ...), condition=%wide.region_6.7_spmd, body=%wide.region_3.6_spmd.sunk | while | flops 55906816 | bytes 8033905 | solution.py:260
  145.2 47.8 %all-gather.3.cloned.1.call-done = bf16[12,512,384]{2,1,0:T(8,128)(2,1)} async-done(((bf16[12,128,384]{2,1,0:T(8,128)(2,1)}), bf16[12,512,384]{2,1,0:T(8,128)(2,1)}) %all-gather.3.cloned.1.call-update) | async-done | bytes 4718608 | tf_op jit(solution)/shard_map/all_gather | solution.py:265
  192.9 6.7 copy.82
  200.8 81.0 %while.39 = (s32[]{:T(128)}, bf16[12,128,384]{1,2,0:T(8,128)(2,1)}, f32[12,128,384]{2,1,0:T(8,128)}, bf16[12,512,384]{1,2,0:T(8,128)(2,1)}, s32[12,128]{1,0:T(8,...) while((s32[]{:T(128)}, bf16[12,128,384]{1,2,0:T(8,128)(2,1)}, ...), condition=%wide.region_8.9_spmd, body=%wide.region_7.8_spmd.sunk | while | flops 408223744 | bytes 13991561 | solution.py:267
  223.9 2.4 fusion.149
  264.3 2.4 fusion.149
  271.1 2.4 fusion.149
  284.7 2.8 fusion.72
  288.2 5.0 fusion.33
  293.2 22.7 %multiply_convert_fusion.1 = (bf16[12,128,1536]{2,1,0:T(8,128)(2,1)S(1)}, f32[12,128,1536]{2,1,0:T(8,128)}) fusion(f32[12,128,1536]{2,1,0:T(8,128)S(1)} %get-tuple-element.409, f32[1536]{0:T(1024)S(1)} %copy-done.33, u16[128,1536]{1,0:T(8,128)(2,1)S(1)} %get-tuple-element.310, u16[128,1536]{1,0:T(8,128)(2,1)S(1)} %get-tuple-element.309), kind=kLoop, calls=%fused_computation.70 | loop fusion | flops 167510016 | bytes 24385536 | tf_op jit(solution)/shard_map/convert_element_type | solution.py:159
  315.9 3.1 fusion.73
  322.2 2.9 convert_reduce_fusion.2
  325.1 9.0 convert_reduce_fusion
  334.1 4.4 multiply_reduce_fusion
  341.0 2.7 convert_multiply_fusion.2
  343.7 3.0 copy.87
  350.0 141.3 %while.40 = (s32[]{:T(128)}, bf16[12,128,384]{1,2,0:T(8,128)(2,1)}, f32[12,512,384]{1,2,0:T(8,128)}, f32[12,512,384]{1,2,0:T(8,128)}, bf16[12,512,384]{1,2,0:T(8...) while((s32[]{:T(128)}, bf16[12,128,384]{1,2,0:T(8,128)(2,1)}, ...), condition=%wide.region_19.20_spmd, body=%wide.region_18.19_spmd.sunk | while | flops 259883008 | bytes 23152296 | solution.py:276
  492.3 3.4 convolution_bitcast_fusion.2
  497.2 6.8 convolution_bitcast_fusion
  504.1 3.7 convolution_bitcast_fusion.1
  507.8 143.4 %reduce-scatter.3.cloned.1.call-done = f32[12,128,384]{1,2,0:T(8,128)} async-done(((f32[12,512,384]{1,2,0:T(8,128)}), f32[12,128,384]{1,2,0:T(8,128)}) %reduce-scatter.3.cloned.1.call-update) | async-done | bytes 2359312 | tf_op jit(solution)/shard_map/reduce_scatter | solution.py:281
  651.2 3.3 convolution_bitcast_fusion.4
  654.5 161.1 %reduce-scatter.5.cloned.1.call-done = f32[12,128,384]{1,2,0:T(8,128)} async-done(((f32[12,512,384]{1,2,0:T(8,128)}), f32[12,128,384]{1,2,0:T(8,128)}) %reduce-scatter.5.cloned.1.call-update) | async-done | bytes 2359312 | tf_op jit(solution)/shard_map/reduce_scatter | solution.py:282
  815.6 3.3 convolution_bitcast_fusion.3
  820.9 3.3 fusion.57
  825.0 43.5 %all-reduce = (f32[384]{0:T(512)}, f32[384]{0:T(512)}, f32[384]{0:T(512)}, f32[384]{0:T(512)}, f32[384]{0:T(512)}, /*index=5*/f32[1536]{0:T(1024)}, f32[384]{0:T(512)}, f32[384]{0:T(512)}, f32[384]{0:T(512)}) all-reduce(f32[384]{0:T(512)S(1)} %copy-done.38, ...), channel_id=1, replica_groups=mesh['rows'=8,'seq'=4] {'rows','seq'}, use_global_device_ids=true, to_apply=%region_24.25 | all-reduce | flops 4608 | bytes 36864 | tf_op jit(solution)/shard_map/psum | solution.py:288
  868.5 2.8 fusion.49
  871.6 4.3 add_add_fusion
  875.9 115.8 %all-reduce.4.cloned.1.call-done = (f32[384,384]{0,1:T(8,128)}, f32[384,384]{0,1:T(8,128)}, f32[384,384]{0,1:T(8,128)}, f32[384,384]{1,0:T(8,128)}, f32[384,1536]{1,0:T(8,128)}, /*index=5*/f32[1536,384]{1,0:T(8,128)}) async-done(((f32[384,384]{0,1:T(8,128)}, f32[384,384]{0,1:T(8,128)}, f32[384,384]{0,1:T(8,128)}, f32[384,384]{1,0:T(8,128)}, f32[384,1536]{1,0:T(8,128)}, /*index=5*/f32[1536,384]{1,0:T(8,128)}), ...) | async-done | bytes 7077904 | tf_op jit(solution)/shard_map/psum | solution.py:288
  (605 shorter events, 284.3 us)
Async XLA Ops:
  7.2 280.9 %copy-start = (bf16[384,1536]{1,0:T(8,128)(2,1)S(1)}, bf16[384,1536]{1,0:T(8,128)(2,1)}, u32[]{:S(2)}) copy-start(bf16[384,1536]{1,0:T(8,128)(2,1)} %param.35) | copy-start | bytes 3538948
  7.2 3.5 copy-start.4
  7.2 3.5 copy-start.25
  7.2 3.5 copy-start.50
  7.2 95.7 %all-gather.5.cloned.1.call-start = ((), (), s32[]{:S(2)}) async-start(), calls=%async_computation.3 | async-start | bytes 5898240 | tf_op jit(solution)/shard_map/all_gather | solution.py:264
  10.7 182.2 %all-gather.3.cloned.1.call-start = ((), (), s32[]{:S(2)}) async-start(), calls=%async_computation.2 | async-start | bytes 5898240 | tf_op jit(solution)/shard_map/all_gather | solution.py:265
  12.7 638.5 %reduce-scatter.3.cloned.1.call-start = ((), (), s32[]{:S(2)}) async-start(), calls=%async_computation.4 | async-start | bytes 11796480 | tf_op jit(solution)/shard_map/reduce_scatter | solution.py:281
  200.8 83.9 %copy-start.45 = (f32[384]{0:T(512)S(1)}, f32[384]{0:T(512)}, u32[]{:S(2)}) copy-start(f32[384]{0:T(512)} %param.32) | copy-start | bytes 4612
  293.2 22.7 %copy-start.49 = (bf16[1536,384]{1,0:T(8,128)(2,1)S(1)}, bf16[1536,384]{1,0:T(8,128)(2,1)}, u32[]{:S(2)}) copy-start(bf16[1536,384]{1,0:T(8,128)(2,1)} %param.37) | copy-start | bytes 3538948
  293.2 22.7 %copy-start.52 = (f32[384]{0:T(512)S(1)}, f32[384]{0:T(512)}, u32[]{:S(2)}) copy-start(f32[384]{0:T(512)} %param.38) | copy-start | bytes 4612
  325.1 9.0 copy-start.19
  334.1 4.4 copy-start.55
  340.1 3.6 copy-start.11
  491.3 324.2 %reduce-scatter.5.cloned.1.call-start = ((), (), s32[]{:S(2)}) async-start(), calls=%async_computation.5 | async-start | bytes 11796480 | tf_op jit(solution)/shard_map/reduce_scatter | solution.py:282
  491.9 3.7 copy-start.5
  491.9 499.8 %all-reduce.4.cloned.1.call-start = ((), (), s32[]{:S(2)}) async-start(), calls=%async_computation.6 | async-start | bytes 14155776 | tf_op jit(solution)/shard_map/psum | solution.py:288
  492.2 3.4 copy-start.6
  492.2 5.0 copy-start.20
  495.6 8.4 slice-start
  497.2 6.9 copy-start.42
  497.2 6.9 copy-start.54
  497.2 6.9 slice-start.1
  820.1 4.1 copy-start.2
  824.3 44.2 %copy-start.18 = (bf16[384,384]{1,0:T(8,128)(2,1)S(1)}, bf16[384,384]{1,0:T(8,128)(2,1)}, u32[]{:S(2)}) copy-start(bf16[384,384]{1,0:T(8,128)(2,1)} %param.28) | copy-start | bytes 884740
  824.3 47.0 %copy-start.29 = (f32[12,128]{1,0:T(8,128)S(1)}, f32[12,128]{1,0:T(8,128)}, u32[]{:S(2)}) copy-start(f32[12,128]{1,0:T(8,128)} %copy-done.28) | copy-start | bytes 18436
  824.3 47.0 %copy-start.31 = (f32[12,128]{1,0:T(8,128)S(1)}, f32[12,128]{1,0:T(8,128)}, u32[]{:S(2)}) copy-start(f32[12,128]{1,0:T(8,128)} %copy-done.30) | copy-start | bytes 18436
  824.3 47.0 %copy-start.43 = (f32[384]{0:T(512)S(1)}, f32[384]{0:T(512)}, u32[]{:S(2)}) copy-start(f32[384]{0:T(512)} %param.33) | copy-start | bytes 4612
  868.5 3.1 copy-start.26
  991.7 4.4 copy-start.22
  991.7 5.4 copy-start.21
  991.7 6.3 copy-start.16
  998.0 3.9 copy-start.1
  (31 other events, 45.9 us)
Sparse Core Ops, SparseCore 0:
  10.8 92.0 all-gather.4
  105.1 87.8 all-gather.2
  491.5 159.7 reduce-scatter.2
  653.4 162.0 reduce-scatter.4
  823.0 168.7 all-reduce.3
where the time goes:
time: 1020 us; the launch traced here: 1010 us
  waiting for transfers between devices  555 us (54%)
  local copies, waits for them, and re-layouts  176 us (17%)
  matrix products  169 us (17%)
  other arithmetic  48.6 us (5%)
  blocking collectives  43.5 us (4%)
  between operations  14.8 us (1%)
    reduce_scatter x1, waiting for transfers between devices, body(): lax.psum_scatter(part_value, 'seq', scatter_dimension=1, tiled=True)  161 us
    reduce_scatter x1, waiting for transfers between devices, body(): lax.psum_scatter(part_key, 'seq', scatter_dimension=1, tiled=True)  143 us
    psum x1, waiting for transfers between devices, body(): summed = lax.psum(partial_grads, ('rows', 'seq'))  116 us
    all_gather x1, waiting for transfers between devices, body(): key_piece = lax.all_gather(key_b, 'seq', axis=1, tiled=True)  86.2 us
    dynamic_slice x132, local copies, waits for them, and re-layouts, body(): lax.map(stats_row, (query_b, pieces, query_seg, piece_seg, running_max, r...  73 us
    all_gather x1, waiting for transfers between devices, body(): value_piece = lax.all_gather(value_b, 'seq', axis=1, tiled=True)  47.8 us
    psum x1, blocking collectives, body(): summed = lax.psum(partial_grads, ('rows', 'seq'))  43.5 us
    dot_general x12, matrix products, output_row(): jnp.einsum('hsn,nhd->shd', probs, value_heads.astype(jnp.float32), precis...  28.7 us
  transfers between devices with their start and end apart: 5, of which 5 were waited for; matrix products, arithmetic and copies ran while one was open for 8% of the time, Pallas kernels for 0%

commit v1 on v0

v1 whole, which is shorter than its diff:
```python
import functools
import math

import jax
import jax.numpy as jnp
from jax import lax
from jax.experimental import pallas as pl
from jax.experimental.pallas import tpu as pltpu
from jax.sharding import PartitionSpec as P

HEADS = 12
HD = 32
GROUPS = 3
PER_GROUP = HEADS // GROUPS
AUG = 16
BIG = 2.0**100
EPSILON = 1e-05
SCALE = HD ** (-0.5)
LOG2E = math.log2(math.e)
Q_FACTOR = SCALE * LOG2E
LN2 = math.log(2.0)
VMEM_LIMIT = 60 * 2**20

f32 = jnp.float32
bf16 = jnp.bfloat16
NN = (((1,), (0,)), ((), ()))
NT = (((1,), (1,)), ((), ()))
TN = (((0,), (0,)), ((), ()))


def dot(left, right, dims=NN):
    return lax.dot_general(left, right, dims, preferred_element_type=f32)


def fold_lanes(values):
    total = values[:, :128]
    for start in range(128, values.shape[1], 128):
        total = total + values[:, start : start + 128]
    return total


def row_sum(partial):
    return jnp.sum(partial.T, axis=0, keepdims=True)


def normalize(hidden):
    scale = 1.0 / hidden.shape[0]
    centre = hidden - jnp.sum(hidden, axis=0, keepdims=True) * scale
    variance = jnp.sum(centre * centre, axis=0, keepdims=True) * scale
    inverse = lax.rsqrt(variance + EPSILON)
    return centre * inverse, inverse


def normalize_back(upstream, scaled, inverse):
    scale = 1.0 / upstream.shape[0]
    mean = jnp.sum(upstream, axis=0, keepdims=True) * scale
    spread = jnp.sum(upstream * scaled, axis=0, keepdims=True) * scale
    return inverse * (upstream - mean - scaled * spread)


def gelu_parts(v):
    size = jnp.abs(v)
    t = 1.0 / (1.0 + (0.3275911 * 0.5**0.5) * size)
    bell = jnp.exp2((v * v) * (-0.5 * LOG2E))
    poly = 0.5 * 1.061405429
    for coefficient in (-1.453152027, 1.421413741, -0.284496736, 0.254829592):
        poly = poly * t + 0.5 * coefficient
    tail = poly * t * bell
    cdf = jnp.where(v < 0, tail, 1.0 - tail)
    slope = cdf + v * bell * (2.0 * math.pi) ** (-0.5)
    return v * cdf, slope


def attend_kernel(
    *refs, pieces, row_base
):
    x_refs = refs[:pieces]
    qaug_ref, kaug_ref, wq_ref, wk_ref, wv_ref, bq_ref, bv_ref = refs[pieces : pieces + 7]
    xt_ref, qt_ref, kt_ref, vt_ref, att_ref, inv_ref, p_ref = refs[pieces + 7 :]
    group = pl.program_id(1)

    @pl.when(group == 0)
    def _():
        xt = jnp.concatenate([ref[0].T for ref in x_refs], axis=1)
        xt_ref[0] = xt
        qt_ref[0] = ((dot(wq_ref[...], xt) + bq_ref[...]) * Q_FACTOR).astype(bf16)
        kt_ref[0] = dot(wk_ref[...], xt).astype(bf16)
        vt_ref[0] = (dot(wv_ref[...], xt) + bv_ref[...]).astype(bf16)

    length = xt_ref.shape[2]
    half = min(256, length)
    ones = jnp.ones((AUG, length), bf16)
    units = [(h, start) for h in range(PER_GROUP) for start in range(0, length, half)]
    keys, values = {}, {}

    def rows(ref, h):
        return ref[0, pl.ds(pl.multiple_of((group * PER_GROUP + h) * HD, HD), HD), :]

    def score(unit):
        h, start = unit
        if h not in keys:
            keys[h] = jnp.concatenate([rows(kt_ref, h), kaug_ref[0]], axis=0)
        query = jnp.concatenate([rows(qt_ref, h), qaug_ref[0]], axis=0)
        return dot(keys[h], query[:, start : start + half], TN)

    scores = score(units[0])
    for index, (h, start) in enumerate(units):
        following = score(units[index + 1]) if index + 1 < len(units) else None
        peak = jnp.max(scores, axis=0, keepdims=True)
        probs = jnp.exp2(scores - peak).astype(bf16)
        p_ref[0, h, :, start : start + half] = probs
        if h not in values:
            values[h] = jnp.concatenate([rows(vt_ref, h), ones], axis=0)
        mixed = dot(values[h], probs)
        inverse = 1.0 / mixed[HD : HD + 1]
        att_ref[0, pl.ds(pl.multiple_of((group * PER_GROUP + h) * HD, HD), HD), start : start + half] = (
            mixed[:HD] * inverse
        )
        inv_ref[0, 0, h : h + 1, start : start + half] = inverse
        scores = following


def attend(pieces, qaug, kaug, weights):
    rows, span, width = pieces[0].shape
    count = len(pieces)
    length = span * count
    wq, wk, wv, bq, bv = weights
    piece_spec = pl.BlockSpec((1, span, width), lambda r, g: (r, 0, 0))
    aug_spec = pl.BlockSpec((1, AUG, length), lambda r, g: (r, 0, 0))
    full = lambda a: pl.BlockSpec(a.shape, lambda r, g: (0, 0))
    wide = pl.BlockSpec((1, width, length), lambda r, g: (r, 0, 0))
    return pl.pallas_call(
        functools.partial(attend_kernel, pieces=count, row_base=0),
        grid=(rows, GROUPS),
        in_specs=[piece_spec] * count + [aug_spec] * 2 + [full(w) for w in weights],
        out_specs=[wide] * 5
        + [
            pl.BlockSpec((1, 1, 8, length), lambda r, g: (r, g, 0, 0)),
            pl.BlockSpec((1, PER_GROUP, length, length), lambda r, g: (r, g, 0, 0)),
        ],
        out_shape=[jax.ShapeDtypeStruct((rows, width, length), bf16)] * 4
        + [
            jax.ShapeDtypeStruct((rows, width, length), f32),
            jax.ShapeDtypeStruct((rows, GROUPS, 8, length), f32),
            jax.ShapeDtypeStruct((rows, HEADS, length, length), bf16),
        ],
        compiler_params=pltpu.CompilerParams(vmem_limit_bytes=VMEM_LIMIT),
        name="attend",
    )(*pieces, qaug, kaug, *weights)


def dense_kernel(*refs, pieces, rows):
    cot_refs = refs[:pieces]
    (
        xt_ref, att_ref, inv_ref, wo_t, wo, wup_t, wup, wdn_t, wdn, bo, gain1, shift1, bup, bdn, gain2, shift2,
    ) = refs[pieces : pieces + 16]
    lo_refs = refs[pieces + 16 : 2 * pieces + 16]
    gres_ref, og_ref, delta_ref, packed_ref = refs[2 * pieces + 16 : 2 * pieces + 20]
    acc_dn, acc_up, acc_out, acc_bias, acc_upb = refs[2 * pieces + 20 :]
    step = pl.program_id(0)
    span = cot_refs[0].shape[1]
    width = xt_ref.shape[1]

    @pl.when(step == 0)
    def _():
        for ref in (acc_dn, acc_up, acc_out, acc_bias, acc_upb):
            ref[...] = jnp.zeros_like(ref)

    att = att_ref[0]
    att_b = att.astype(bf16)
    res1 = xt_ref[0].astype(f32) + dot(wo_t[...], att_b) + bo[...]
    scaled1, inverse1 = normalize(res1)
    normed = scaled1 * gain1[...] + shift1[...]
    normed_b = normed.astype(bf16)
    upward = dot(wup_t[...], normed_b) + bup[...]
    act, slope = gelu_parts(upward)
    act_b = act.astype(bf16)
    res2 = normed + dot(wdn_t[...], act_b) + bdn[...]
    scaled2, inverse2 = normalize(res2)
    out = (scaled2 * gain2[...] + shift2[...]).astype(bf16)
    for index, ref in enumerate(lo_refs):
        ref[0] = out[:, index * span : (index + 1) * span].T
    cot = jnp.concatenate([ref[0].T for ref in cot_refs], axis=1).astype(f32)
    acc_bias[0] += fold_lanes(cot * scaled2)
    acc_bias[1] += fold_lanes(cot)
    gres2 = normalize_back(cot * gain2[...], scaled2, inverse2)
    down_b = gres2.astype(bf16)
    acc_bias[2] += fold_lanes(down_b.astype(f32))
    acc_dn[...] += dot(act_b, down_b, NT)
    up_b = (dot(wdn[...], down_b) * slope).astype(bf16)
    acc_upb[...] += fold_lanes(up_b.astype(f32))
    acc_up[...] += dot(normed_b, up_b, NT)
    gnormed = gres2 + dot(wup[...], up_b)
    acc_bias[3] += fold_lanes(gnormed * scaled1)
    acc_bias[4] += fold_lanes(gnormed)
    gres1 = normalize_back(gnormed * gain1[...], scaled1, inverse1)
    gres_ref[0] = gres1
    branch_b = gres1.astype(bf16)
    acc_bias[5] += fold_lanes(branch_b.astype(f32))
    acc_out[...] += dot(att_b, branch_b, NT)
    og = dot(wo[...], branch_b)
    for h in range(HEADS):
        part = slice(h * HD, (h + 1) * HD)
        scaled_og = (og[part] * inv_ref[0, h // PER_GROUP, h % PER_GROUP : h % PER_GROUP + 1, :]).astype(bf16)
        og_ref[0, part, :] = scaled_og
        delta_ref[0, h : h + 1, :] = jnp.sum(scaled_og.astype(f32) * att[part], axis=0, keepdims=True)

    @pl.when(step == rows - 1)
    def _():
        ff = acc_up.shape[1]
        packed_ref[:ff] = acc_dn[...].astype(bf16)
        for index in range(ff // width):
            packed_ref[ff + index * width : ff + (index + 1) * width] = acc_up[
                :, index * width : (index + 1) * width
            ].astype(bf16)
        packed_ref[2 * ff : 2 * ff + width] = acc_out[...].astype(bf16)
        bias_rows = [row_sum(acc_bias[i]) for i in range(6)]
        bias_rows += [row_sum(acc_upb[i * width : (i + 1) * width]) for i in range(ff // width)]
        tail = packed_ref.shape[0] - 2 * ff - width
        bias_rows.append(jnp.zeros((tail - len(bias_rows), width), f32))
        packed_ref[2 * ff + width :] = jnp.concatenate(bias_rows, axis=0).astype(bf16)


def dense(pieces, xt, att, inv, weights, packed_rows):
    rows, span, width = pieces[0].shape
    count = len(pieces)
    length = span * count
    ff = weights[2].shape[0]
    piece_spec = pl.BlockSpec((1, span, width), lambda r: (r, 0, 0))
    wide = pl.BlockSpec((1, width, length), lambda r: (r, 0, 0))
    full = lambda a: pl.BlockSpec(a.shape, lambda r: (0, 0))
    return pl.pallas_call(
        functools.partial(dense_kernel, pieces=count, rows=rows),
        grid=(rows,),
        in_specs=[piece_spec] * count
        + [wide, wide, pl.BlockSpec((1, GROUPS, 8, length), lambda r: (r, 0, 0, 0))]
        + [full(w) for w in weights],
        out_specs=[piece_spec] * count
        + [
            wide,
            wide,
            pl.BlockSpec((1, 16, length), lambda r: (r, 0, 0)),
            pl.BlockSpec((packed_rows, width), lambda r: (0, 0)),
        ],
        out_shape=[jax.ShapeDtypeStruct((rows, span, width), bf16)] * count
        + [
            jax.ShapeDtypeStruct((rows, width, length), f32),
            jax.ShapeDtypeStruct((rows, width, length), bf16),
            jax.ShapeDtypeStruct((rows, 16, length), f32),
            jax.ShapeDtypeStruct((packed_rows, width), bf16),
        ],
        scratch_shapes=[
            pltpu.VMEM((ff, width), f32),
            pltpu.VMEM((width, ff), f32),
            pltpu.VMEM((width, width), f32),
            pltpu.VMEM((6, width, 128), f32),
            pltpu.VMEM((ff, 128), f32),
        ],
        compiler_params=pltpu.CompilerParams(vmem_limit_bytes=VMEM_LIMIT),
        name="dense",
    )(*pieces, xt, att, inv, *weights)


def back_kernel(*refs, pieces, rows):
    xt_ref, qt_ref, kt_ref, vt_ref, og_ref, delta_ref, p_ref, gres_ref, w_ref = refs[:9]
    out_refs = refs[9 : 9 + pieces]
    packed_ref = refs[9 + pieces]
    grads, acc_w, acc_bias = refs[10 + pieces :]
    row = pl.program_id(0)
    group = pl.program_id(1)
    length = xt_ref.shape[2]
    width = xt_ref.shape[1]
    span = out_refs[0].shape[1]

    @pl.when((row == 0) & (group == 0))
    def _():
        acc_w[...] = jnp.zeros_like(acc_w)
        acc_bias[...] = jnp.zeros_like(acc_bias)

    def start_of(h):
        return pl.multiple_of((group * PER_GROUP + h) * HD, HD)

    def rows_of(ref, h):
        return ref[0, pl.ds(start_of(h), HD), :]

    sign = jnp.where(lax.broadcasted_iota(jnp.int32, (AUG, length), 0) < 3, 1.0, 0.0).astype(bf16)

    def grad_probs(h):
        delta = delta_ref[0, pl.ds(group * PER_GROUP + h, 1), :]
        first = delta.astype(bf16)
        rest = delta - first.astype(f32)
        second = rest.astype(bf16)
        third = (rest - second.astype(f32)).astype(bf16)
        aug = jnp.concatenate(
            [-first.astype(f32), -second.astype(f32), -third.astype(f32), jnp.zeros((AUG - 3, length), f32)], axis=0
        ).astype(bf16)
        left = jnp.concatenate([rows_of(vt_ref, h), sign], axis=0)
        right = jnp.concatenate([rows_of(og_ref, h), aug], axis=0)
        return dot(left, right, TN)

    upstream = grad_probs(0)
    for h in range(PER_GROUP):
        following = grad_probs(h + 1) if h + 1 < PER_GROUP else None
        probs = p_ref[0, h]
        grad_logits = (probs.astype(f32) * upstream).astype(bf16)
        start = start_of(h)
        grads[pl.ds(start, HD), :] = (dot(rows_of(kt_ref, h), grad_logits) * SCALE).astype(bf16)
        grads[pl.ds(width + start, HD), :] = (dot(rows_of(qt_ref, h), grad_logits, NT) * LN2).astype(bf16)
        grads[pl.ds(2 * width + start, HD), :] = dot(rows_of(og_ref, h), probs, NT).astype(bf16)
        upstream = following

    @pl.when(group == GROUPS - 1)
    def _():
        total = grads[...]
        acc_w[...] += dot(xt_ref[0], total, NT)
        acc_bias[0] += fold_lanes(total[:width].astype(f32))
        acc_bias[1] += fold_lanes(total[2 * width :].astype(f32))
        result = (gres_ref[0] + dot(w_ref[...], total)).astype(bf16)
        for index, ref in enumerate(out_refs):
            ref[0] = result[:, index * span : (index + 1) * span].T

    @pl.when((row == rows - 1) & (group == GROUPS - 1))
    def _():
        for index in range(3):
            packed_ref[index * width : (index + 1) * width] = acc_w[
                :, index * width : (index + 1) * width
            ].astype(bf16)
        bias_rows = [row_sum(acc_bias[i]) for i in range(2)]
        tail = packed_ref.shape[0] - 3 * width
        bias_rows.append(jnp.zeros((tail - len(bias_rows), width), f32))
        packed_ref[3 * width :] = jnp.concatenate(bias_rows, axis=0).astype(bf16)


def back(count, xt, qt, kt, vt, og, delta, probs, gres, w_all, packed_rows):
    rows, width, length = xt.shape
    span = length // count
    wide = pl.BlockSpec((1, width, length), lambda r, g: (r, 0, 0))
    return pl.pallas_call(
        functools.partial(back_kernel, pieces=count, rows=rows),
        grid=(rows, GROUPS),
        in_specs=[wide] * 5
        + [
            pl.BlockSpec((1, 16, length), lambda r, g: (r, 0, 0)),
            pl.BlockSpec((1, PER_GROUP, length, length), lambda r, g: (r, g, 0, 0)),
            wide,
            pl.BlockSpec(w_all.shape, lambda r, g: (0, 0)),
        ],
        out_specs=[pl.BlockSpec((1, span, width), lambda r, g: (r, 0, 0))] * count
        + [pl.BlockSpec((packed_rows, width), lambda r, g: (0, 0))],
        out_shape=[jax.ShapeDtypeStruct((rows, span, width), bf16)] * count
        + [jax.ShapeDtypeStruct((packed_rows, width), bf16)],
        scratch_shapes=[
            pltpu.VMEM((3 * width, length), bf16),
            pltpu.VMEM((width, 3 * width), f32),
            pltpu.VMEM((2, width, 128), f32),
        ],
        compiler_params=pltpu.CompilerParams(vmem_limit_bytes=VMEM_LIMIT),
        name="back",
    )(xt, qt, kt, vt, og, delta, probs, gres, w_all)


def exchange(pieces, axis):
    count = len(pieces)
    moved = [pieces[0]]
    for shift in range(1, count):
        moved.append(lax.ppermute(pieces[shift], axis, [(i, i ^ shift) for i in range(count)]))
    return moved


def halve(block, axis, bit, size):
    rows = block.shape[0] // 2
    side = (lax.axis_index(axis) // bit) % 2
    kept = lax.dynamic_slice_in_dim(block, side * rows, rows, 0)
    given = lax.dynamic_slice_in_dim(block, (1 - side) * rows, rows, 0)
    taken = lax.ppermute(given, axis, [(i, i ^ bit) for i in range(size)])
    return (kept.astype(f32) + taken.astype(f32)).astype(bf16)


def double(block, axis, bit, size):
    side = (lax.axis_index(axis) // bit) % 2
    taken = lax.ppermute(block, axis, [(i, i ^ bit) for i in range(size)])
    first = jnp.where(side == 0, block, taken)
    second = jnp.where(side == 0, taken, block)
    return jnp.concatenate([first, second], axis=0)


def sum_all(packed, axes):
    steps = []
    for axis, size in axes:
        bit = 1
        while bit < size:
            steps.append((axis, bit, size))
            bit *= 2
    for step in steps:
        packed = halve(packed, *step)
    for step in reversed(steps):
        packed = double(packed, *step)
    return packed


def round_up(value, unit):
    return -(-value // unit) * unit


def body(
    tokens, lengths, w_query, b_query, w_key, w_value, b_value, w_out, b_out, gain_attn, shift_attn,
    w_up, b_up, w_down, b_down, gain_ffn, shift_ffn, cotangent, *, sizes,
):
    count = sizes["seq"]
    devices = count * sizes["rows"]
    row_count, span, width = tokens.shape
    ff = w_up.shape[1]
    length = span * count
    rows = row_count // count
    me = lax.axis_index("seq")
    order = me ^ jnp.arange(count, dtype=jnp.int32)

    def column(vector):
        return vector.reshape(-1, 1)

    def spread(array):
        return jnp.take(array.reshape(count, rows, span, width), order, axis=0)

    token_parts = spread(tokens)
    cot_parts = spread(cotangent)
    token_rows = [exchange([token_parts[s, j : j + 1] for s in range(count)], "seq") for j in range(rows)]
    cot_moved = exchange([cot_parts[s] for s in range(count)], "seq")

    bounds = lax.dynamic_slice_in_dim(jnp.cumsum(lengths, axis=1), me * rows, rows, 0)
    places = (order[:, None] * span + jnp.arange(span, dtype=jnp.int32)[None, :]).reshape(length)
    segment = jnp.sum((places[None, None, :] >= bounds[:, :, None]).astype(jnp.int32), axis=1)
    ids = jnp.arange(AUG, dtype=jnp.int32)[None, :, None]
    same = segment[:, None, :] == ids
    qaug = same.astype(bf16)
    kaug = jnp.where(same | (ids >= lengths.shape[1]), 0.0, -BIG).astype(bf16)

    attend_weights = (w_query.T, w_key.T, w_value.T, column(b_query), column(b_value))
    dense_weights = (
        w_out.T, w_out, w_up.T, w_up, w_down.T, w_down, column(b_out), column(gain_attn), column(shift_attn),
        column(b_up), column(b_down), column(gain_ffn), column(shift_ffn),
    )
    first = [attend(token_rows[j], qaug[j : j + 1], kaug[j : j + 1], attend_weights) for j in range(rows)]
    xt, att, inv = [jnp.concatenate([f[i] for f in first], axis=0) for i in (0, 4, 5)]
    later_rows = round_up(2 * ff + width + 16, 16 * devices)
    dense_out = dense(cot_moved, xt, att, inv, dense_weights, later_rows)
    lo_moved = exchange(dense_out[:count], "seq")
    gres, og, delta, later = dense_out[count:]
    axes = [("rows", sizes["rows"]), ("seq", count)]
    later = sum_all(later, axes)
    w_all = jnp.concatenate([w_query, w_key, w_value], axis=1)
    first_rows = round_up(3 * width + 16, 16 * devices)
    qt, kt, vt, probs = [jnp.concatenate([f[i] for f in first], axis=0) for i in (1, 2, 3, 6)]
    back_out = back(count, xt, qt, kt, vt, og, delta, probs, gres, w_all, first_rows)
    grad_moved = exchange(back_out[:count], "seq")
    early = sum_all(back_out[count], axes)

    def place(moved, dtype):
        whole = jnp.zeros((count, rows, span, width), dtype)
        for shift in range(count):
            whole = lax.dynamic_update_slice(whole, moved[shift][None].astype(dtype), (me ^ shift, 0, 0, 0))
        return whole.reshape(row_count, span, width)

    layer_out = place(lo_moved, bf16)
    grad_tokens = place(grad_moved, f32)
    early = early.astype(f32)
    grad_query, grad_key, grad_value = [early[i * width : (i + 1) * width] for i in range(3)]
    grad_qbias, grad_vbias = early[3 * width], early[3 * width + 1]
    later = later.astype(f32)
    grad_down = later[:ff]
    grad_up = jnp.concatenate([later[ff + i * width : ff + (i + 1) * width] for i in range(ff // width)], axis=1)
    grad_output = later[2 * ff : 2 * ff + width]
    biases = later[2 * ff + width : 2 * ff + width + 6 + ff // width]
    grad_gain2, grad_shift2, grad_dnbias, grad_gain1, grad_shift1, grad_obias = [biases[i] for i in range(6)]
    grad_upbias = biases[6:].reshape(ff)
    return (
        layer_out, grad_tokens, grad_query, grad_qbias, grad_key, grad_value, grad_vbias, grad_output, grad_obias,
        grad_gain1, grad_shift1, grad_up, grad_upbias, grad_down, grad_dnbias, grad_gain2, grad_shift2,
    )


def solution(mesh):
    split = P("rows", "seq", None)
    in_specs = (split, P("rows", None)) + (P(),) * 15 + (split,)
    out_specs = (split, split) + (P(),) * 15
    sizes = dict(mesh.shape)
    return jax.shard_map(
        functools.partial(body, sizes=sizes), mesh=mesh, in_specs=in_specs, out_specs=out_specs, check_vma=False
    )
```

time: 1020 us -> 286 us (0.28)
  waiting for transfers between devices: 555 us -> 68.9 us
  matrix products: 169 us -> 0 us
  local copies, waits for them, and re-layouts: 176 us -> 51.2 us
  Pallas kernels: 0 us -> 72.8 us
  starting transfers between devices: 0.45 us -> 59.7 us
  blocking collectives: 43.5 us -> 0 us
  other arithmetic: 48.6 us -> 30.8 us
  between operations: 14.8 us -> 1.46 us
    reduce_scatter x2 -> x0, waiting for transfers between devices: 305 us -> none  [the longest x1 161 us: body(): lax.psum_scatter(part_value, 'seq', scatter_dimension=1, tiled=True)]
    dot_general x126 -> x0, matrix products: 169 us -> none  [the longest x12 28.7 us: output_row(): jnp.einsum('hsn,nhd->shd', probs, value_heads.astype(jnp.float32), precis...]
    all_gather x2 -> x0, waiting for transfers between devices: 134 us -> none  [the longest x1 86.2 us: body(): key_piece = lax.all_gather(key_b, 'seq', axis=1, tiled=True)]
    psum x1 -> x0, waiting for transfers between devices: 116 us -> none  [body(): summed = lax.psum(partial_grads, ('rows', 'seq'))]
    pallas_call x0 -> x3, Pallas kernels: none -> 72.8 us  [the longest x1 34.1 us: dense(): pl.pallas_call(functools.partial(dense_kernel, pieces=count, rows=rows),...]
    dynamic_slice x132 -> x12, local copies, waits for them, and re-layouts: 73 us -> 2.77 us  [the longest x10 2.61 us: halve(): given = lax.dynamic_slice_in_dim(block, (1 - side) * rows, rows, 0)]
    ppermute x0 -> x38, waiting for transfers between devices: none -> 68.9 us  [the longest x10 38.1 us: halve(): taken = lax.ppermute(given, axis, [(i, i ^ bit) for i in range(size)])]
    ppermute x0 -> x38, starting transfers between devices: none -> 59.7 us  [the longest x18 30.2 us: exchange(): lax.ppermute(pieces[shift], axis, [(i, i ^ shift) for i in range(count)])]
  transfers between devices with their start and end apart: 5 -> 38, of which waited for: 5 -> 17; matrix products, arithmetic and copies ran while one was open for 8% -> 24% of each run, Pallas kernels for 0% -> 3%
where the time goes in v1:
time: 286 us; the launch traced here: 285 us
  Pallas kernels  72.8 us (25%)
  waiting for transfers between devices  68.9 us (24%)
  starting transfers between devices  59.7 us (21%)
  local copies, waits for them, and re-layouts  51.2 us (18%)
  other arithmetic  30.8 us (11%)
    ppermute x10, waiting for transfers between devices, halve(): taken = lax.ppermute(given, axis, [(i, i ^ bit) for i in range(size)])  38.1 us
    pallas_call x1, Pallas kernels, dense(): pl.pallas_call(functools.partial(dense_kernel, pieces=count, rows=rows),...  34.1 us
    ppermute x10, waiting for transfers between devices, double(): taken = lax.ppermute(block, axis, [(i, i ^ bit) for i in range(size)])  30.8 us
    ppermute x18, starting transfers between devices, exchange(): lax.ppermute(pieces[shift], axis, [(i, i ^ shift) for i in range(count)])  30.2 us
    pallas_call x1, Pallas kernels, back(): pl.pallas_call(functools.partial(back_kernel, pieces=count, rows=rows), g...  28.9 us
    concatenate x6, other arithmetic, body(): jnp.concatenate([f[i] for f in first], axis=0)  21.5 us
    pallas_call x2, local copies, waits for them, and re-layouts, attend(): pl.pallas_call(functools.partial(attend_kernel, pieces=count, row_base=0)...  19.1 us
    ppermute x10, starting transfers between devices, double(): taken = lax.ppermute(block, axis, [(i, i ^ bit) for i in range(size)])  15.5 us
  transfers between devices with their start and end apart: 38, of which 17 were waited for; matrix products, arithmetic and copies ran while one was open for 24% of the time, Pallas kernels for 3%

profile of v1, /device:TPU:0, one launch (start us, length us, event | category | flops | bytes accessed | tf_op | source)
XLA Modules:
  0.0 284.9 jit_solution(8751731766943896563)
XLA Ops:
  6.1 3.1 %collective-permute-start.3 = (bf16[1,128,384]{2,1,0:T(8,128)(2,1)S(1)}, bf16[1,128,384]{2,1,0:T(8,128)(2,1)S(1)}, u32[]{:S(2)}, u32[]{:S(2)}) collective-permute-start(bf16[1,128,384]{2,1,0:T(8,128)(2,1)S(1)} %get-tuple-element.146), channel_id=1, source_target_pairs={{0,1},{1,0},{2,3},{3,2},{4,5},{5,4},{6,7},{7,6},{8,9},{9,8},{10,11... | collective-permute-start | bytes 294920 | tf_op jit(solution)/shard_map/ppermute | solution.py:366
  9.1 2.6 collective-permute-start.4
  12.6 3.5 %collective-permute-start.7 = (bf16[1,128,384]{2,1,0:T(8,128)(2,1)}, bf16[1,128,384]{2,1,0:T(8,128)(2,1)}, u32[]{:S(2)}, u32[]{:S(2)}) collective-permute-start(bf16[1,128,384]{2,1,0:T(8,128)(2,1)} %get-tuple-element.141), channel_id=1, source_target_pairs={{0,2},{1,3},{2,0},{3,1},{4,6},{5,7},{6,4},{7,5},{8,10},{9,11},{10,... | collective-permute-start | bytes 294920 | tf_op jit(solution)/shard_map/ppermute | solution.py:366
  34.7 3.8 %collective-permute-start.10 = (bf16[1,128,384]{2,1,0:T(8,128)(2,1)}, bf16[1,128,384]{2,1,0:T(8,128)(2,1)S(1)}, u32[]{:S(2)}, u32[]{:S(2)}) collective-permute-start(bf16[1,128,384]{2,1,0:T(8,128)(2,1)} %get-tuple-element.137), channel_id=1, source_target_pairs={{0,2},{1,3},{2,0},{3,1},{4,6},{5,7},{6,4},{7,5},{8,10},{9,11},{10,... | collective-permute-start | bytes 294920 | tf_op jit(solution)/shard_map/ppermute | solution.py:366
  38.5 9.9 %attend.3 = (bf16[1,384,512]{2,1,0:T(8,128)(2,1)}, bf16[1,384,512]{2,1,0:T(8,128)(2,1)}, bf16[1,384,512]{2,1,0:T(8,128)(2,1)}, bf16[1,384,512]{2,1,0:T(8,128)(2,...) custom-call(bf16[1,128,384]{2,1,0:T(8,128)(2,1)} %get-tuple-element.147.refs_0_, ...), custom_call_target="tpu_custom_call" | custom-call | tf_op jit(solution)/shard_map/attend/pallas_call | solution.py:132
  50.2 3.8 %collective-permute-start.1 = (bf16[3,128,384]{2,1,0:T(8,128)(2,1)}, bf16[3,128,384]{2,1,0:T(8,128)(2,1)}, u32[]{:S(2)}, u32[]{:S(2)}) collective-permute-start(bf16[3,128,384]{2,1,0:T(8,128)(2,1)} %get-tuple-element.149), channel_id=1, source_target_pairs={{0,2},{1,3},{2,0},{3,1},{4,6},{5,7},{6,4},{7,5},{8,10},{9,11},{10,... | collective-permute-start | bytes 884744 | tf_op jit(solution)/shard_map/ppermute | solution.py:366
  54.0 9.4 %attend.5 = (bf16[3,384,512]{2,1,0:T(8,128)(2,1)S(1)}, f32[1,384,512]{2,1,0:T(8,128)S(1)}, f32[1,3,8,512]{3,2,1,0:T(8,128)S(1)}, bf16[1,384,512]{2,1,0:T(8,128)(...) fusion(bf16[3,384,512]{2,1,0:T(8,128)(2,1)S(1)} %constant_dynamic-updat, ...), kind=kCustom, calls=%fused_computation.93 | custom fusion | bytes 10403840 | tf_op jit(solution)/shard_map/attend/pallas_call | solution.py:132
  64.6 9.7 %attend.4 = (bf16[3,384,512]{2,1,0:T(8,128)(2,1)S(1)}, f32[1,384,512]{2,1,0:T(8,128)}, f32[1,3,8,512]{3,2,1,0:T(8,128)S(1)}, bf16[1,384,512]{2,1,0:T(8,128)(2,1)...) fusion(bf16[3,384,512]{2,1,0:T(8,128)(2,1)S(1)} %get-tuple-element.102, ...), kind=kCustom, calls=%fused_computation.92 | custom fusion | bytes 10403840 | tf_op jit(solution)/shard_map/attend/pallas_call | solution.py:132
  74.4 2.8 pad_maximum_fusion.4.refs_1_
  78.4 13.9 %pad_maximum_fusion.refs_6_ = bf16[3,12,512,512]{3,2,1,0:T(8,128)(2,1)} fusion(bf16[1,12,512,512]{3,2,1,0:T(8,128)(2,1)} %get-tuple-element.99, bf16[1,12,512,512]{3,2,1,0:T(8,128)(2,1)} %get-tuple-element.113, bf16[1,12,512,512]{3,2,1,0:T(8,128)(2,1)} %get-tuple-element.76), kind=kLoop, calls=%fused_computation.2 | loop fusion | flops 18874368 | bytes 37748736 | tf_op jit(solution)/shard_map/concatenate | solution.py:452
  95.9 34.1 %dense.1 = (bf16[3,128,384]{2,1,0:T(8,128)(2,1)}, bf16[3,128,384]{2,1,0:T(8,128)(2,1)}, bf16[3,128,384]{2,1,0:T(8,128)(2,1)}, bf16[3,128,384]{2,1,0:T(8,128)(2,1...) custom-call(bf16[3,128,384]{2,1,0:T(8,128)(2,1)} %get-tuple-element., ...), custom_call_target="tpu_custom_call" | custom-call | tf_op jit(solution)/shard_map/dense/pallas_call | solution.py:232
  130.0 28.9 %back.1 = (bf16[3,128,384]{2,1,0:T(8,128)(2,1)}, bf16[3,128,384]{2,1,0:T(8,128)(2,1)}, bf16[3,128,384]{2,1,0:T(8,128)(2,1)}, bf16[3,128,384]{2,1,0:T(8,128)(2,1)}, bf16[1536,384]{1,0:T(8,128)(2,1)}) custom-call(bf16[3,384,512]{2,1,0:T(8,128)(2,1)} %copy-done.2, bf16[3,384,512]{2,1,0:T(8,128)(2,1)} %pad_maximum_fusion.4.refs_1_, ...), custom_call_target="tpu_custom_call" | custom-call | tf_op jit(solution)/shard_map/back/pallas_call | solution.py:338
  165.6 3.2 %collective-permute-start.13 = (bf16[3,128,384]{2,1,0:T(8,128)(2,1)S(1)}, bf16[3,128,384]{2,1,0:T(8,128)(2,1)S(1)}, u32[]{:S(2)}, u32[]{:S(2)}) collective-permute-start(bf16[3,128,384]{2,1,0:T(8,128)(2,1)S(1)} %copy-done.47), channel_id=1, source_target_pairs={{0,2},{1,3},{2,0},{3,1},{4,6},{5,7},{6,4},{7,5},{8,10},{9,11},{10,... | collective-permute-start | bytes 884744 | tf_op jit(solution)/shard_map/ppermute | solution.py:366
  169.6 2.9 %collective-permute-done.19 = bf16[384,384]{1,0:T(8,128)(2,1)S(1)} collective-permute-done((bf16[384,384]{1,0:T(8,128)(2,1)S(1)}, bf16[384,384]{1,0:T(8,128)(2,1)S(1)}, u32[]{:S(2)}, u32[]{:S(2)}) %collective-permute-start.19) | collective-permute-done | bytes 294944 | tf_op jit(solution)/shard_map/ppermute | solution.py:375
  176.4 3.4 %collective-permute-done.20 = bf16[192,384]{1,0:T(8,128)(2,1)S(1)} collective-permute-done((bf16[192,384]{1,0:T(8,128)(2,1)S(1)}, bf16[192,384]{1,0:T(8,128)(2,1)S(1)}, u32[]{:S(2)}, u32[]{:S(2)}) %collective-permute-start.20) | collective-permute-done | bytes 147488 | tf_op jit(solution)/shard_map/ppermute | solution.py:375
  180.6 9.2 %collective-permute-done.29 = bf16[896,384]{1,0:T(8,128)(2,1)S(1)} collective-permute-done((bf16[896,384]{1,0:T(8,128)(2,1)S(1)}, bf16[896,384]{1,0:T(8,128)(2,1)S(1)}, u32[]{:S(2)}, u32[]{:S(2)}) %collective-permute-start.29) | collective-permute-done | bytes 688160 | tf_op jit(solution)/shard_map/ppermute | solution.py:375
  192.3 3.1 %collective-permute-done.21 = bf16[96,384]{1,0:T(8,128)(2,1)S(1)} collective-permute-done((bf16[96,384]{1,0:T(8,128)(2,1)S(1)}, bf16[96,384]{1,0:T(8,128)(2,1)S(1)}, u32[]{:S(2)}, u32[]{:S(2)}) %collective-permute-start.21) | collective-permute-done | bytes 73760 | tf_op jit(solution)/shard_map/ppermute | solution.py:375
  198.8 3.2 %collective-permute-start.22 = (bf16[48,384]{1,0:T(8,128)(2,1)S(1)}, bf16[48,384]{1,0:T(8,128)(2,1)S(1)}, u32[]{:S(2)}, u32[]{:S(2)}) collective-permute-start(bf16[48,384]{1,0:T(8,128)(2,1)S(1)} %constant_dynamic-slice_fusion.5), channel_id=1, source_target_pairs={{0,2},{1,3},{2,0},{3,1},{4,6},{5,7},{6,4},{7,5},{8,10},{9,11},{10,... | collective-permute-start | bytes 110600 | tf_op jit(solution)/shard_map/ppermute | solution.py:375
  202.1 9.7 %collective-permute-done.22 = bf16[48,384]{1,0:T(8,128)(2,1)S(1)} collective-permute-done((bf16[48,384]{1,0:T(8,128)(2,1)S(1)}, bf16[48,384]{1,0:T(8,128)(2,1)S(1)}, u32[]{:S(2)}, u32[]{:S(2)}) %collective-permute-start.22) | collective-permute-done | bytes 36896 | tf_op jit(solution)/shard_map/ppermute | solution.py:375
  212.4 4.9 %collective-permute-done.31 = bf16[224,384]{1,0:T(8,128)(2,1)S(1)} collective-permute-done((bf16[224,384]{1,0:T(8,128)(2,1)S(1)}, bf16[224,384]{1,0:T(8,128)(2,1)S(1)}, u32[]{:S(2)}, u32[]{:S(2)}) %collective-permute-start.31) | collective-permute-done | bytes 172064 | tf_op jit(solution)/shard_map/ppermute | solution.py:375
  217.2 3.0 %collective-permute-start.23 = (bf16[48,384]{1,0:T(8,128)(2,1)S(1)}, bf16[48,384]{1,0:T(8,128)(2,1)S(1)}, u32[]{:S(2)}, u32[]{:S(2)}) collective-permute-start(bf16[48,384]{1,0:T(8,128)(2,1)S(1)} %add_convert_fusion.9), channel_id=1, source_target_pairs={{0,2},{1,3},{2,0},{3,1},{4,6},{5,7},{6,4},{7,5},{8,10},{9,11},{10,... | collective-permute-start | bytes 110600 | tf_op jit(solution)/shard_map/ppermute | solution.py:381
  222.3 2.9 %collective-permute-start.32 = (bf16[112,384]{1,0:T(8,128)(2,1)S(1)}, bf16[112,384]{1,0:T(8,128)(2,1)S(1)}, u32[]{:S(2)}, u32[]{:S(2)}) collective-permute-start(bf16[112,384]{1,0:T(8,128)(2,1)S(1)} %constant_dynamic-slice_fusion), channel_id=1, source_target_pairs={{0,2},{1,3},{2,0},{3,1},{4,6},{5,7},{6,4},{7,5},{8,10},{9,11},{10,... | collective-permute-start | bytes 258056 | tf_op jit(solution)/shard_map/ppermute | solution.py:375
  225.2 2.5 collective-permute-done.32
  227.7 3.0 %collective-permute-start.33 = (bf16[112,384]{1,0:T(8,128)(2,1)S(1)}, bf16[112,384]{1,0:T(8,128)(2,1)S(1)}, u32[]{:S(2)}, u32[]{:S(2)}) collective-permute-start(bf16[112,384]{1,0:T(8,128)(2,1)S(1)} %add_convert_fusion.7), channel_id=1, source_target_pairs={{0,2},{1,3},{2,0},{3,1},{4,6},{5,7},{6,4},{7,5},{8,10},{9,11},{10,... | collective-permute-start | bytes 258056 | tf_op jit(solution)/shard_map/ppermute | solution.py:381
  230.7 2.7 collective-permute-done.33
  233.4 2.1 collective-permute-start.24
  235.6 3.0 %collective-permute-done.24 = bf16[96,384]{1,0:T(8,128)(2,1)S(1)} collective-permute-done((bf16[96,384]{1,0:T(8,128)(2,1)S(1)}, bf16[96,384]{1,0:T(8,128)(2,1)S(1)}, u32[]{:S(2)}, u32[]{:S(2)}) %collective-permute-start.24) | collective-permute-done | bytes 73760 | tf_op jit(solution)/shard_map/ppermute | solution.py:381
  240.7 3.3 %collective-permute-done.34 = bf16[224,384]{1,0:T(8,128)(2,1)S(1)} collective-permute-done((bf16[224,384]{1,0:T(8,128)(2,1)S(1)}, bf16[224,384]{1,0:T(8,128)(2,1)S(1)}, u32[]{:S(2)}, u32[]{:S(2)}) %collective-permute-start.34) | collective-permute-done | bytes 172064 | tf_op jit(solution)/shard_map/ppermute | solution.py:381
  245.6 5.2 %collective-permute-done.25 = bf16[192,384]{1,0:T(8,128)(2,1)S(1)} collective-permute-done((bf16[192,384]{1,0:T(8,128)(2,1)S(1)}, bf16[192,384]{1,0:T(8,128)(2,1)S(1)}, u32[]{:S(2)}, u32[]{:S(2)}) %collective-permute-start.25) | collective-permute-done | bytes 147488 | tf_op jit(solution)/shard_map/ppermute | solution.py:381
  252.4 5.6 %collective-permute-done.35 = bf16[448,384]{1,0:T(8,128)(2,1)S(1)} collective-permute-done((bf16[448,384]{1,0:T(8,128)(2,1)S(1)}, bf16[448,384]{1,0:T(8,128)(2,1)S(1)}, u32[]{:S(2)}, u32[]{:S(2)}) %collective-permute-start.35) | collective-permute-done | bytes 344096 | tf_op jit(solution)/shard_map/ppermute | solution.py:381
  260.4 4.9 %collective-permute-start.17 = (bf16[3,128,384]{2,1,0:T(8,128)(2,1)S(1)}, bf16[3,128,384]{2,1,0:T(8,128)(2,1)S(1)}, u32[]{:S(2)}, u32[]{:S(2)}) collective-permute-start(bf16[3,128,384]{2,1,0:T(8,128)(2,1)S(1)} %copy-done.45), channel_id=1, source_target_pairs={{0,3},{1,2},{2,1},{3,0},{4,7},{5,6},{6,5},{7,4},{8,11},{9,10},{10,... | collective-permute-start | bytes 884744 | tf_op jit(solution)/shard_map/ppermute | solution.py:366
  267.6 7.1 %collective-permute-done.36 = bf16[896,384]{1,0:T(8,128)(2,1)S(1)} collective-permute-done((bf16[896,384]{1,0:T(8,128)(2,1)S(1)}, bf16[896,384]{1,0:T(8,128)(2,1)S(1)}, u32[]{:S(2)}, u32[]{:S(2)}) %collective-permute-start.36) | collective-permute-done | bytes 688160 | tf_op jit(solution)/shard_map/ppermute | solution.py:381
  (246 shorter events, 73.1 us)
Async XLA Ops:
  6.1 28.0 %collective-permute-start.3 = (bf16[1,128,384]{2,1,0:T(8,128)(2,1)S(1)}, bf16[1,128,384]{2,1,0:T(8,128)(2,1)S(1)}, u32[]{:S(2)}, u32[]{:S(2)}) collective-permute-start(bf16[1,128,384]{2,1,0:T(8,128)(2,1)S(1)} %get-tuple-element.146), channel_id=1, source_target_pairs={{0,1},{1,0},{2,3},{3,2},{4,5},{5,4},{6,7},{7,6},{8,9},{9,8},{10,11... | collective-permute-start | bytes 294920 | tf_op jit(solution)/shard_map/ppermute | solution.py:366
  9.1 25.0 %collective-permute-start.4 = (bf16[1,128,384]{2,1,0:T(8,128)(2,1)S(1)}, bf16[1,128,384]{2,1,0:T(8,128)(2,1)S(1)}, u32[]{:S(2)}, u32[]{:S(2)}) collective-permute-start(bf16[1,128,384]{2,1,0:T(8,128)(2,1)S(1)} %get-tuple-element.145), channel_id=1, source_target_pairs={{0,2},{1,3},{2,0},{3,1},{4,6},{5,7},{6,4},{7,5},{8,10},{9,11},{10,... | collective-permute-start | bytes 294920 | tf_op jit(solution)/shard_map/ppermute | solution.py:366
  11.7 22.9 %collective-permute-start.5 = (bf16[1,128,384]{2,1,0:T(8,128)(2,1)S(1)}, bf16[1,128,384]{2,1,0:T(8,128)(2,1)}, u32[]{:S(2)}, u32[]{:S(2)}) collective-permute-start(bf16[1,128,384]{2,1,0:T(8,128)(2,1)S(1)} %get-tuple-element.144), channel_id=1, source_target_pairs={{0,3},{1,2},{2,1},{3,0},{4,7},{5,6},{6,5},{7,4},{8,11},{9,10},{10,... | collective-permute-start | bytes 294920 | tf_op jit(solution)/shard_map/ppermute | solution.py:366
  11.7 36.6 %collective-permute-start.6 = (bf16[1,128,384]{2,1,0:T(8,128)(2,1)S(1)}, bf16[1,128,384]{2,1,0:T(8,128)(2,1)S(1)}, u32[]{:S(2)}, u32[]{:S(2)}) collective-permute-start(bf16[1,128,384]{2,1,0:T(8,128)(2,1)S(1)} %get-tuple-element.142), channel_id=1, source_target_pairs={{0,1},{1,0},{2,3},{3,2},{4,5},{5,4},{6,7},{7,6},{8,9},{9,8},{10,11... | collective-permute-start | bytes 294920 | tf_op jit(solution)/shard_map/ppermute | solution.py:366
  12.6 37.4 %collective-permute-start.7 = (bf16[1,128,384]{2,1,0:T(8,128)(2,1)}, bf16[1,128,384]{2,1,0:T(8,128)(2,1)}, u32[]{:S(2)}, u32[]{:S(2)}) collective-permute-start(bf16[1,128,384]{2,1,0:T(8,128)(2,1)} %get-tuple-element.141), channel_id=1, source_target_pairs={{0,2},{1,3},{2,0},{3,1},{4,6},{5,7},{6,4},{7,5},{8,10},{9,11},{10,... | collective-permute-start | bytes 294920 | tf_op jit(solution)/shard_map/ppermute | solution.py:366
  34.1 16.1 %collective-permute-start.8 = (bf16[1,128,384]{2,1,0:T(8,128)(2,1)}, bf16[1,128,384]{2,1,0:T(8,128)(2,1)S(1)}, u32[]{:S(2)}, u32[]{:S(2)}) collective-permute-start(bf16[1,128,384]{2,1,0:T(8,128)(2,1)} %get-tuple-element.140), channel_id=1, source_target_pairs={{0,3},{1,2},{2,1},{3,0},{4,7},{5,6},{6,5},{7,4},{8,11},{9,10},{10,... | collective-permute-start | bytes 294920 | tf_op jit(solution)/shard_map/ppermute | solution.py:366
  34.1 29.3 %collective-permute-start.9 = (bf16[1,128,384]{2,1,0:T(8,128)(2,1)}, bf16[1,128,384]{2,1,0:T(8,128)(2,1)S(1)}, u32[]{:S(2)}, u32[]{:S(2)}) collective-permute-start(bf16[1,128,384]{2,1,0:T(8,128)(2,1)} %get-tuple-element.138), channel_id=1, source_target_pairs={{0,1},{1,0},{2,3},{3,2},{4,5},{5,4},{6,7},{7,6},{8,9},{9,8},{10,11... | collective-permute-start | bytes 294920 | tf_op jit(solution)/shard_map/ppermute | solution.py:366
  34.7 29.3 %collective-permute-start.10 = (bf16[1,128,384]{2,1,0:T(8,128)(2,1)}, bf16[1,128,384]{2,1,0:T(8,128)(2,1)S(1)}, u32[]{:S(2)}, u32[]{:S(2)}) collective-permute-start(bf16[1,128,384]{2,1,0:T(8,128)(2,1)} %get-tuple-element.137), channel_id=1, source_target_pairs={{0,2},{1,3},{2,0},{3,1},{4,6},{5,7},{6,4},{7,5},{8,10},{9,11},{10,... | collective-permute-start | bytes 294920 | tf_op jit(solution)/shard_map/ppermute | solution.py:366
  48.4 15.6 %collective-permute-start.11 = (bf16[1,128,384]{2,1,0:T(8,128)(2,1)}, bf16[1,128,384]{2,1,0:T(8,128)(2,1)}, u32[]{:S(2)}, u32[]{:S(2)}) collective-permute-start(bf16[1,128,384]{2,1,0:T(8,128)(2,1)} %get-tuple-element.136), channel_id=1, source_target_pairs={{0,3},{1,2},{2,1},{3,0},{4,7},{5,6},{6,5},{7,4},{8,11},{9,10},{10,... | collective-permute-start | bytes 294920 | tf_op jit(solution)/shard_map/ppermute | solution.py:366
  50.1 45.8 %collective-permute-start = (bf16[3,128,384]{2,1,0:T(8,128)(2,1)}, bf16[3,128,384]{2,1,0:T(8,128)(2,1)}, u32[]{:S(2)}, u32[]{:S(2)}) collective-permute-start(bf16[3,128,384]{2,1,0:T(8,128)(2,1)} %get-tuple-element.150), channel_id=1, source_target_pairs={{0,1},{1,0},{2,3},{3,2},{4,5},{5,4},{6,7},{7,6},{8,9},{9,8},{10,11... | collective-permute-start | bytes 884744 | tf_op jit(solution)/shard_map/ppermute | solution.py:366
  50.2 45.7 %collective-permute-start.1 = (bf16[3,128,384]{2,1,0:T(8,128)(2,1)}, bf16[3,128,384]{2,1,0:T(8,128)(2,1)}, u32[]{:S(2)}, u32[]{:S(2)}) collective-permute-start(bf16[3,128,384]{2,1,0:T(8,128)(2,1)} %get-tuple-element.149), channel_id=1, source_target_pairs={{0,2},{1,3},{2,0},{3,1},{4,6},{5,7},{6,4},{7,5},{8,10},{9,11},{10,... | collective-permute-start | bytes 884744 | tf_op jit(solution)/shard_map/ppermute | solution.py:366
  63.4 32.5 %collective-permute-start.2 = (bf16[3,128,384]{2,1,0:T(8,128)(2,1)}, bf16[3,128,384]{2,1,0:T(8,128)(2,1)}, u32[]{:S(2)}, u32[]{:S(2)}) collective-permute-start(bf16[3,128,384]{2,1,0:T(8,128)(2,1)} %get-tuple-element.148), channel_id=1, source_target_pairs={{0,3},{1,2},{2,1},{3,0},{4,7},{5,6},{6,5},{7,4},{8,11},{9,10},{10,... | collective-permute-start | bytes 884744 | tf_op jit(solution)/shard_map/ppermute | solution.py:366
  161.3 11.2 %collective-permute-start.28 = (bf16[1792,384]{1,0:T(8,128)(2,1)}, bf16[1792,384]{1,0:T(8,128)(2,1)S(1)}, u32[]{:S(2)}, u32[]{:S(2)}) collective-permute-start(bf16[1792,384]{1,0:T(8,128)(2,1)} %constant_dynamic-slice_fusion.4), channel_id=1, source_target_pairs={{0,4},{4,0},{8,12},{12,8},{16,20},{20,16},{24,28},{28,24},{1,5},{5... | collective-permute-start | bytes 4128776 | tf_op jit(solution)/shard_map/ppermute | solution.py:375
  163.4 9.1 %collective-permute-start.19 = (bf16[384,384]{1,0:T(8,128)(2,1)S(1)}, bf16[384,384]{1,0:T(8,128)(2,1)S(1)}, u32[]{:S(2)}, u32[]{:S(2)}) collective-permute-start(bf16[384,384]{1,0:T(8,128)(2,1)S(1)} %constant_dynamic-slice_fusion.8), channel_id=1, source_target_pairs={{0,8},{4,12},{8,0},{12,4},{16,24},{20,28},{24,16},{28,20},{1,9},{5... | collective-permute-start | bytes 884744 | tf_op jit(solution)/shard_map/ppermute | solution.py:375
  164.9 25.7 %collective-permute-start.12 = (bf16[3,128,384]{2,1,0:T(8,128)(2,1)}, bf16[3,128,384]{2,1,0:T(8,128)(2,1)S(1)}, u32[]{:S(2)}, u32[]{:S(2)}) collective-permute-start(bf16[3,128,384]{2,1,0:T(8,128)(2,1)} %get-tuple-element.62), channel_id=1, source_target_pairs={{0,1},{1,0},{2,3},{3,2},{4,5},{5,4},{6,7},{7,6},{8,9},{9,8},{10,11... | collective-permute-start | bytes 884744 | tf_op jit(solution)/shard_map/ppermute | solution.py:366
  165.6 92.7 %collective-permute-start.13 = (bf16[3,128,384]{2,1,0:T(8,128)(2,1)S(1)}, bf16[3,128,384]{2,1,0:T(8,128)(2,1)S(1)}, u32[]{:S(2)}, u32[]{:S(2)}) collective-permute-start(bf16[3,128,384]{2,1,0:T(8,128)(2,1)S(1)} %copy-done.47), channel_id=1, source_target_pairs={{0,2},{1,3},{2,0},{3,1},{4,6},{5,7},{6,4},{7,5},{8,10},{9,11},{10,... | collective-permute-start | bytes 884744 | tf_op jit(solution)/shard_map/ppermute | solution.py:366
  168.8 106.4 %collective-permute-start.14 = (bf16[3,128,384]{2,1,0:T(8,128)(2,1)S(1)}, bf16[3,128,384]{2,1,0:T(8,128)(2,1)S(1)}, u32[]{:S(2)}, u32[]{:S(2)}) collective-permute-start(bf16[3,128,384]{2,1,0:T(8,128)(2,1)S(1)} %copy-done.44), channel_id=1, source_target_pairs={{0,3},{1,2},{2,1},{3,0},{4,7},{5,6},{6,5},{7,4},{8,11},{9,10},{10,... | collective-permute-start | bytes 884744 | tf_op jit(solution)/shard_map/ppermute | solution.py:366
  173.1 16.7 %collective-permute-start.29 = (bf16[896,384]{1,0:T(8,128)(2,1)S(1)}, bf16[896,384]{1,0:T(8,128)(2,1)S(1)}, u32[]{:S(2)}, u32[]{:S(2)}) collective-permute-start(bf16[896,384]{1,0:T(8,128)(2,1)S(1)} %constant_dynamic-slice_fusion.3), channel_id=1, source_target_pairs={{0,8},{4,12},{8,0},{12,4},{16,24},{20,28},{24,16},{28,20},{1,9},{5... | collective-permute-start | bytes 2064392 | tf_op jit(solution)/shard_map/ppermute | solution.py:375
  179.9 80.5 %collective-permute-start.15 = (bf16[3,128,384]{2,1,0:T(8,128)(2,1)S(1)}, bf16[3,128,384]{2,1,0:T(8,128)(2,1)S(1)}, u32[]{:S(2)}, u32[]{:S(2)}) collective-permute-start(bf16[3,128,384]{2,1,0:T(8,128)(2,1)S(1)} %copy-done.48), channel_id=1, source_target_pairs={{0,1},{1,0},{2,3},{3,2},{4,5},{5,4},{6,7},{7,6},{8,9},{9,8},{10,11... | collective-permute-start | bytes 884744 | tf_op jit(solution)/shard_map/ppermute | solution.py:366
  189.8 5.6 %collective-permute-start.21 = (bf16[96,384]{1,0:T(8,128)(2,1)S(1)}, bf16[96,384]{1,0:T(8,128)(2,1)S(1)}, u32[]{:S(2)}, u32[]{:S(2)}) collective-permute-start(bf16[96,384]{1,0:T(8,128)(2,1)S(1)} %constant_dynamic-slice_fusion.6), channel_id=1, source_target_pairs={{0,1},{1,0},{2,3},{3,2},{4,5},{5,4},{6,7},{7,6},{8,9},{9,8},{10,11... | collective-permute-start | bytes 221192 | tf_op jit(solution)/shard_map/ppermute | solution.py:375
  190.7 8.1 %collective-permute-start.30 = (bf16[448,384]{1,0:T(8,128)(2,1)S(1)}, bf16[448,384]{1,0:T(8,128)(2,1)S(1)}, u32[]{:S(2)}, u32[]{:S(2)}) collective-permute-start(bf16[448,384]{1,0:T(8,128)(2,1)S(1)} %constant_dynamic-slice_fusion.2), channel_id=1, source_target_pairs={{0,16},{4,20},{8,24},{12,28},{16,0},{20,4},{24,8},{28,12},{1,17},{... | collective-permute-start | bytes 1032200 | tf_op jit(solution)/shard_map/ppermute | solution.py:375
  195.4 79.9 %collective-permute-start.16 = (bf16[3,128,384]{2,1,0:T(8,128)(2,1)S(1)}, bf16[3,128,384]{2,1,0:T(8,128)(2,1)S(1)}, u32[]{:S(2)}, u32[]{:S(2)}) collective-permute-start(bf16[3,128,384]{2,1,0:T(8,128)(2,1)S(1)} %copy-done.46), channel_id=1, source_target_pairs={{0,2},{1,3},{2,0},{3,1},{4,6},{5,7},{6,4},{7,5},{8,10},{9,11},{10,... | collective-permute-start | bytes 884744 | tf_op jit(solution)/shard_map/ppermute | solution.py:366
  198.8 13.0 %collective-permute-start.22 = (bf16[48,384]{1,0:T(8,128)(2,1)S(1)}, bf16[48,384]{1,0:T(8,128)(2,1)S(1)}, u32[]{:S(2)}, u32[]{:S(2)}) collective-permute-start(bf16[48,384]{1,0:T(8,128)(2,1)S(1)} %constant_dynamic-slice_fusion.5), channel_id=1, source_target_pairs={{0,2},{1,3},{2,0},{3,1},{4,6},{5,7},{6,4},{7,5},{8,10},{9,11},{10,... | collective-permute-start | bytes 110600 | tf_op jit(solution)/shard_map/ppermute | solution.py:375
  211.8 5.4 %collective-permute-start.31 = (bf16[224,384]{1,0:T(8,128)(2,1)S(1)}, bf16[224,384]{1,0:T(8,128)(2,1)S(1)}, u32[]{:S(2)}, u32[]{:S(2)}) collective-permute-start(bf16[224,384]{1,0:T(8,128)(2,1)S(1)} %constant_dynamic-slice_fusion.1), channel_id=1, source_target_pairs={{0,1},{1,0},{2,3},{3,2},{4,5},{5,4},{6,7},{7,6},{8,9},{9,8},{10,11... | collective-permute-start | bytes 516104 | tf_op jit(solution)/shard_map/ppermute | solution.py:375
  227.7 5.7 %collective-permute-start.33 = (bf16[112,384]{1,0:T(8,128)(2,1)S(1)}, bf16[112,384]{1,0:T(8,128)(2,1)S(1)}, u32[]{:S(2)}, u32[]{:S(2)}) collective-permute-start(bf16[112,384]{1,0:T(8,128)(2,1)S(1)} %add_convert_fusion.7), channel_id=1, source_target_pairs={{0,2},{1,3},{2,0},{3,1},{4,6},{5,7},{6,4},{7,5},{8,10},{9,11},{10,... | collective-permute-start | bytes 258056 | tf_op jit(solution)/shard_map/ppermute | solution.py:381
  238.6 5.4 %collective-permute-start.34 = (bf16[224,384]{1,0:T(8,128)(2,1)S(1)}, bf16[224,384]{1,0:T(8,128)(2,1)S(1)}, u32[]{:S(2)}, u32[]{:S(2)}) collective-permute-start(bf16[224,384]{1,0:T(8,128)(2,1)S(1)} %pad_maximum_fusion.12), channel_id=1, source_target_pairs={{0,1},{1,0},{2,3},{3,2},{4,5},{5,4},{6,7},{7,6},{8,9},{9,8},{10,11... | collective-permute-start | bytes 516104 | tf_op jit(solution)/shard_map/ppermute | solution.py:381
  244.0 6.8 %collective-permute-start.25 = (bf16[192,384]{1,0:T(8,128)(2,1)S(1)}, bf16[192,384]{1,0:T(8,128)(2,1)S(1)}, u32[]{:S(2)}, u32[]{:S(2)}) collective-permute-start(bf16[192,384]{1,0:T(8,128)(2,1)S(1)} %pad_maximum_fusion.14), channel_id=1, source_target_pairs={{0,16},{4,20},{8,24},{12,28},{16,0},{20,4},{24,8},{28,12},{1,17},{... | collective-permute-start | bytes 442376 | tf_op jit(solution)/shard_map/ppermute | solution.py:381
  250.8 7.2 %collective-permute-start.35 = (bf16[448,384]{1,0:T(8,128)(2,1)S(1)}, bf16[448,384]{1,0:T(8,128)(2,1)S(1)}, u32[]{:S(2)}, u32[]{:S(2)}) collective-permute-start(bf16[448,384]{1,0:T(8,128)(2,1)S(1)} %pad_maximum_fusion.10), channel_id=1, source_target_pairs={{0,16},{4,20},{8,24},{12,28},{16,0},{20,4},{24,8},{28,12},{1,17},{... | collective-permute-start | bytes 1032200 | tf_op jit(solution)/shard_map/ppermute | solution.py:381
  258.0 9.3 %collective-permute-start.26 = (bf16[384,384]{1,0:T(8,128)(2,1)S(1)}, bf16[384,384]{1,0:T(8,128)(2,1)S(1)}, u32[]{:S(2)}, u32[]{:S(2)}) collective-permute-start(bf16[384,384]{1,0:T(8,128)(2,1)S(1)} %pad_maximum_fusion.11), channel_id=1, source_target_pairs={{0,8},{4,12},{8,0},{12,4},{16,24},{20,28},{24,16},{28,20},{1,9},{5... | collective-permute-start | bytes 884744 | tf_op jit(solution)/shard_map/ppermute | solution.py:381
  258.3 16.5 %collective-permute-start.36 = (bf16[896,384]{1,0:T(8,128)(2,1)S(1)}, bf16[896,384]{1,0:T(8,128)(2,1)S(1)}, u32[]{:S(2)}, u32[]{:S(2)}) collective-permute-start(bf16[896,384]{1,0:T(8,128)(2,1)S(1)} %pad_maximum_fusion.8), channel_id=1, source_target_pairs={{0,8},{4,12},{8,0},{12,4},{16,24},{20,28},{24,16},{28,20},{1,9},{5... | collective-permute-start | bytes 2064392 | tf_op jit(solution)/shard_map/ppermute | solution.py:381
  260.4 14.9 %collective-permute-start.17 = (bf16[3,128,384]{2,1,0:T(8,128)(2,1)S(1)}, bf16[3,128,384]{2,1,0:T(8,128)(2,1)S(1)}, u32[]{:S(2)}, u32[]{:S(2)}) collective-permute-start(bf16[3,128,384]{2,1,0:T(8,128)(2,1)S(1)} %copy-done.45), channel_id=1, source_target_pairs={{0,3},{1,2},{2,1},{3,0},{4,7},{5,6},{6,5},{7,4},{8,11},{9,10},{10,... | collective-permute-start | bytes 884744 | tf_op jit(solution)/shard_map/ppermute | solution.py:366
  267.5 7.9 %collective-permute-start.27 = (bf16[768,384]{1,0:T(8,128)(2,1)S(1)}, bf16[768,384]{1,0:T(8,128)(2,1)S(1)}, u32[]{:S(2)}, u32[]{:S(2)}) collective-permute-start(bf16[768,384]{1,0:T(8,128)(2,1)S(1)} %pad_maximum_fusion.9), channel_id=1, source_target_pairs={{0,4},{4,0},{8,12},{12,8},{16,20},{20,16},{24,28},{28,24},{1,5},{5... | collective-permute-start | bytes 1769480 | tf_op jit(solution)/shard_map/ppermute | solution.py:381
  (55 other events, 382.9 us)

commit v2 on v1

v2 whole, which is shorter than its diff:
```python
import functools
import math

import jax
import jax.numpy as jnp
from jax import lax
from jax.experimental import pallas as pl
from jax.experimental.pallas import tpu as pltpu
from jax.sharding import PartitionSpec as P

HEADS = 12
HD = 32
GROUPS = 3
PER_GROUP = HEADS // GROUPS
AUG = 16
BIG = 2.0**100
SMALL_SCORE = 60.0
EPSILON = 1e-05
SCALE = HD ** (-0.5)
LOG2E = math.log2(math.e)
Q_FACTOR = SCALE * LOG2E
LN2 = math.log(2.0)
VMEM_LIMIT = 60 * 2**20

f32 = jnp.float32
bf16 = jnp.bfloat16
NN = (((1,), (0,)), ((), ()))
NT = (((1,), (1,)), ((), ()))
TN = (((0,), (0,)), ((), ()))


def dot(left, right, dims=NN):
    return lax.dot_general(left, right, dims, preferred_element_type=f32)


def fold_lanes(values):
    total = values[:, :128]
    for start in range(128, values.shape[1], 128):
        total = total + values[:, start : start + 128]
    return total


def row_sum(partial):
    return jnp.sum(partial.T, axis=0, keepdims=True)


def normalize(hidden):
    scale = 1.0 / hidden.shape[0]
    centre = hidden - jnp.sum(hidden, axis=0, keepdims=True) * scale
    variance = jnp.sum(centre * centre, axis=0, keepdims=True) * scale
    inverse = lax.rsqrt(variance + EPSILON)
    return centre * inverse, inverse


def normalize_back(upstream, scaled, inverse):
    scale = 1.0 / upstream.shape[0]
    mean = jnp.sum(upstream, axis=0, keepdims=True) * scale
    spread = jnp.sum(upstream * scaled, axis=0, keepdims=True) * scale
    return inverse * (upstream - mean - scaled * spread)


def gelu_parts(v):
    cdf = 0.5 + 0.5 * lax.erf(v * 0.5**0.5)
    bell = jnp.exp2((v * v) * (-0.5 * LOG2E))
    return v * cdf, cdf + v * bell * (2.0 * math.pi) ** (-0.5)


def prepare_kernel(wq, wk, wv, wo, wup, wdn, rows, wq_t, wk_t, wv_t, wo_t, wup_t, wdn_t, columns):
    for source, target in ((wq, wq_t), (wk, wk_t), (wv, wv_t), (wo, wo_t), (wup, wup_t), (wdn, wdn_t)):
        target[...] = source[...].T
    width = rows.shape[1]
    columns[...] = jnp.concatenate([rows[...], jnp.zeros((128 - rows.shape[0], width), f32)], axis=0).T


def prepare(weights, rows):
    shapes = [jax.ShapeDtypeStruct(w.shape[::-1], w.dtype) for w in weights]
    shapes.append(jax.ShapeDtypeStruct((rows.shape[1], 128), f32))
    return pl.pallas_call(
        prepare_kernel,
        out_shape=shapes,
        compiler_params=pltpu.CompilerParams(vmem_limit_bytes=VMEM_LIMIT),
        cost_estimate=cost(5),
        name="prepare",
    )(*weights, rows)


def cost(micros):
    return pl.CostEstimate(flops=int(micros * 5e8), transcendentals=0, bytes_accessed=int(micros * 2e6))


B_QUERY, B_VALUE, B_OUT, GAIN1, SHIFT1, B_DOWN, GAIN2, SHIFT2, B_UP = range(9)


def forward_kernel(*refs, pieces, carried):
    x_refs = refs[:pieces]
    aug_ref, cols, wq, wk, wv, wo, wup, wdn = refs[pieces : pieces + 8]
    outs = refs[pieces + 8 + carried :]
    lo_refs = outs[:pieces]
    (
        xt_ref, qt_ref, kt_ref, vt_ref, p_ref, att_ref, s1_ref, s2_ref, stat_ref, act_ref, slope_ref, small_ref,
    ) = outs[pieces:]
    group = pl.program_id(1)
    span = x_refs[0].shape[1]

    def column(index):
        return cols[:, index : index + 1]

    @pl.when(group == 0)
    def _():
        xt = jnp.concatenate([ref[0].T for ref in x_refs], axis=1)
        xt_ref[0] = xt
        query = (dot(wq[...], xt) + column(B_QUERY)) * Q_FACTOR
        key = dot(wk[...], xt)
        qt_ref[0] = query.astype(bf16)
        kt_ref[0] = key.astype(bf16)
        bounds = [
            jnp.max(head_sums(query * query), axis=1, keepdims=True),
            jnp.max(head_sums(key * key), axis=1, keepdims=True),
        ]
        small_ref[0] = (jnp.max(bounds[0] * bounds[1]) < SMALL_SCORE**2).astype(jnp.int32)
        vt_ref[0] = (dot(wv[...], xt) + column(B_VALUE)).astype(bf16)

    length = xt_ref.shape[2]
    ones = jnp.ones((AUG, length), bf16)

    def rows(ref, h):
        return ref[0, pl.ds(pl.multiple_of((group * PER_GROUP + h) * HD, HD), HD), :]

    def score(h):
        keys = jnp.concatenate([rows(kt_ref, h), aug_ref[0, AUG:]], axis=0)
        query = jnp.concatenate([rows(qt_ref, h), aug_ref[0, :AUG]], axis=0)
        return dot(keys, query, TN)

    def mix(h):
        values = jnp.concatenate([rows(vt_ref, h), ones], axis=0)
        mixed = dot(values, p_ref[0, h])
        inverse = 1.0 / mixed[HD : HD + 1]
        att_ref[0, pl.ds(pl.multiple_of((group * PER_GROUP + h) * HD, HD), HD), :] = mixed[:HD] * inverse
        stat_ref[0, pl.ds(group * PER_GROUP + h, 1), :] = inverse

    def heads(shifted):
        scores = score(0)
        for h in range(PER_GROUP):
            following = score(h + 1) if h + 1 < PER_GROUP else None
            if h >= 1:
                mix(h - 1)
            if shifted:
                scores = scores - jnp.max(scores, axis=0, keepdims=True)
            p_ref[0, h] = jnp.exp2(scores).astype(bf16)
            scores = following
        mix(PER_GROUP - 1)

    @pl.when(small_ref[0] == 1)
    def _():
        heads(False)

    @pl.when(small_ref[0] == 0)
    def _():
        heads(True)

    @pl.when(group == GROUPS - 1)
    def _():
        res1 = xt_ref[0].astype(f32) + dot(wo[...], att_ref[0].astype(bf16)) + column(B_OUT)
        scaled1, inverse1 = normalize(res1)
        s1_ref[0] = scaled1
        stat_ref[0, HEADS : HEADS + 1] = inverse1
        normed = scaled1 * column(GAIN1) + shift_of(cols, SHIFT1)
        ff = wup.shape[0]
        width = wup.shape[1]
        b_up = jnp.concatenate([column(B_UP + i) for i in range(ff // width)], axis=0)
        upward = dot(wup[...], normed.astype(bf16)) + b_up
        act, slope = gelu_parts(upward)
        act_b = act.astype(bf16)
        act_ref[0] = act_b
        slope_ref[0] = slope.astype(bf16)
        res2 = normed + dot(wdn[...], act_b) + column(B_DOWN)
        scaled2, inverse2 = normalize(res2)
        s2_ref[0] = scaled2
        stat_ref[0, HEADS + 1 : HEADS + 2] = inverse2
        out = (scaled2 * column(GAIN2) + column(SHIFT2)).astype(bf16)
        for index, ref in enumerate(lo_refs):
            ref[0] = out[:, index * span : (index + 1) * span].T


def head_sums(values):
    return jnp.sum(values.reshape(HEADS, HD, values.shape[1]), axis=1)


def shift_of(cols, index):
    return cols[:, index : index + 1]


def forward(pieces, base, total, aug, weights, carried):
    rows, span, width = pieces[0].shape
    count = len(pieces)
    length = span * count
    ff = weights[5].shape[0]
    piece_spec = pl.BlockSpec((1, span, width), lambda r, g: (r, 0, 0))
    full = lambda a: pl.BlockSpec(a.shape, lambda r, g: (0, 0))

    def tall(height):
        return pl.BlockSpec((1, height, length), lambda r, g: (r + base, 0, 0))

    saved_specs = [tall(width)] * 4 + [
        pl.BlockSpec((1, PER_GROUP, length, length), lambda r, g: (r + base, g, 0, 0)),
        tall(width), tall(width), tall(width), tall(16), tall(ff), tall(ff),
    ]
    saved_shapes = [jax.ShapeDtypeStruct((total, width, length), bf16)] * 4 + [
        jax.ShapeDtypeStruct((total, HEADS, length, length), bf16),
        jax.ShapeDtypeStruct((total, width, length), f32),
        jax.ShapeDtypeStruct((total, width, length), f32),
        jax.ShapeDtypeStruct((total, width, length), f32),
        jax.ShapeDtypeStruct((total, 16, length), f32),
        jax.ShapeDtypeStruct((total, ff, length), bf16),
        jax.ShapeDtypeStruct((total, ff, length), bf16),
    ]
    first = count + 1 + len(weights)
    out = pl.pallas_call(
        functools.partial(forward_kernel, pieces=count, carried=len(carried)),
        grid=(rows, GROUPS),
        in_specs=[piece_spec] * count
        + [pl.BlockSpec((1, 2 * AUG, length), lambda r, g: (r + base, 0, 0))]
        + [full(w) for w in weights]
        + [pl.BlockSpec(memory_space=pl.ANY)] * len(carried),
        out_specs=[pl.BlockSpec((1, span, width), lambda r, g: (r + base, 0, 0))] * count + saved_specs,
        out_shape=[jax.ShapeDtypeStruct((total, span, width), bf16)] * count + saved_shapes,
        scratch_shapes=[pltpu.SMEM((1,), jnp.int32)],
        input_output_aliases={first + i: i for i in range(len(carried))},
        compiler_params=pltpu.CompilerParams(vmem_limit_bytes=VMEM_LIMIT),
        cost_estimate=cost(14 * rows),
        name="forward",
    )(*pieces, aug, *weights, *carried)
    return out


def emit(packed, index, outs, inner):
    size = outs[0].shape[0] // inner
    for shift, ref in enumerate(outs):
        for block in range(inner):
            start = pl.multiple_of((block * len(outs) + (index ^ shift)) * size, 16)
            ref[block * size : (block + 1) * size] = packed[pl.ds(start, size), :]


def dense_kernel(*refs, pieces, rows, parts, inner):
    index_ref = refs[0]
    cot_refs = refs[1 : 1 + pieces]
    (
        att_ref, s1_ref, s2_ref, stat_ref, act_ref, slope_ref, cols, wo, wup, wdn,
    ) = refs[1 + pieces : 11 + pieces]
    gres_ref, og_ref, delta_ref = refs[11 + pieces : 14 + pieces]
    part_refs = refs[14 + pieces : 14 + pieces + parts]
    acc_dn, acc_up, acc_out, acc_bias, acc_upb, packed = refs[14 + pieces + parts :]
    step = pl.program_id(0)
    width = s1_ref.shape[1]
    ff = acc_up.shape[1]

    def column(index):
        return cols[:, index : index + 1]

    @pl.when(step == 0)
    def _():
        for ref in (acc_dn, acc_up, acc_out, acc_bias, acc_upb):
            ref[...] = jnp.zeros_like(ref)

    att = att_ref[0]
    att_b = att.astype(bf16)
    scaled1 = s1_ref[0]
    scaled2 = s2_ref[0]
    inverse1 = stat_ref[0, HEADS : HEADS + 1]
    inverse2 = stat_ref[0, HEADS + 1 : HEADS + 2]
    normed_b = (scaled1 * column(GAIN1) + column(SHIFT1)).astype(bf16)
    act_b = act_ref[0]
    cot = jnp.concatenate([ref[0].T for ref in cot_refs], axis=1).astype(f32)
    acc_bias[0] += fold_lanes(cot * scaled2)
    acc_bias[1] += fold_lanes(cot)
    gres2 = normalize_back(cot * column(GAIN2), scaled2, inverse2)
    down_b = gres2.astype(bf16)
    acc_bias[2] += fold_lanes(down_b.astype(f32))
    up_b = (dot(wdn[...], down_b) * slope_ref[0].astype(f32)).astype(bf16)
    acc_dn[...] += dot(act_b, down_b, NT)
    acc_upb[...] += fold_lanes(up_b.astype(f32))
    gnormed = gres2 + dot(wup[...], up_b)
    acc_up[...] += dot(normed_b, up_b, NT)
    acc_bias[3] += fold_lanes(gnormed * scaled1)
    acc_bias[4] += fold_lanes(gnormed)
    gres1 = normalize_back(gnormed * column(GAIN1), scaled1, inverse1)
    gres_ref[0] = gres1
    branch_b = gres1.astype(bf16)
    acc_bias[5] += fold_lanes(branch_b.astype(f32))
    og = dot(wo[...], branch_b)
    acc_out[...] += dot(att_b, branch_b, NT)
    for h in range(HEADS):
        part = slice(h * HD, (h + 1) * HD)
        scaled_og = (og[part] * stat_ref[0, h : h + 1, :]).astype(bf16)
        og_ref[0, part, :] = scaled_og
        delta_ref[0, h : h + 1, :] = jnp.sum(scaled_og.astype(f32) * att[part], axis=0, keepdims=True)

    @pl.when(step == rows - 1)
    def _():
        packed[:ff] = acc_dn[...].astype(bf16)
        for index in range(ff // width):
            packed[ff + index * width : ff + (index + 1) * width] = acc_up[
                :, index * width : (index + 1) * width
            ].astype(bf16)
        packed[2 * ff : 2 * ff + width] = acc_out[...].astype(bf16)
        bias_rows = [row_sum(acc_bias[i]) for i in range(6)]
        bias_rows += [row_sum(acc_upb[i * width : (i + 1) * width]) for i in range(ff // width)]
        tail = packed.shape[0] - 2 * ff - width
        bias_rows.append(jnp.zeros((tail - len(bias_rows), width), f32))
        packed[2 * ff + width :] = jnp.concatenate(bias_rows, axis=0).astype(bf16)
        emit(packed, index_ref[0], part_refs, inner)


def dense(pieces, saved, cols, weights, packed_rows, parts, inner, index):
    rows, span, width = pieces[0].shape
    count = len(pieces)
    length = span * count
    ff = weights[2].shape[0]
    piece_spec = pl.BlockSpec((1, span, width), lambda r, i: (r, 0, 0))
    full = lambda a: pl.BlockSpec(a.shape, lambda r, i: (0, 0))

    def tall(height):
        return pl.BlockSpec((1, height, length), lambda r, i: (r, 0, 0))

    part = (packed_rows // parts, width)
    out = pl.pallas_call(
        functools.partial(dense_kernel, pieces=count, rows=rows, parts=parts, inner=inner),
        grid_spec=pltpu.PrefetchScalarGridSpec(
            num_scalar_prefetch=1,
            grid=(rows,),
            in_specs=[piece_spec] * count
            + [tall(a.shape[1]) for a in saved]
            + [full(cols)]
            + [full(w) for w in weights],
            out_specs=[tall(width), tall(width), tall(16)] + [pl.BlockSpec(part, lambda r, i: (0, 0))] * parts,
            scratch_shapes=[
                pltpu.VMEM((ff, width), f32),
                pltpu.VMEM((width, ff), f32),
                pltpu.VMEM((width, width), f32),
                pltpu.VMEM((6, width, 128), f32),
                pltpu.VMEM((ff, 128), f32),
                pltpu.VMEM((packed_rows, width), bf16),
            ],
        ),
        out_shape=[
            jax.ShapeDtypeStruct((rows, width, length), f32),
            jax.ShapeDtypeStruct((rows, width, length), bf16),
            jax.ShapeDtypeStruct((rows, 16, length), f32),
        ]
        + [jax.ShapeDtypeStruct(part, bf16)] * parts,
        compiler_params=pltpu.CompilerParams(vmem_limit_bytes=VMEM_LIMIT),
        cost_estimate=cost(20),
        name="dense",
    )(index, *pieces, *saved, cols, *weights)
    return out[0], out[1], out[2], out[3:]


def back_kernel(*refs, pieces, parts, inner, carried, after):
    index_ref, xt_ref, qt_ref, kt_ref, vt_ref, og_ref, delta_ref, p_ref, gres_ref, w_ref = refs[:10]
    if carried:
        acc_in, bias_in = refs[10:12]
    out_refs = refs[10 + carried + after : 10 + carried + after + pieces]
    rest = refs[10 + carried + after + pieces :]
    if parts:
        part_refs, (grads, held, packed) = rest[:parts], rest[parts:]
    else:
        acc_ref, bias_ref, grads, held = rest
    group = pl.program_id(1)
    length = xt_ref.shape[2]
    width = xt_ref.shape[1]
    span = out_refs[0].shape[1]

    def start_of(h):
        return pl.multiple_of((group * PER_GROUP + h) * HD, HD)

    def rows_of(ref, h):
        return ref[0, pl.ds(start_of(h), HD), :]

    sign = jnp.where(lax.broadcasted_iota(jnp.int32, (AUG, length), 0) < 3, 1.0, 0.0).astype(bf16)

    def grad_probs(h):
        delta = delta_ref[0, pl.ds(group * PER_GROUP + h, 1), :]
        first = delta.astype(bf16)
        rest = delta - first.astype(f32)
        second = rest.astype(bf16)
        third = (rest - second.astype(f32)).astype(bf16)
        aug = jnp.concatenate(
            [-first.astype(f32), -second.astype(f32), -third.astype(f32), jnp.zeros((AUG - 3, length), f32)], axis=0
        ).astype(bf16)
        left = jnp.concatenate([rows_of(vt_ref, h), sign], axis=0)
        right = jnp.concatenate([rows_of(og_ref, h), aug], axis=0)
        return dot(left, right, TN)

    for h in range(PER_GROUP):
        probs = p_ref[0, h]
        held[h] = (probs.astype(f32) * grad_probs(h)).astype(bf16)
        grads[pl.ds(2 * width + start_of(h), HD), :] = dot(rows_of(og_ref, h), probs, NT).astype(bf16)
    for h in range(PER_GROUP):
        start = start_of(h)
        grads[pl.ds(start, HD), :] = (dot(rows_of(kt_ref, h), held[h]) * SCALE).astype(bf16)
        grads[pl.ds(width + start, HD), :] = (dot(rows_of(qt_ref, h), held[h], NT) * LN2).astype(bf16)

    @pl.when(group == GROUPS - 1)
    def _():
        total = grads[...]
        acc = dot(xt_ref[0], total, NT)
        bias_q = fold_lanes(total[:width].astype(f32))
        bias_v = fold_lanes(total[2 * width :].astype(f32))
        if carried:
            acc = acc + acc_in[...]
            bias_q = bias_q + bias_in[0]
            bias_v = bias_v + bias_in[1]
        if parts:
            for index in range(3 * width // 128):
                packed[index * width : (index + 1) * width] = acc[:, index * 128 : (index + 1) * 128].astype(bf16)
            bias_rows = []
            for bias in (bias_q, bias_v):
                flat = row_sum(bias)
                bias_rows += [flat[:, i * 128 : (i + 1) * 128] for i in range(width // 128)]
            tail = packed.shape[0] - 9 * width
            bias_rows.append(jnp.zeros((tail - len(bias_rows), 128), f32))
            packed[9 * width :] = jnp.concatenate(bias_rows, axis=0).astype(bf16)
            emit(packed, index_ref[0], part_refs, inner)
        else:
            acc_ref[...] = acc
            bias_ref[0] = bias_q
            bias_ref[1] = bias_v
        result = (gres_ref[0] + dot(w_ref[...], total)).astype(bf16)
        for index, ref in enumerate(out_refs):
            ref[0] = result[:, index * span : (index + 1) * span].T


def back(
    shared, at, row, saved, gres, og, delta, probs, w_all, packed_rows, parts, inner, index, sums, after
):
    count = len(shared) if isinstance(shared, (list, tuple)) else shared
    fresh = not isinstance(shared, (list, tuple))
    height = -at if fresh else shared[0].shape[0]
    target = 0 if fresh else at
    carried = list(sums)
    xt, qt, kt, vt = saved
    rows, width, length = xt.shape
    span = length // count
    wide = pl.BlockSpec((1, width, length), lambda r, g, i: (row, 0, 0))
    sums = [((width, 3 * width), lambda r, g, i: (0, 0)), ((2, width, 128), lambda r, g, i: (0, 0, 0))]
    sum_specs = [pl.BlockSpec(*s) for s in sums]
    part = (packed_rows // max(parts, 1), 128)
    if parts:
        last_specs = [pl.BlockSpec(part, lambda r, g, i: (0, 0))] * parts
        last_shapes = [jax.ShapeDtypeStruct(part, bf16)] * parts
    else:
        last_specs = sum_specs
        last_shapes = [jax.ShapeDtypeStruct(s[0], f32) for s in sums]
    scratch = [pltpu.VMEM((3 * width, length), bf16), pltpu.VMEM((PER_GROUP, length, length), bf16)]
    if parts:
        scratch.append(pltpu.VMEM((packed_rows, 128), bf16))
    out = pl.pallas_call(
        functools.partial(
            back_kernel, pieces=count, parts=parts, inner=inner, carried=len(carried), after=len(after) + (0 if fresh else count)
        ),
        grid_spec=pltpu.PrefetchScalarGridSpec(
            num_scalar_prefetch=1,
            grid=(1, GROUPS),
            in_specs=[wide] * 5
            + [
                pl.BlockSpec((1, 16, length), lambda r, g, i: (row, 0, 0)),
                pl.BlockSpec((1, PER_GROUP, length, length), lambda r, g, i: (row, g, 0, 0)),
                wide,
                pl.BlockSpec(w_all.shape, lambda r, g, i: (0, 0)),
            ]
            + (sum_specs if carried else [])
            + ([] if fresh else [pl.BlockSpec(memory_space=pl.ANY)] * count)
            + [pl.BlockSpec(memory_space=pl.ANY)] * len(after),
            out_specs=[pl.BlockSpec((1, span, width), lambda r, g, i: (target, 0, 0))] * count + last_specs,
            scratch_shapes=scratch,
        ),
        out_shape=[jax.ShapeDtypeStruct((height, span, width), bf16)] * count + last_shapes,
        input_output_aliases={} if fresh else {10 + len(carried) + i: i for i in range(count)},
        compiler_params=pltpu.CompilerParams(vmem_limit_bytes=VMEM_LIMIT),
        cost_estimate=cost(10),
        name="back",
    )(index, xt, qt, kt, vt, og, delta, probs, gres, w_all, *carried, *([] if fresh else shared), *after)
    return out[:count], out[count:]


def exchange(pieces, axis, devices, unit=1):
    moved = [pieces[0]]
    for shift in range(1, len(pieces)):
        moved.append(lax.ppermute(pieces[shift], axis, [(i, i ^ (shift * unit)) for i in range(devices)]))
    return moved


def tree_sum(blocks):
    while len(blocks) > 1:
        blocks = [left + right for left, right in zip(blocks[::2], blocks[1::2])]
    return blocks[0]


def combine_kernel(index_ref, *refs, inputs, after, inner):
    total = tree_sum([ref[...].astype(f32) for ref in refs[:inputs]]).astype(bf16)
    outs = refs[inputs + after :]
    if len(outs) == 1:
        outs[0][...] = total
    else:
        packed = outs[-1]
        packed[...] = total
        emit(packed, index_ref[0], outs[:-1], inner)


def combine(blocks, parts, inner, index, after=()):
    rows, width = blocks[0].shape
    part = (rows // parts, width)
    full = lambda s: pl.BlockSpec(s, lambda i, j: (0, 0))
    return pl.pallas_call(
        functools.partial(combine_kernel, inputs=len(blocks), after=len(after), inner=inner),
        grid_spec=pltpu.PrefetchScalarGridSpec(
            num_scalar_prefetch=1,
            grid=(1,),
            in_specs=[full((rows, width))] * len(blocks) + [pl.BlockSpec(memory_space=pl.ANY)] * len(after),
            out_specs=[full(part)] * parts,
            scratch_shapes=[pltpu.VMEM((rows, width), bf16)] if parts > 1 else [],
        ),
        out_shape=[jax.ShapeDtypeStruct(part, bf16)] * parts,
        compiler_params=pltpu.CompilerParams(vmem_limit_bytes=VMEM_LIMIT),
        cost_estimate=cost(1),
        name="combine",
    )(index, *blocks, *after)


def assemble_kernel(index_ref, *refs, inputs):
    out = refs[-1]
    size = refs[0].shape[0]
    for shift, ref in enumerate(refs[:inputs]):
        out[pl.ds(pl.multiple_of((index_ref[0] ^ shift) * size, 16), size), :] = ref[...]


def assemble(blocks, index, after=()):
    rows, width = blocks[0].shape
    full = lambda s: pl.BlockSpec(s, lambda i, j: (0, 0))
    shape = (rows * len(blocks), width)
    return pl.pallas_call(
        functools.partial(assemble_kernel, inputs=len(blocks)),
        grid_spec=pltpu.PrefetchScalarGridSpec(
            num_scalar_prefetch=1,
            grid=(1,),
            in_specs=[full((rows, width))] * len(blocks) + [pl.BlockSpec(memory_space=pl.ANY)] * len(after),
            out_specs=full(shape),
        ),
        out_shape=jax.ShapeDtypeStruct(shape, bf16),
        compiler_params=pltpu.CompilerParams(vmem_limit_bytes=VMEM_LIMIT),
        cost_estimate=cost(1),
        name="assemble",
    )(index, *blocks, *after)


def place_kernel(index_ref, *refs, sets, count):
    out = refs[-1]
    row = pl.program_id(0)
    start = 0
    for number, size in enumerate(sets):

        @pl.when((row >= start) & (row < start + size))
        def _(number=number):
            for shift in range(count):
                out[index_ref[0] ^ shift] = refs[number * count + shift][...].astype(out.dtype)

        start += size


def place(sets, dtype, index, after=()):
    sizes = [pieces[0].shape[0] for pieces in sets]
    count = len(sets[0])
    rows = sum(sizes)
    _, span, width = sets[0][0].shape
    shape = (count, rows, span, width)
    in_specs = []
    start = 0
    for size in sizes:
        block = lambda r, i, start=start, size=size: (jnp.clip(r - start, 0, size - 1), 0, 0)
        in_specs += [pl.BlockSpec((1, span, width), block)] * count
        start += size
    out = pl.pallas_call(
        functools.partial(place_kernel, sets=sizes, count=count),
        grid_spec=pltpu.PrefetchScalarGridSpec(
            num_scalar_prefetch=1,
            grid=(rows,),
            in_specs=in_specs + [pl.BlockSpec(memory_space=pl.ANY)] * len(after),
            out_specs=pl.BlockSpec((count, 1, span, width), lambda r, i: (0, r, 0, 0)),
        ),
        out_shape=jax.ShapeDtypeStruct(shape, dtype),
        compiler_params=pltpu.CompilerParams(vmem_limit_bytes=VMEM_LIMIT),
        cost_estimate=cost(3),
        name="place",
    )(index, *[piece for pieces in sets for piece in pieces], *after)
    return out.reshape(count * rows, span, width)


def sum_stages(sizes):
    stages = []
    for axis in ("rows", "seq"):
        devices = sizes[axis]
        unit = 1
        while unit < devices:
            size = 2 if unit == 1 and devices.bit_length() % 2 == 0 else 4
            stages.append((axis, devices, unit, size, devices // (unit * size)))
            unit *= size
    return stages


def place_of(stage):
    axis, _, unit, size, _ = stage
    return ((lax.axis_index(axis) // unit) % size).astype(jnp.int32).reshape(1)


def send_parts(parts, stage):
    axis, devices, unit, _, _ = stage
    return exchange(parts, axis, devices, unit)


def cut_for(taken, stage, after=()):
    return combine(taken, stage[3], stage[4], place_of(stage), after)


def add(taken, after=()):
    return combine(taken, 1, 1, jnp.zeros((1,), jnp.int32), after)[0]


def unpack_later_kernel(block, down, up, out, *biases):
    ff, width = down.shape
    down[...] = block[:ff].astype(f32)
    for index in range(ff // width):
        up[:, index * width : (index + 1) * width] = block[ff + index * width : ff + (index + 1) * width].astype(f32)
    out[...] = block[2 * ff : 2 * ff + width].astype(f32)
    rows = block[2 * ff + width : 2 * ff + width + 16].astype(f32)
    for index, ref in enumerate(biases[:-1]):
        ref[...] = rows[index]
    per = ff // width
    biases[-1][...] = jnp.concatenate([rows[len(biases) - 1 + i] for i in range(per)], axis=0)


def unpack_later(block, width, ff):
    shapes = [(ff, width), (width, ff), (width, width)] + [(width,)] * 6 + [(ff,)]
    return pl.pallas_call(
        unpack_later_kernel,
        out_shape=[jax.ShapeDtypeStruct(s, f32) for s in shapes],
        compiler_params=pltpu.CompilerParams(vmem_limit_bytes=VMEM_LIMIT),
        cost_estimate=cost(4),
        name="unpack_later",
    )(block)


def unpack_early_kernel(block, query, key, value, bias_q, bias_v):
    width = query.shape[0]
    per = width // 128
    for number, ref in enumerate((query, key, value)):
        for index in range(per):
            start = (number * per + index) * width
            ref[:, index * 128 : (index + 1) * 128] = block[start : start + width].astype(f32)
    rows = block[3 * per * width : 3 * per * width + 16].astype(f32)
    for number, ref in enumerate((bias_q, bias_v)):
        ref[...] = jnp.concatenate([rows[number * per + i] for i in range(per)], axis=0)


def unpack_early(block, width):
    shapes = [(width, width)] * 3 + [(width,)] * 2
    return pl.pallas_call(
        unpack_early_kernel,
        out_shape=[jax.ShapeDtypeStruct(s, f32) for s in shapes],
        compiler_params=pltpu.CompilerParams(vmem_limit_bytes=VMEM_LIMIT),
        cost_estimate=cost(2),
        name="unpack_early",
    )(block)


def round_up(value, unit):
    return -(-value // unit) * unit


def body(
    tokens, lengths, w_query, b_query, w_key, w_value, b_value, w_out, b_out, gain_attn, shift_attn,
    w_up, b_up, w_down, b_down, gain_ffn, shift_ffn, cotangent, *, sizes,
):
    count = sizes["seq"]
    devices = count * sizes["rows"]
    row_count, span, width = tokens.shape
    ff = w_up.shape[1]
    length = span * count
    rows = row_count // count
    me = lax.axis_index("seq")
    order = me ^ jnp.arange(count, dtype=jnp.int32)

    def send(array, start, stop):
        parts = jnp.take(array.reshape(count, rows, span, width)[:, start:stop], order, axis=0)
        return exchange([parts[s] for s in range(count)], "seq", count)

    chunks = [(0, 1), (1, rows)] if rows > 1 else [(0, rows)]
    token_rows = [send(tokens, *chunk) for chunk in chunks]
    cot_moved = send(cotangent, 0, rows)

    bounds = lax.dynamic_slice_in_dim(jnp.cumsum(lengths, axis=1), me * rows, rows, 0)
    places = (order[:, None] * span + jnp.arange(span, dtype=jnp.int32)[None, :]).reshape(length)
    segment = jnp.sum((places[None, None, :] >= bounds[:, :, None]).astype(jnp.int32), axis=1)
    ids = jnp.arange(2 * AUG, dtype=jnp.int32)[None, :, None]
    same = segment[:, None, :] == ids % AUG
    aug = jnp.where(ids < AUG, jnp.where(same, 1.0, 0.0), jnp.where(same | (ids % AUG >= lengths.shape[1]), 0.0, -BIG))
    aug = aug.astype(bf16)

    vectors = [b_query, b_value, b_out, gain_attn, shift_attn, b_down, gain_ffn, shift_ffn]
    vectors = jnp.concatenate([jnp.stack(vectors), b_up.reshape(-1, width)], axis=0)
    *turned, cols = prepare((w_query, w_key, w_value, w_out, w_up, w_down), vectors)
    carried = []
    for (start, _), pieces in zip(chunks, token_rows):
        carried = forward(pieces, start, rows, aug, [cols] + turned, carried)
    lo_moved = exchange(carried[:count], "seq", count)
    carried = carried[count:]
    stages = sum_stages(sizes)
    row_stages, seq_stages = [[stage for stage in stages if stage[0] == axis] for axis in ("rows", "seq")]
    first = stages[0]
    index = place_of(first)
    later_rows = round_up(2 * ff + width + 16, 16 * devices)
    gres, og, delta, later = dense(
        cot_moved, carried[5:], cols, (w_out, w_up, w_down), later_rows, first[3], first[4], index
    )
    w_all = jnp.concatenate([w_query, w_key, w_value], axis=1)
    first_rows = round_up(9 * width + 16, 16 * devices)

    def back_row(shared, at, row, sums, after):
        parts = first[3] if row == rows - 1 else 0
        return back(
            shared, at, row, carried[:4], gres, og, delta, carried[4], w_all, first_rows, parts, first[4], index, sums,
            after,
        )

    number = 0
    taken = send_parts(later, stages[0])
    sums = []
    done = []
    sets = []
    shared = None
    waits = []
    for row in range(rows):
        if number + 1 < len(stages):
            number += 1
            later = cut_for(taken, stages[number], done)
            waits += list(later)
            taken = send_parts(later, stages[number])
        elif taken is not None:
            later = add(taken, done)
            waits.append(later)
            taken = None
        if row == 0:
            waits += lo_moved[2:3]
        elif row == 1:
            waits += lo_moved[1:2] + lo_moved[3:]
        if row >= 2:
            waits += sets[row - 2][1:]
        shared, sums = back_row(count, -1, row, sums, waits)
        done = sums[:1]
        waits = []
        if row < rows - 1:
            sets.append(exchange(shared, "seq", count))
    while number + 1 < len(stages):
        number += 1
        later = cut_for(taken, stages[number], done)
        taken = send_parts(later, stages[number])
    if taken is not None:
        later = add(taken, done)
    waits = list(sets[-1][1:]) if sets else []
    early = sums
    for number, stage in enumerate(row_stages):
        taken = send_parts(early, stage)
        if number + 1 < len(row_stages):
            early = cut_for(taken, row_stages[number + 1])
    early = add(taken)
    for stage in reversed(seq_stages):
        later = assemble(send_parts([later] * stage[3], stage), place_of(stage), list(done) + waits)
        waits = []
    later = lax.all_gather(later, "rows", axis=0, tiled=True)
    for stage in seq_stages:
        early = add(send_parts([early] * stage[3], stage))
    here = me.astype(jnp.int32).reshape(1)
    layer_out = place([lo_moved], bf16, here, done)
    sets.append(exchange(shared, "seq", count))
    grad_tokens = place(sets, f32, here, [early])
    early = lax.all_gather(early, "rows", axis=0, tiled=True)
    (
        grad_down, grad_up, grad_output, grad_gain2, grad_shift2, grad_dnbias, grad_gain1, grad_shift1, grad_obias,
        grad_upbias,
    ) = unpack_later(later, width, ff)
    grad_query, grad_key, grad_value, grad_qbias, grad_vbias = unpack_early(early, width)
    return (
        layer_out, grad_tokens, grad_query, grad_qbias, grad_key, grad_value, grad_vbias, grad_output, grad_obias,
        grad_gain1, grad_shift1, grad_up, grad_upbias, grad_down, grad_dnbias, grad_gain2, grad_shift2,
    )


def solution(mesh):
    split = P("rows", "seq", None)
    in_specs = (split, P("rows", None)) + (P(),) * 15 + (split,)
    out_specs = (split, split) + (P(),) * 15
    sizes = dict(mesh.shape)
    return jax.shard_map(
        functools.partial(body, sizes=sizes), mesh=mesh, in_specs=in_specs, out_specs=out_specs, check_vma=False
    )
```

time: 286 us -> 247 us (0.86)
  Pallas kernels: 72.8 us -> 130 us
  waiting for transfers between devices: 68.9 us -> 20.5 us
  local copies, waits for them, and re-layouts: 51.2 us -> 15.6 us
  other arithmetic: 30.8 us -> 1.46 us
  between operations: 1.46 us -> 14.9 us
  blocking collectives: 0 us -> 12.3 us
  starting transfers between devices: 59.7 us -> 51.6 us
    pallas_call x3 -> x18, Pallas kernels: 72.8 us -> 130 us  [the longest x2 41.8 us: forward(): pl.pallas_call(functools.partial(forward_kernel, pieces=count, carried=le...]
    ppermute x38, waiting for transfers between devices: 68.9 us -> 20.5 us  [exchange(): lax.ppermute(pieces[shift], axis, [(i, i ^ shift * unit) for i in range(d...]
    concatenate x16 -> x0, other arithmetic: 24.6 us -> none  [the longest x6 21.5 us: body(): jnp.concatenate([f[i] for f in first], axis=0)]
    pallas_call x2 -> x0, local copies, waits for them, and re-layouts: 19.1 us -> none  [attend(): pl.pallas_call(functools.partial(attend_kernel, pieces=count, row_base=0)...]
    all_gather x0 -> x1, blocking collectives: none -> 12.3 us  [body(): early = lax.all_gather(early, 'rows', axis=0, tiled=True)]
    reshape x10 -> x1, local copies, waits for them, and re-layouts: 8.21 us -> 0.01 us  [body(): b_up.reshape(-1, width)]
    ppermute x38, starting transfers between devices: 59.7 us -> 51.6 us  [exchange(): lax.ppermute(pieces[shift], axis, [(i, i ^ shift * unit) for i in range(d...]
    slice x5 -> x2, local copies, waits for them, and re-layouts: 5.05 us -> 1.21 us  [send(): array.reshape(count, rows, span, width)[:, start:stop]]
  transfers between devices with their start and end apart: 38 -> 39, of which waited for: 17 -> 6; matrix products, arithmetic and copies ran while one was open for 24% -> 2% of each run, Pallas kernels for 3% -> 42%
where the time goes in v2:
time: 247 us
  Pallas kernels  130 us (53%)
  starting transfers between devices  51.6 us (21%)
  waiting for transfers between devices  20.5 us (8%)
  local copies, waits for them, and re-layouts  15.6 us (6%)
  between operations  14.9 us (6%)
  blocking collectives  12.3 us (5%)
    ppermute x38, starting transfers between devices, exchange(): lax.ppermute(pieces[shift], axis, [(i, i ^ shift * unit) for i in range(d...  51.6 us
    pallas_call x2, Pallas kernels, forward(): pl.pallas_call(functools.partial(forward_kernel, pieces=count, carried=le...  41.8 us
    pallas_call x3, Pallas kernels, back(): pl.pallas_call(functools.partial(back_kernel, pieces=count, parts=parts,...  36 us
    ppermute x38, waiting for transfers between devices, exchange(): lax.ppermute(pieces[shift], axis, [(i, i ^ shift * unit) for i in range(d...  20.5 us
    pallas_call x1, Pallas kernels, dense(): pl.pallas_call(functools.partial(dense_kernel, pieces=count, rows=rows, p...  20.1 us
    pallas_call x6, Pallas kernels, combine(): pl.pallas_call(functools.partial(combine_kernel, inputs=len(blocks), afte...  13.2 us
    all_gather x1, blocking collectives, body(): early = lax.all_gather(early, 'rows', axis=0, tiled=True)  12.3 us
    unnamed x116, local copies, waits for them, and re-layouts  8.39 us
  transfers between devices with their start and end apart: 39, of which 6 were waited for; matrix products, arithmetic and copies ran while one was open for 2% of the time, Pallas kernels for 42%

profile of v2, /device:TPU:0, one launch (start us, length us, event | category | flops | bytes accessed | tf_op | source)
XLA Modules:
  0.0 246.7 jit_solution(446841562125191003)
XLA Ops:
  9.9 3.0 %collective-permute-start.3 = (bf16[1,128,384]{2,1,0:T(8,128)(2,1)S(1)}, bf16[1,128,384]{2,1,0:T(8,128)(2,1)}, u32[]{:S(2)}, u32[]{:S(2)}) collective-permute-start(bf16[1,128,384]{2,1,0:T(8,128)(2,1)S(1)} %get-tuple-element.201), channel_id=1, source_target_pairs={{0,1},{1,0},{2,3},{3,2},{4,5},{5,4},{6,7},{7,6},{8,9},{9,8},{10,11... | collective-permute-start | bytes 294920 | tf_op jit(solution)/shard_map/ppermute | solution.py:489
  12.9 2.6 %collective-permute-start.4 = (bf16[1,128,384]{2,1,0:T(8,128)(2,1)S(1)}, bf16[1,128,384]{2,1,0:T(8,128)(2,1)}, u32[]{:S(2)}, u32[]{:S(2)}) collective-permute-start(bf16[1,128,384]{2,1,0:T(8,128)(2,1)S(1)} %get-tuple-element.200), channel_id=1, source_target_pairs={{0,2},{1,3},{2,0},{3,1},{4,6},{5,7},{6,4},{7,5},{8,10},{9,11},{10,... | collective-permute-start | bytes 294920 | tf_op jit(solution)/shard_map/ppermute | solution.py:489
  18.3 3.5 %collective-permute-start.1 = (bf16[2,128,384]{2,1,0:T(8,128)(2,1)S(1)}, bf16[2,128,384]{2,1,0:T(8,128)(2,1)}, u32[]{:S(2)}, u32[]{:S(2)}) collective-permute-start(bf16[2,128,384]{2,1,0:T(8,128)(2,1)S(1)} %get-tuple-element.196), channel_id=1, source_target_pairs={{0,2},{1,3},{2,0},{3,1},{4,6},{5,7},{6,4},{7,5},{8,10},{9,11},{10,... | collective-permute-start | bytes 589832 | tf_op jit(solution)/shard_map/ppermute | solution.py:489
  25.5 4.1 %prepare.1 = (bf16[384,384]{1,0:T(8,128)(2,1)}, bf16[384,384]{1,0:T(8,128)(2,1)}, bf16[384,384]{1,0:T(8,128)(2,1)}, bf16[384,384]{1,0:T(8,128)(2,1)}, bf16[1536,...) custom-call(bf16[384,384]{1,0:T(8,128)(2,1)} %wq.1, bf16[384,384]{1,0:T(8,128)(2,1)} %wk.1, ...), custom_call_target="tpu_custom_call" | custom-call | flops 2500000000 | bytes 10000000 | tf_op jit(solution)/shard_map/prepare/pallas_call | solution.py:78
  31.8 2.4 collective-permute-start.11
  34.2 15.4 %forward.2 = (bf16[3,128,384]{2,1,0:T(8,128)(2,1)}, bf16[3,128,384]{2,1,0:T(8,128)(2,1)}, bf16[3,128,384]{2,1,0:T(8,128)(2,1)}, bf16[3,128,384]{2,1,0:T(8,128)(2...) custom-call(bf16[1,128,384]{2,1,0:T(8,128)(2,1)} %get-tuple-element., ...), custom_call_target="tpu_custom_call" | custom-call | flops 7000000000 | bytes 28000000 | tf_op jit(solution)/shard_map/forward/pallas_call | solution.py:218
  51.6 26.4 %forward.3 = (bf16[3,128,384]{2,1,0:T(8,128)(2,1)}, bf16[3,128,384]{2,1,0:T(8,128)(2,1)}, bf16[3,128,384]{2,1,0:T(8,128)(2,1)}, bf16[3,128,384]{2,1,0:T(8,128)(2...) custom-call(bf16[2,128,384]{2,1,0:T(8,128)(2,1)} %get-tuple-element., ...), custom_call_target="tpu_custom_call", output_to_operand_aliasing={{0}: (12, {}), {1}: (13, {}), {2}: (14, {}), {3}: (15, {}),... | custom-call | flops 14000000000 | bytes 56000000 | tf_op jit(solution)/shard_map/forward/pallas_call | solution.py:218
  78.9 20.1 %dense.1 = (f32[3,384,512]{2,1,0:T(8,128)}, bf16[3,384,512]{2,1,0:T(8,128)(2,1)}, f32[3,16,512]{2,1,0:T(8,128)}, bf16[1792,384]{1,0:T(8,128)(2,1)}, bf16[1792,384]{1,0:T(8,128)(2,1)}) custom-call(s32[1]{0:T(128)} %bitcast.14.refs_0_, bf16[3,128,384]{2,1,0:T(8,128)(2,1)} %get-tuple-element.194.refs_1_, bf16[3,128,384]{2,1,0:T(8,128)(2,1)} %copy-done.34, ...), custom_call_target="tpu_custom_call" | custom-call | flops 10000000000 | bytes 40000000 | tf_op jit(solution)/shard_map/dense/pallas_call | solution.py:326
  99.1 5.8 %collective-permute-start.7 = (bf16[3,128,384]{2,1,0:T(8,128)(2,1)}, bf16[3,128,384]{2,1,0:T(8,128)(2,1)S(1)}, u32[]{:S(2)}, u32[]{:S(2)}) collective-permute-start(bf16[3,128,384]{2,1,0:T(8,128)(2,1)} %get-tuple-element.128), channel_id=1, source_target_pairs={{0,2},{1,3},{2,0},{3,1},{4,6},{5,7},{6,4},{7,5},{8,10},{9,11},{10,... | collective-permute-start | bytes 884744 | tf_op jit(solution)/shard_map/ppermute | solution.py:489
  105.2 2.1 collective-permute-start.8
  108.4 3.5 %combine.6 = (bf16[448,384]{1,0:T(8,128)(2,1)}, bf16[448,384]{1,0:T(8,128)(2,1)}, bf16[448,384]{1,0:T(8,128)(2,1)}, bf16[448,384]{1,0:T(8,128)(2,1)}) custom-call(s32[1]{0:T(128)} %bitcast.20.index_ref, bf16[1792,384]{1,0:T(8,128)(2,1)} %get-tuple-element.144.refs_0_, bf16[1792,384]{1,0:T(8,128)(2,1)} %copy-done.3), custom_call_target="tpu_custom_call" | custom-call | flops 500000000 | bytes 2000000 | tf_op jit(solution)/shard_map/combine/pallas_call | solution.py:514
  113.4 5.9 %collective-permute-done.7.refs_14_.refs_2_ = bf16[3,128,384]{2,1,0:T(8,128)(2,1)S(1)} collective-permute-done((bf16[3,128,384]{2,1,0:T(8,128)(2,1)}, bf16[3,128,384]{2,1,0:T(8,128)(2,1)S(1)}, u32[]{:S(2)}, u32[]{:S(2)}) %collective-permute-start.7) | collective-permute-done | bytes 294944 | tf_op jit(solution)/shard_map/ppermute | solution.py:489
  120.0 11.7 %back.3 = (bf16[1,128,384]{2,1,0:T(8,128)(2,1)}, bf16[1,128,384]{2,1,0:T(8,128)(2,1)}, bf16[1,128,384]{2,1,0:T(8,128)(2,1)}, bf16[1,128,384]{2,1,0:T(8,128)(2,1)...) custom-call(s32[1]{0:T(128)} %bitcast.14.refs_0_, bf16[3,384,512]{2,1,0:T(8,128)(2,1)} %get-tuple-element.130.refs_1_, ...), custom_call_target="tpu_custom_call" | custom-call | flops 5000000000 | bytes 20000000 | tf_op jit(solution)/shard_map/back/pallas_call | solution.py:457
  134.4 2.3 combine.7
  137.0 2.8 %collective-permute-start.17 = (bf16[112,384]{1,0:T(8,128)(2,1)}, bf16[112,384]{1,0:T(8,128)(2,1)S(1)}, u32[]{:S(2)}, u32[]{:S(2)}) collective-permute-start(bf16[112,384]{1,0:T(8,128)(2,1)} %get-tuple-element.154.refs_14_), channel_id=1, source_target_pairs={{0,2},{1,3},{2,0},{3,1},{4,6},{5,7},{6,4},{7,5},{8,10},{9,11},{10,... | collective-permute-start | bytes 258056 | tf_op jit(solution)/shard_map/ppermute | solution.py:489
  141.2 12.3 %back.4 = (bf16[1,128,384]{2,1,0:T(8,128)(2,1)}, bf16[1,128,384]{2,1,0:T(8,128)(2,1)}, bf16[1,128,384]{2,1,0:T(8,128)(2,1)}, bf16[1,128,384]{2,1,0:T(8,128)(2,1)...) custom-call(s32[1]{0:T(128)} %bitcast.14.refs_0_, bf16[3,384,512]{2,1,0:T(8,128)(2,1)} %get-tuple-element.130.refs_1_, ...), custom_call_target="tpu_custom_call" | custom-call | flops 5000000000 | bytes 20000000 | tf_op jit(solution)/shard_map/back/pallas_call | solution.py:457
  153.5 2.6 %collective-permute-start.21 = (bf16[1,128,384]{2,1,0:T(8,128)(2,1)S(1)}, bf16[1,128,384]{2,1,0:T(8,128)(2,1)S(1)}, u32[]{:S(2)}, u32[]{:S(2)}) collective-permute-start(bf16[1,128,384]{2,1,0:T(8,128)(2,1)S(1)} %copy-done.49), channel_id=1, source_target_pairs={{0,3},{1,2},{2,1},{3,0},{4,7},{5,6},{6,5},{7,4},{8,11},{9,10},{10,... | collective-permute-start | bytes 294920 | tf_op jit(solution)/shard_map/ppermute | solution.py:489
  159.7 2.6 %collective-permute-start.24 = (bf16[1,128,384]{2,1,0:T(8,128)(2,1)S(1)}, bf16[1,128,384]{2,1,0:T(8,128)(2,1)S(1)}, u32[]{:S(2)}, u32[]{:S(2)}) collective-permute-start(bf16[1,128,384]{2,1,0:T(8,128)(2,1)S(1)} %copy-done.52), channel_id=1, source_target_pairs={{0,3},{1,2},{2,1},{3,0},{4,7},{5,6},{6,5},{7,4},{8,11},{9,10},{10,... | collective-permute-start | bytes 294920 | tf_op jit(solution)/shard_map/ppermute | solution.py:489
  162.3 1.8 collective-permute-start.36
  164.2 2.5 %collective-permute-start.37 = (bf16[112,384]{1,0:T(8,128)(2,1)}, bf16[112,384]{1,0:T(8,128)(2,1)S(1)}, u32[]{:S(2)}, u32[]{:S(2)}) collective-permute-start(bf16[112,384]{1,0:T(8,128)(2,1)} %combine.8.refs_12_.refs_0_), channel_id=1, source_target_pairs={{0,3},{1,2},{2,1},{3,0},{4,7},{5,6},{6,5},{7,4},{8,11},{9,10},{10,... | collective-permute-start | bytes 258056 | tf_op jit(solution)/shard_map/ppermute | solution.py:489
  166.7 11.9 %back.5 = (bf16[1,128,384]{2,1,0:T(8,128)(2,1)}, bf16[1,128,384]{2,1,0:T(8,128)(2,1)}, bf16[1,128,384]{2,1,0:T(8,128)(2,1)}, bf16[1,128,384]{2,1,0:T(8,128)(2,1)...) custom-call(s32[1]{0:T(128)} %bitcast.14.refs_0_, bf16[3,384,512]{2,1,0:T(8,128)(2,1)} %get-tuple-element.130.refs_1_, ...), custom_call_target="tpu_custom_call" | custom-call | flops 5000000000 | bytes 20000000 | tf_op jit(solution)/shard_map/back/pallas_call | solution.py:457
  183.9 2.1 combine.9
  186.1 2.6 %collective-permute-start.29 = (bf16[448,128]{1,0:T(8,128)(2,1)}, bf16[448,128]{1,0:T(8,128)(2,1)S(1)}, u32[]{:S(2)}, u32[]{:S(2)}) collective-permute-start(bf16[448,128]{1,0:T(8,128)(2,1)} %get-tuple-element.173), channel_id=1, source_target_pairs={{0,8},{4,12},{8,0},{12,4},{16,24},{20,28},{24,16},{28,20},{1,9},{5... | collective-permute-start | bytes 344072 | tf_op jit(solution)/shard_map/ppermute | solution.py:489
  191.4 3.6 %collective-permute-done.29.refs_1_ = bf16[448,128]{1,0:T(8,128)(2,1)S(1)} collective-permute-done((bf16[448,128]{1,0:T(8,128)(2,1)}, bf16[448,128]{1,0:T(8,128)(2,1)S(1)}, u32[]{:S(2)}, u32[]{:S(2)}) %collective-permute-start.29) | collective-permute-done | bytes 114720 | tf_op jit(solution)/shard_map/ppermute | solution.py:489
  195.0 4.0 %collective-permute-done.30.refs_2_ = bf16[448,128]{1,0:T(8,128)(2,1)S(1)} collective-permute-done((bf16[448,128]{1,0:T(8,128)(2,1)}, bf16[448,128]{1,0:T(8,128)(2,1)S(1)}, u32[]{:S(2)}, u32[]{:S(2)}) %collective-permute-start.30) | collective-permute-done | bytes 114720 | tf_op jit(solution)/shard_map/ppermute | solution.py:489
  201.8 4.1 %collective-permute-start.34 = (bf16[448,128]{1,0:T(8,128)(2,1)}, bf16[448,128]{1,0:T(8,128)(2,1)S(1)}, u32[]{:S(2)}, u32[]{:S(2)}) collective-permute-start(bf16[448,128]{1,0:T(8,128)(2,1)} %combine.10.refs_0_), channel_id=1, source_target_pairs={{0,3},{1,2},{2,1},{3,0},{4,7},{5,6},{6,5},{7,4},{8,11},{9,10},{10,... | collective-permute-start | bytes 344072 | tf_op jit(solution)/shard_map/ppermute | solution.py:489
  205.9 3.3 %place.2 = bf16[4,3,128,384]{3,2,1,0:T(8,128)(2,1)} custom-call(s32[1]{0:T(128)} %bitcast.index_ref, bf16[3,128,384]{2,1,0:T(8,128)(2,1)} %get-tuple-element.126.refs_0_, bf16[3,128,384]{2,1,0:T(8,128)(2,1)} %copy-done.12, bf16[3,128,384]{2,1,0:T(8,128)(2,1)} %copy-done.8, bf16[3,128,384]{2,1,0:T(8,128)(2,1)} %copy-done.13, ...), custom_call_target="tpu_custom_call" | custom-call | flops 1500000000 | bytes 6000000 | tf_op jit(solution)/shard_map/place/pallas_call | solution.py:582
  209.2 4.4 %collective-permute-done.33.refs_2_ = bf16[448,128]{1,0:T(8,128)(2,1)S(1)} collective-permute-done((bf16[448,128]{1,0:T(8,128)(2,1)}, bf16[448,128]{1,0:T(8,128)(2,1)S(1)}, u32[]{:S(2)}, u32[]{:S(2)}) %collective-permute-start.33) | collective-permute-done | bytes 114720 | tf_op jit(solution)/shard_map/ppermute | solution.py:489
  216.7 12.3 %all_gather.6.block = bf16[3584,128]{1,0:T(8,128)(2,1)} all-gather(bf16[448,128]{1,0:T(8,128)(2,1)} %combine.11.refs_12_), channel_id=1, replica_groups=mesh['rows'=8,'seq'=4] {'rows'}, dimensions={0}, use_global_device_ids=true | all-gather | bytes 1032192 | tf_op jit(solution)/shard_map/all_gather | solution.py:785
  229.0 2.4 unpack_early.1
  232.2 3.2 %place.3 = f32[4,3,128,384]{3,2,1,0:T(8,128)} custom-call(s32[1]{0:T(128)} %bitcast.index_ref, bf16[1,128,384]{2,1,0:T(8,128)(2,1)} %get-tuple-element.162.refs_0_, bf16[1,128,384]{2,1,0:T(8,128)(2,1)} %copy-done.14, bf16[1,128,384]{2,1,0:T(8,128)(2,1)} %copy-done.15, bf16[1,128,384]{2,1,0:T(8,128)(2,1)} %copy-done.16, ...), custom_call_target="tpu_custom_call" | custom-call | flops 1500000000 | bytes 6000000 | tf_op jit(solution)/shard_map/place/pallas_call | solution.py:582
  235.4 4.4 %unpack_later.1 = (f32[1536,384]{1,0:T(8,128)}, f32[384,1536]{1,0:T(8,128)}, f32[384,384]{1,0:T(8,128)}, f32[384]{0:T(512)}, f32[384]{0:T(512)}, /*index=5*/f32[...) custom-call(bf16[3584,384]{1,0:T(8,128)(2,1)} %all-gather.2.cloned.1.call-done.block), custom_call_target="tpu_custom_call" | custom-call | flops 2000000000 | bytes 8000000 | tf_op jit(solution)/shard_map/unpack_later/pallas_call | solution.py:643
  (216 shorter events, 39.8 us)
Async XLA Ops:
  7.2 228.2 %all-gather.2.cloned.1.call-start = ((), (), s32[]{:S(2)}) async-start(), calls=%async_computation | async-start | bytes 3096576 | tf_op jit(solution)/shard_map/all_gather | solution.py:778
  9.9 20.5 %collective-permute-start.3 = (bf16[1,128,384]{2,1,0:T(8,128)(2,1)S(1)}, bf16[1,128,384]{2,1,0:T(8,128)(2,1)}, u32[]{:S(2)}, u32[]{:S(2)}) collective-permute-start(bf16[1,128,384]{2,1,0:T(8,128)(2,1)S(1)} %get-tuple-element.201), channel_id=1, source_target_pairs={{0,1},{1,0},{2,3},{3,2},{4,5},{5,4},{6,7},{7,6},{8,9},{9,8},{10,11... | collective-permute-start | bytes 294920 | tf_op jit(solution)/shard_map/ppermute | solution.py:489
  12.9 17.4 %collective-permute-start.4 = (bf16[1,128,384]{2,1,0:T(8,128)(2,1)S(1)}, bf16[1,128,384]{2,1,0:T(8,128)(2,1)}, u32[]{:S(2)}, u32[]{:S(2)}) collective-permute-start(bf16[1,128,384]{2,1,0:T(8,128)(2,1)S(1)} %get-tuple-element.200), channel_id=1, source_target_pairs={{0,2},{1,3},{2,0},{3,1},{4,6},{5,7},{6,4},{7,5},{8,10},{9,11},{10,... | collective-permute-start | bytes 294920 | tf_op jit(solution)/shard_map/ppermute | solution.py:489
  15.5 16.3 %collective-permute-start.5 = (bf16[1,128,384]{2,1,0:T(8,128)(2,1)S(1)}, bf16[1,128,384]{2,1,0:T(8,128)(2,1)}, u32[]{:S(2)}, u32[]{:S(2)}) collective-permute-start(bf16[1,128,384]{2,1,0:T(8,128)(2,1)S(1)} %get-tuple-element.199), channel_id=1, source_target_pairs={{0,3},{1,2},{2,1},{3,0},{4,7},{5,6},{6,5},{7,4},{8,11},{9,10},{10,... | collective-permute-start | bytes 294920 | tf_op jit(solution)/shard_map/ppermute | solution.py:489
  17.4 32.3 %collective-permute-start = (bf16[2,128,384]{2,1,0:T(8,128)(2,1)S(1)}, bf16[2,128,384]{2,1,0:T(8,128)(2,1)S(1)}, u32[]{:S(2)}, u32[]{:S(2)}) collective-permute-start(bf16[2,128,384]{2,1,0:T(8,128)(2,1)S(1)} %get-tuple-element.197), channel_id=1, source_target_pairs={{0,1},{1,0},{2,3},{3,2},{4,5},{5,4},{6,7},{7,6},{8,9},{9,8},{10,11... | collective-permute-start | bytes 589832 | tf_op jit(solution)/shard_map/ppermute | solution.py:489
  18.3 32.6 %collective-permute-start.1 = (bf16[2,128,384]{2,1,0:T(8,128)(2,1)S(1)}, bf16[2,128,384]{2,1,0:T(8,128)(2,1)}, u32[]{:S(2)}, u32[]{:S(2)}) collective-permute-start(bf16[2,128,384]{2,1,0:T(8,128)(2,1)S(1)} %get-tuple-element.196), channel_id=1, source_target_pairs={{0,2},{1,3},{2,0},{3,1},{4,6},{5,7},{6,4},{7,5},{8,10},{9,11},{10,... | collective-permute-start | bytes 589832 | tf_op jit(solution)/shard_map/ppermute | solution.py:489
  30.3 20.6 %collective-permute-start.2 = (bf16[2,128,384]{2,1,0:T(8,128)(2,1)S(1)}, bf16[2,128,384]{2,1,0:T(8,128)(2,1)S(1)}, u32[]{:S(2)}, u32[]{:S(2)}) collective-permute-start(bf16[2,128,384]{2,1,0:T(8,128)(2,1)S(1)} %get-tuple-element.195), channel_id=1, source_target_pairs={{0,3},{1,2},{2,1},{3,0},{4,7},{5,6},{6,5},{7,4},{8,11},{9,10},{10,... | collective-permute-start | bytes 589832 | tf_op jit(solution)/shard_map/ppermute | solution.py:489
  30.3 47.7 %collective-permute-start.10 = (bf16[3,128,384]{2,1,0:T(8,128)(2,1)S(1)}, bf16[3,128,384]{2,1,0:T(8,128)(2,1)S(1)}, u32[]{:S(2)}, u32[]{:S(2)}) collective-permute-start(bf16[3,128,384]{2,1,0:T(8,128)(2,1)S(1)} %get-tuple-element.192), channel_id=1, source_target_pairs={{0,2},{1,3},{2,0},{3,1},{4,6},{5,7},{6,4},{7,5},{8,10},{9,11},{10,... | collective-permute-start | bytes 884744 | tf_op jit(solution)/shard_map/ppermute | solution.py:489
  31.8 46.2 %collective-permute-start.11 = (bf16[3,128,384]{2,1,0:T(8,128)(2,1)S(1)}, bf16[3,128,384]{2,1,0:T(8,128)(2,1)S(1)}, u32[]{:S(2)}, u32[]{:S(2)}) collective-permute-start(bf16[3,128,384]{2,1,0:T(8,128)(2,1)S(1)} %get-tuple-element.191), channel_id=1, source_target_pairs={{0,3},{1,2},{2,1},{3,0},{4,7},{5,6},{6,5},{7,4},{8,11},{9,10},{10,... | collective-permute-start | bytes 884744 | tf_op jit(solution)/shard_map/ppermute | solution.py:489
  49.7 28.4 %collective-permute-start.9 = (bf16[3,128,384]{2,1,0:T(8,128)(2,1)S(1)}, bf16[3,128,384]{2,1,0:T(8,128)(2,1)S(1)}, u32[]{:S(2)}, u32[]{:S(2)}) collective-permute-start(bf16[3,128,384]{2,1,0:T(8,128)(2,1)S(1)} %get-tuple-element.193), channel_id=1, source_target_pairs={{0,1},{1,0},{2,3},{3,2},{4,5},{5,4},{6,7},{7,6},{8,9},{9,8},{10,11... | collective-permute-start | bytes 884744 | tf_op jit(solution)/shard_map/ppermute | solution.py:489
  99.1 20.2 %collective-permute-start.7 = (bf16[3,128,384]{2,1,0:T(8,128)(2,1)}, bf16[3,128,384]{2,1,0:T(8,128)(2,1)S(1)}, u32[]{:S(2)}, u32[]{:S(2)}) collective-permute-start(bf16[3,128,384]{2,1,0:T(8,128)(2,1)} %get-tuple-element.128), channel_id=1, source_target_pairs={{0,2},{1,3},{2,0},{3,1},{4,6},{5,7},{6,4},{7,5},{8,10},{9,11},{10,... | collective-permute-start | bytes 884744 | tf_op jit(solution)/shard_map/ppermute | solution.py:489
  105.1 31.9 %collective-permute-start.6 = (bf16[3,128,384]{2,1,0:T(8,128)(2,1)}, bf16[3,128,384]{2,1,0:T(8,128)(2,1)S(1)}, u32[]{:S(2)}, u32[]{:S(2)}) collective-permute-start(bf16[3,128,384]{2,1,0:T(8,128)(2,1)} %get-tuple-element.127), channel_id=1, source_target_pairs={{0,1},{1,0},{2,3},{3,2},{4,5},{5,4},{6,7},{7,6},{8,9},{9,8},{10,11... | collective-permute-start | bytes 884744 | tf_op jit(solution)/shard_map/ppermute | solution.py:489
  105.2 34.7 %collective-permute-start.8 = (bf16[3,128,384]{2,1,0:T(8,128)(2,1)}, bf16[3,128,384]{2,1,0:T(8,128)(2,1)S(1)}, u32[]{:S(2)}, u32[]{:S(2)}) collective-permute-start(bf16[3,128,384]{2,1,0:T(8,128)(2,1)} %get-tuple-element.129), channel_id=1, source_target_pairs={{0,3},{1,2},{2,1},{3,0},{4,7},{5,6},{6,5},{7,4},{8,11},{9,10},{10,... | collective-permute-start | bytes 884744 | tf_op jit(solution)/shard_map/ppermute | solution.py:489
  111.8 19.9 %collective-permute-start.13 = (bf16[448,384]{1,0:T(8,128)(2,1)}, bf16[448,384]{1,0:T(8,128)(2,1)S(1)}, u32[]{:S(2)}, u32[]{:S(2)}) collective-permute-start(bf16[448,384]{1,0:T(8,128)(2,1)} %get-tuple-element.147.refs_11_), channel_id=1, source_target_pairs={{0,8},{4,12},{8,0},{12,4},{16,24},{20,28},{24,16},{28,20},{1,9},{5... | collective-permute-start | bytes 1032200 | tf_op jit(solution)/shard_map/ppermute | solution.py:489
  111.8 20.0 %collective-permute-start.14 = (bf16[448,384]{1,0:T(8,128)(2,1)}, bf16[448,384]{1,0:T(8,128)(2,1)S(1)}, u32[]{:S(2)}, u32[]{:S(2)}) collective-permute-start(bf16[448,384]{1,0:T(8,128)(2,1)} %get-tuple-element.148.refs_12_), channel_id=1, source_target_pairs={{0,16},{4,20},{8,24},{12,28},{16,0},{20,4},{24,8},{28,12},{1,17},{... | collective-permute-start | bytes 1032200 | tf_op jit(solution)/shard_map/ppermute | solution.py:489
  119.3 14.4 %collective-permute-start.15 = (bf16[448,384]{1,0:T(8,128)(2,1)}, bf16[448,384]{1,0:T(8,128)(2,1)S(1)}, u32[]{:S(2)}, u32[]{:S(2)}) collective-permute-start(bf16[448,384]{1,0:T(8,128)(2,1)} %get-tuple-element.149.refs_13_), channel_id=1, source_target_pairs={{0,24},{4,28},{8,16},{12,20},{16,8},{20,12},{24,0},{28,4},{1,25},{... | collective-permute-start | bytes 1032200 | tf_op jit(solution)/shard_map/ppermute | solution.py:489
  131.8 27.9 %collective-permute-start.19 = (bf16[1,128,384]{2,1,0:T(8,128)(2,1)}, bf16[1,128,384]{2,1,0:T(8,128)(2,1)S(1)}, u32[]{:S(2)}, u32[]{:S(2)}) collective-permute-start(bf16[1,128,384]{2,1,0:T(8,128)(2,1)} %get-tuple-element.158), channel_id=1, source_target_pairs={{0,1},{1,0},{2,3},{3,2},{4,5},{5,4},{6,7},{7,6},{8,9},{9,8},{10,11... | collective-permute-start | bytes 294920 | tf_op jit(solution)/shard_map/ppermute | solution.py:489
  131.9 30.5 %collective-permute-start.20 = (bf16[1,128,384]{2,1,0:T(8,128)(2,1)}, bf16[1,128,384]{2,1,0:T(8,128)(2,1)S(1)}, u32[]{:S(2)}, u32[]{:S(2)}) collective-permute-start(bf16[1,128,384]{2,1,0:T(8,128)(2,1)} %get-tuple-element.159), channel_id=1, source_target_pairs={{0,2},{1,3},{2,0},{3,1},{4,6},{5,7},{6,4},{7,5},{8,10},{9,11},{10,... | collective-permute-start | bytes 294920 | tf_op jit(solution)/shard_map/ppermute | solution.py:489
  136.7 16.8 %collective-permute-start.16 = (bf16[112,384]{1,0:T(8,128)(2,1)}, bf16[112,384]{1,0:T(8,128)(2,1)S(1)}, u32[]{:S(2)}, u32[]{:S(2)}) collective-permute-start(bf16[112,384]{1,0:T(8,128)(2,1)} %get-tuple-element.153.refs_13_), channel_id=1, source_target_pairs={{0,1},{1,0},{2,3},{3,2},{4,5},{5,4},{6,7},{7,6},{8,9},{9,8},{10,11... | collective-permute-start | bytes 258056 | tf_op jit(solution)/shard_map/ppermute | solution.py:489
  137.0 19.1 %collective-permute-start.17 = (bf16[112,384]{1,0:T(8,128)(2,1)}, bf16[112,384]{1,0:T(8,128)(2,1)S(1)}, u32[]{:S(2)}, u32[]{:S(2)}) collective-permute-start(bf16[112,384]{1,0:T(8,128)(2,1)} %get-tuple-element.154.refs_14_), channel_id=1, source_target_pairs={{0,2},{1,3},{2,0},{3,1},{4,6},{5,7},{6,4},{7,5},{8,10},{9,11},{10,... | collective-permute-start | bytes 258056 | tf_op jit(solution)/shard_map/ppermute | solution.py:489
  139.9 16.3 %collective-permute-start.18 = (bf16[112,384]{1,0:T(8,128)(2,1)}, bf16[112,384]{1,0:T(8,128)(2,1)S(1)}, u32[]{:S(2)}, u32[]{:S(2)}) collective-permute-start(bf16[112,384]{1,0:T(8,128)(2,1)} %get-tuple-element.155.refs_15_), channel_id=1, source_target_pairs={{0,3},{1,2},{2,1},{3,0},{4,7},{5,6},{6,5},{7,4},{8,11},{9,10},{10,... | collective-permute-start | bytes 258056 | tf_op jit(solution)/shard_map/ppermute | solution.py:489
  156.2 22.5 %collective-permute-start.23 = (bf16[1,128,384]{2,1,0:T(8,128)(2,1)}, bf16[1,128,384]{2,1,0:T(8,128)(2,1)S(1)}, u32[]{:S(2)}, u32[]{:S(2)}) collective-permute-start(bf16[1,128,384]{2,1,0:T(8,128)(2,1)} %get-tuple-element.165), channel_id=1, source_target_pairs={{0,2},{1,3},{2,0},{3,1},{4,6},{5,7},{6,4},{7,5},{8,10},{9,11},{10,... | collective-permute-start | bytes 294920 | tf_op jit(solution)/shard_map/ppermute | solution.py:489
  159.7 19.0 %collective-permute-start.24 = (bf16[1,128,384]{2,1,0:T(8,128)(2,1)S(1)}, bf16[1,128,384]{2,1,0:T(8,128)(2,1)S(1)}, u32[]{:S(2)}, u32[]{:S(2)}) collective-permute-start(bf16[1,128,384]{2,1,0:T(8,128)(2,1)S(1)} %copy-done.52), channel_id=1, source_target_pairs={{0,3},{1,2},{2,1},{3,0},{4,7},{5,6},{6,5},{7,4},{8,11},{9,10},{10,... | collective-permute-start | bytes 294920 | tf_op jit(solution)/shard_map/ppermute | solution.py:489
  162.3 16.4 %collective-permute-start.35 = (bf16[112,384]{1,0:T(8,128)(2,1)}, bf16[112,384]{1,0:T(8,128)(2,1)S(1)}, u32[]{:S(2)}, u32[]{:S(2)}) collective-permute-start(bf16[112,384]{1,0:T(8,128)(2,1)} %combine.8.refs_12_.refs_0_), channel_id=1, source_target_pairs={{0,1},{1,0},{2,3},{3,2},{4,5},{5,4},{6,7},{7,6},{8,9},{9,8},{10,11... | collective-permute-start | bytes 258056 | tf_op jit(solution)/shard_map/ppermute | solution.py:489
  162.3 16.4 %collective-permute-start.36 = (bf16[112,384]{1,0:T(8,128)(2,1)}, bf16[112,384]{1,0:T(8,128)(2,1)S(1)}, u32[]{:S(2)}, u32[]{:S(2)}) collective-permute-start(bf16[112,384]{1,0:T(8,128)(2,1)} %combine.8.refs_12_.refs_0_), channel_id=1, source_target_pairs={{0,2},{1,3},{2,0},{3,1},{4,6},{5,7},{6,4},{7,5},{8,10},{9,11},{10,... | collective-permute-start | bytes 258056 | tf_op jit(solution)/shard_map/ppermute | solution.py:489
  164.2 14.6 %collective-permute-start.37 = (bf16[112,384]{1,0:T(8,128)(2,1)}, bf16[112,384]{1,0:T(8,128)(2,1)S(1)}, u32[]{:S(2)}, u32[]{:S(2)}) collective-permute-start(bf16[112,384]{1,0:T(8,128)(2,1)} %combine.8.refs_12_.refs_0_), channel_id=1, source_target_pairs={{0,3},{1,2},{2,1},{3,0},{4,7},{5,6},{6,5},{7,4},{8,11},{9,10},{10,... | collective-permute-start | bytes 258056 | tf_op jit(solution)/shard_map/ppermute | solution.py:489
  188.6 10.4 %collective-permute-start.30 = (bf16[448,128]{1,0:T(8,128)(2,1)}, bf16[448,128]{1,0:T(8,128)(2,1)S(1)}, u32[]{:S(2)}, u32[]{:S(2)}) collective-permute-start(bf16[448,128]{1,0:T(8,128)(2,1)} %get-tuple-element.174), channel_id=1, source_target_pairs={{0,16},{4,20},{8,24},{12,28},{16,0},{20,4},{24,8},{28,12},{1,17},{... | collective-permute-start | bytes 344072 | tf_op jit(solution)/shard_map/ppermute | solution.py:489
  190.1 41.4 %collective-permute-start.25 = (bf16[1,128,384]{2,1,0:T(8,128)(2,1)S(1)}, bf16[1,128,384]{2,1,0:T(8,128)(2,1)S(1)}, u32[]{:S(2)}, u32[]{:S(2)}) collective-permute-start(bf16[1,128,384]{2,1,0:T(8,128)(2,1)S(1)} %copy-done.48), channel_id=1, source_target_pairs={{0,1},{1,0},{2,3},{3,2},{4,5},{5,4},{6,7},{7,6},{8,9},{9,8},{10,11... | collective-permute-start | bytes 294920 | tf_op jit(solution)/shard_map/ppermute | solution.py:489
  190.1 41.4 %collective-permute-start.26 = (bf16[1,128,384]{2,1,0:T(8,128)(2,1)S(1)}, bf16[1,128,384]{2,1,0:T(8,128)(2,1)S(1)}, u32[]{:S(2)}, u32[]{:S(2)}) collective-permute-start(bf16[1,128,384]{2,1,0:T(8,128)(2,1)S(1)} %copy-done.47), channel_id=1, source_target_pairs={{0,2},{1,3},{2,0},{3,1},{4,6},{5,7},{6,4},{7,5},{8,10},{9,11},{10,... | collective-permute-start | bytes 294920 | tf_op jit(solution)/shard_map/ppermute | solution.py:489
  201.5 12.2 %collective-permute-start.33 = (bf16[448,128]{1,0:T(8,128)(2,1)}, bf16[448,128]{1,0:T(8,128)(2,1)S(1)}, u32[]{:S(2)}, u32[]{:S(2)}) collective-permute-start(bf16[448,128]{1,0:T(8,128)(2,1)} %combine.10.refs_0_), channel_id=1, source_target_pairs={{0,2},{1,3},{2,0},{3,1},{4,6},{5,7},{6,4},{7,5},{8,10},{9,11},{10,... | collective-permute-start | bytes 344072 | tf_op jit(solution)/shard_map/ppermute | solution.py:489
  201.8 11.9 %collective-permute-start.34 = (bf16[448,128]{1,0:T(8,128)(2,1)}, bf16[448,128]{1,0:T(8,128)(2,1)S(1)}, u32[]{:S(2)}, u32[]{:S(2)}) collective-permute-start(bf16[448,128]{1,0:T(8,128)(2,1)} %combine.10.refs_0_), channel_id=1, source_target_pairs={{0,3},{1,2},{2,1},{3,0},{4,7},{5,6},{6,5},{7,4},{8,11},{9,10},{10,... | collective-permute-start | bytes 344072 | tf_op jit(solution)/shard_map/ppermute | solution.py:489
  209.1 22.4 %collective-permute-start.27 = (bf16[1,128,384]{2,1,0:T(8,128)(2,1)S(1)}, bf16[1,128,384]{2,1,0:T(8,128)(2,1)S(1)}, u32[]{:S(2)}, u32[]{:S(2)}) collective-permute-start(bf16[1,128,384]{2,1,0:T(8,128)(2,1)S(1)} %copy-done.46), channel_id=1, source_target_pairs={{0,3},{1,2},{2,1},{3,0},{4,7},{5,6},{6,5},{7,4},{8,11},{9,10},{10,... | collective-permute-start | bytes 294920 | tf_op jit(solution)/shard_map/ppermute | solution.py:489
  (64 other events, 313.9 us)
Sparse Core Ops, SparseCore 0:
  181.4 31.8 all-gather.1

commit v3 on v1

v3 whole, which is shorter than its diff:
```python
import functools
import math

import jax
import jax.numpy as jnp
from jax import lax
from jax.experimental import pallas as pl
from jax.experimental.pallas import tpu as pltpu
from jax.sharding import PartitionSpec as P

HEADS = 12
HD = 32
GROUPS = 3
PER_GROUP = HEADS // GROUPS
AUG = 16
BIG = 2.0**100
SMALL_SCORE = 60.0
EPSILON = 1e-05
SCALE = HD ** (-0.5)
LOG2E = math.log2(math.e)
Q_FACTOR = SCALE * LOG2E
LN2 = math.log(2.0)
VMEM_LIMIT = 60 * 2**20

f32 = jnp.float32
bf16 = jnp.bfloat16
NN = (((1,), (0,)), ((), ()))
NT = (((1,), (1,)), ((), ()))
TN = (((0,), (0,)), ((), ()))


def dot(left, right, dims=NN):
    return lax.dot_general(left, right, dims, preferred_element_type=f32)


def fold_lanes(values):
    total = values[:, :128]
    for start in range(128, values.shape[1], 128):
        total = total + values[:, start : start + 128]
    return total


def row_sum(partial):
    return jnp.sum(partial.T, axis=0, keepdims=True)


def normalize(hidden):
    scale = 1.0 / hidden.shape[0]
    centre = hidden - jnp.sum(hidden, axis=0, keepdims=True) * scale
    variance = jnp.sum(centre * centre, axis=0, keepdims=True) * scale
    inverse = lax.rsqrt(variance + EPSILON)
    return centre * inverse, inverse


def normalize_back(upstream, scaled, inverse):
    scale = 1.0 / upstream.shape[0]
    mean = jnp.sum(upstream, axis=0, keepdims=True) * scale
    spread = jnp.sum(upstream * scaled, axis=0, keepdims=True) * scale
    return inverse * (upstream - mean - scaled * spread)


def gelu_parts(v):
    cdf = 0.5 + 0.5 * lax.erf(v * 0.5**0.5)
    bell = jnp.exp2((v * v) * (-0.5 * LOG2E))
    return v * cdf, cdf + v * bell * (2.0 * math.pi) ** (-0.5)


def prepare_kernel(wq, wk, wv, wo, wup, wdn, rows, wq_t, wk_t, wv_t, wo_t, wup_t, wdn_t, columns):
    for source, target in ((wq, wq_t), (wk, wk_t), (wv, wv_t), (wo, wo_t), (wup, wup_t), (wdn, wdn_t)):
        target[...] = source[...].T
    width = rows.shape[1]
    columns[...] = jnp.concatenate([rows[...], jnp.zeros((128 - rows.shape[0], width), f32)], axis=0).T


def prepare(weights, rows):
    shapes = [jax.ShapeDtypeStruct(w.shape[::-1], w.dtype) for w in weights]
    shapes.append(jax.ShapeDtypeStruct((rows.shape[1], 128), f32))
    return pl.pallas_call(
        prepare_kernel,
        out_shape=shapes,
        compiler_params=pltpu.CompilerParams(vmem_limit_bytes=VMEM_LIMIT),
        cost_estimate=cost(5),
        name="prepare",
    )(*weights, rows)


def cost(micros):
    return pl.CostEstimate(flops=int(micros * 1e5), transcendentals=0, bytes_accessed=int(micros * 1e3))


B_QUERY, B_VALUE, B_OUT, GAIN1, SHIFT1, B_DOWN, GAIN2, SHIFT2, B_UP = range(9)


ANY = pl.BlockSpec(memory_space=pl.ANY)


def head_sums(values):
    return jnp.sum(values.reshape(HEADS, HD, values.shape[1]), axis=1)


def pick_kernel(index_ref, *refs, count):
    for shift in range(count):
        out = refs[len(refs) - count + shift]
        out[0] = refs[shift][0]
        out[1] = refs[count + shift][0]


def pick(tokens, cotangent, count, rows, row, index, after):
    _, span, width = tokens.shape
    specs = [
        pl.BlockSpec((1, span, width), lambda i, place, shift=shift: ((place[0] ^ shift) * rows + row, 0, 0))
        for shift in range(count)
    ]
    return pl.pallas_call(
        functools.partial(pick_kernel, count=count),
        grid_spec=pltpu.PrefetchScalarGridSpec(
            num_scalar_prefetch=1,
            grid=(1,),
            in_specs=specs * 2 + [ANY] * len(after),
            out_specs=[pl.BlockSpec((2, span, width), lambda i, place: (0, 0, 0))] * count,
        ),
        out_shape=[jax.ShapeDtypeStruct((2, span, width), bf16)] * count,
        compiler_params=pltpu.CompilerParams(vmem_limit_bytes=VMEM_LIMIT),
        cost_estimate=cost(1),
        name="pick",
    )(index, *[tokens] * count, *[cotangent] * count, *after)


def emit(packed, index, outs, inner):
    size = outs[0].shape[0] // inner
    for shift, ref in enumerate(outs):
        for block in range(inner):
            start = pl.multiple_of((block * len(outs) + (index ^ shift)) * size, 16)
            ref[block * size : (block + 1) * size] = packed[pl.ds(start, size), :]


class Taker:
    def __init__(self, refs):
        self.refs = list(refs)

    def __call__(self, number):
        taken = self.refs[:number]
        del self.refs[:number]
        return taken


def column_of(cols, index):
    return cols[:, index : index + 1]


def project_row(piece_refs, cols, wq, wk, wv, saved, small_ref):
    xt = jnp.concatenate([ref[0].T for ref in piece_refs], axis=1)
    query = (dot(wq[...], xt) + column_of(cols, B_QUERY)) * Q_FACTOR
    key = dot(wk[...], xt)
    saved[0] = query.astype(bf16)
    saved[1] = key.astype(bf16)
    saved[2] = (dot(wv[...], xt) + column_of(cols, B_VALUE)).astype(bf16)
    saved[3] = xt
    bounds = [
        jnp.max(head_sums(query * query), axis=1, keepdims=True),
        jnp.max(head_sums(key * key), axis=1, keepdims=True),
    ]
    small_ref[0] = (jnp.max(bounds[0] * bounds[1]) < SMALL_SCORE**2).astype(jnp.int32)


def head_rows(group, h):
    return pl.ds(pl.multiple_of((group * PER_GROUP + h) * HD, HD), HD)


def attend_heads(group, saved, aug_ref, probs, att_ref, stat_ref, small_ref):
    length = saved.shape[2]
    ones = jnp.ones((AUG, length), bf16)

    def score(h):
        keys = jnp.concatenate([saved[1, head_rows(group, h), :], aug_ref[0, AUG:]], axis=0)
        query = jnp.concatenate([saved[0, head_rows(group, h), :], aug_ref[0, :AUG]], axis=0)
        return dot(keys, query, TN)

    def mix(h):
        values = jnp.concatenate([saved[2, head_rows(group, h), :], ones], axis=0)
        mixed = dot(values, probs(h)[...])
        inverse = 1.0 / mixed[HD : HD + 1]
        att_ref[head_rows(group, h), :] = mixed[:HD] * inverse
        stat_ref[pl.ds(group * PER_GROUP + h, 1), :] = inverse

    def heads(shifted):
        scores = score(0)
        for h in range(PER_GROUP):
            following = score(h + 1) if h + 1 < PER_GROUP else None
            if h >= 1:
                mix(h - 1)
            if shifted:
                scores = scores - jnp.max(scores, axis=0, keepdims=True)
            probs(h)[...] = jnp.exp2(scores).astype(bf16)
            scores = following
        mix(PER_GROUP - 1)

    @pl.when(small_ref[0] == 1)
    def _():
        heads(False)

    @pl.when(small_ref[0] == 0)
    def _():
        heads(True)


def dense_row(piece_refs, cols, saved, att_ref, stat_ref, weights, sums, carried, write_out, summed, og_ref, delta_ref, gres_ref):
    wo_t, wo, wup_t, wup, wdn_t, wdn = weights
    acc_dn, acc_up, acc_out = sums
    ff = acc_dn.shape[0]
    width = att_ref.shape[0]

    def column(index):
        return column_of(cols, index)

    def add(number, value):
        ref = sums[number]
        ref[...] = ref[...] + value if carried else value
        summed(number)

    att = att_ref[...]
    att_b = att.astype(bf16)
    res1 = saved[3].astype(f32) + dot(wo_t[...], att_b) + column(B_OUT)
    scaled1, inverse1 = normalize(res1)
    normed = scaled1 * column(GAIN1) + column(SHIFT1)
    normed_b = normed.astype(bf16)
    b_up = jnp.concatenate([column(B_UP + i) for i in range(ff // width)], axis=0)
    act, slope = gelu_parts(dot(wup_t[...], normed_b) + b_up)
    act_b = act.astype(bf16)
    res2 = normed + dot(wdn_t[...], act_b) + column(B_DOWN)
    scaled2, inverse2 = normalize(res2)
    write_out((scaled2 * column(GAIN2) + column(SHIFT2)).astype(bf16))
    cot = jnp.concatenate([ref[1].T for ref in piece_refs], axis=1).astype(f32)
    gres2 = normalize_back(cot * column(GAIN2), scaled2, inverse2)
    down_b = gres2.astype(bf16)
    up_b = (dot(wdn[...], down_b) * slope).astype(bf16)
    add(0, dot(act_b, down_b, NT))
    gnormed = gres2 + dot(wup[...], up_b)
    add(1, dot(normed_b, up_b, NT))
    gres1 = normalize_back(gnormed * column(GAIN1), scaled1, inverse1)
    gres_ref[...] = gres1
    branch_b = gres1.astype(bf16)
    og = dot(wo[...], branch_b)
    add(2, dot(att_b, branch_b, NT))
    for h in range(HEADS):
        part = slice(h * HD, (h + 1) * HD)
        scaled_og = (og[part] * stat_ref[h : h + 1, :]).astype(bf16)
        og_ref[part, :] = scaled_og
        delta_ref[h : h + 1, :] = jnp.sum(scaled_og.astype(f32) * att[part], axis=0, keepdims=True)
    biases = [cot * scaled2, cot, down_b.astype(f32), gnormed * scaled1, gnormed, branch_b.astype(f32)]
    bias_rows = [row_sum(fold_lanes(value)) for value in biases]
    up_sum = fold_lanes(up_b.astype(f32))
    bias_rows += [row_sum(up_sum[i * width : (i + 1) * width]) for i in range(ff // width)]
    bias_rows.append(jnp.zeros((16 - len(bias_rows), width), f32))
    return jnp.concatenate(bias_rows, axis=0)


def back_heads(group, saved, og_ref, delta_ref, probs, grads, held):
    length = og_ref.shape[1]
    width = og_ref.shape[0]
    sign = jnp.where(lax.broadcasted_iota(jnp.int32, (AUG, length), 0) < 3, 1.0, 0.0).astype(bf16)

    def grad_probs(h):
        delta = delta_ref[pl.ds(group * PER_GROUP + h, 1), :]
        first = delta.astype(bf16)
        rest = delta - first.astype(f32)
        second = rest.astype(bf16)
        third = (rest - second.astype(f32)).astype(bf16)
        aug = jnp.concatenate(
            [-first.astype(f32), -second.astype(f32), -third.astype(f32), jnp.zeros((AUG - 3, length), f32)], axis=0
        ).astype(bf16)
        left = jnp.concatenate([saved[2, head_rows(group, h), :], sign], axis=0)
        right = jnp.concatenate([og_ref[head_rows(group, h), :], aug], axis=0)
        return dot(left, right, TN)

    def target(which, h):
        return pl.ds(pl.multiple_of(which * width + (group * PER_GROUP + h) * HD, HD), HD)

    for h in range(PER_GROUP):
        held[h] = (probs(h)[...].astype(f32) * grad_probs(h)).astype(bf16)
        grads[target(2, h), :] = dot(og_ref[head_rows(group, h), :], probs(h)[...], NT).astype(bf16)
    for h in range(PER_GROUP):
        grads[target(0, h), :] = (dot(saved[1, head_rows(group, h), :], held[h]) * SCALE).astype(bf16)
        grads[target(1, h), :] = (dot(saved[0, head_rows(group, h), :], held[h], NT) * LN2).astype(bf16)


def back_biases(total, width):
    rows = [row_sum(fold_lanes(part.astype(f32))) for part in (total[:width], total[2 * width :])]
    return jnp.concatenate(rows + [jnp.zeros((6, width), f32)], axis=0)


def write_pieces(values, ref, here, at=0):
    span = ref.shape[2]
    for shift in range(ref.shape[0]):
        ref[here ^ shift, at] = values[:, shift * span : (shift + 1) * span].T


def copies_of(sources, targets, sem):
    return [pltpu.make_async_copy(a, b, sem.at[i]) for i, (a, b) in enumerate(zip(sources, targets))]


def whole_kernel(here_ref, *refs, pieces, carried, after):
    take = Taker(refs)
    piece_refs = take(pieces)
    aug_ref, cols, wq, wk, wv = take(5)
    weights_hbm = take(7)
    sums_hbm = take(4 if carried else 0)
    bias_in = take(2 if carried else 0)
    take(1 if carried else 0)
    take(after)
    (out_ref,) = take(1)
    sums_out = take(4)
    bias_out = take(2)
    saved, p_all, att_ref, stat_ref, og_ref, delta_ref, gres_ref, grads, held = take(9)
    weights = take(7)
    sums = take(4)
    small_ref, weight_sem, sum_sem, out_sem = take(4)
    step = pl.program_id(0)
    width = att_ref.shape[0]
    weight_copies = copies_of(weights_hbm, weights, weight_sem)
    sum_copies = copies_of(sums_hbm, sums, sum_sem)
    out_copies = copies_of(sums, sums_out, out_sem)

    @pl.when(step == 0)
    def _():
        for copy in weight_copies + sum_copies:
            copy.start()
        project_row(piece_refs, cols, wq, wk, wv, saved, small_ref)

    @pl.when(step < GROUPS)
    def _():
        attend_heads(step, saved, aug_ref, lambda h: p_all.at[step * PER_GROUP + h], att_ref, stat_ref, small_ref)

    @pl.when(step == GROUPS - 1)
    def _():
        for copy in weight_copies[:6] + sum_copies[:3]:
            copy.wait()
        total = dense_row(
            piece_refs, cols, saved, att_ref, stat_ref, weights[:6], sums[:3], carried,
            lambda values: write_pieces(values, out_ref, here_ref[0], 0), lambda number: out_copies[number].start(),
            og_ref, delta_ref, gres_ref,
        )
        bias_out[0][...] = total + bias_in[0][...] if carried else total

    @pl.when(step >= GROUPS)
    def _():
        group = step - GROUPS
        back_heads(group, saved, og_ref, delta_ref, lambda h: p_all.at[group * PER_GROUP + h], grads, held)

    @pl.when(step == 2 * GROUPS - 1)
    def _():
        for copy in weight_copies[6:] + sum_copies[3:]:
            copy.wait()
        total = grads[...]
        acc = dot(saved[3], total, NT)
        sums[3][...] = sums[3][...] + acc if carried else acc
        out_copies[3].start()
        bias = back_biases(total, width)
        bias_out[1][...] = bias + bias_in[1][...] if carried else bias
        result = (gres_ref[...] + dot(weights[6][...], total)).astype(bf16)
        write_pieces(result, out_ref, here_ref[0], 1)
        for copy in out_copies:
            copy.wait()


def whole(here, pieces, row, height, aug, cols, wqkv, weights, carried, after):
    _, span, width = pieces[0].shape
    count = len(pieces)
    length = span * count
    ff = weights[3].shape[1]
    full = lambda shape: pl.BlockSpec(shape, lambda g, i: (0,) * len(shape))
    sum_shapes = [(ff, width), (width, ff), (width, width), (width, 3 * width)]
    bias_shapes = [(16, width), (8, width)]
    first = 1 + count + 5 + 7
    out = pl.pallas_call(
        functools.partial(whole_kernel, pieces=count, carried=bool(carried), after=len(after)),
        grid_spec=pltpu.PrefetchScalarGridSpec(
            num_scalar_prefetch=1,
            grid=(2 * GROUPS,),
            in_specs=[full((2, span, width))] * count
            + [pl.BlockSpec((1, 2 * AUG, length), lambda g, i: (row, 0, 0)), full(cols.shape)]
            + [full(w.shape) for w in wqkv]
            + [ANY] * 7
            + ([ANY] * 4 + [full(s) for s in bias_shapes] + [ANY] if carried else [])
            + [ANY] * len(after),
            out_specs=[pl.BlockSpec((count, 2, span, width), lambda g, i: (0, row, 0, 0))]
            + [ANY] * 4
            + [full(s) for s in bias_shapes],
            scratch_shapes=[
                pltpu.VMEM((4, width, length), bf16),
                pltpu.VMEM((HEADS, length, length), bf16),
                pltpu.VMEM((width, length), f32),
                pltpu.VMEM((16, length), f32),
                pltpu.VMEM((width, length), bf16),
                pltpu.VMEM((16, length), f32),
                pltpu.VMEM((width, length), f32),
                pltpu.VMEM((3 * width, length), bf16),
                pltpu.VMEM((PER_GROUP, length, length), bf16),
            ]
            + [pltpu.VMEM(w.shape, bf16) for w in weights]
            + [pltpu.VMEM(s, f32) for s in sum_shapes]
            + [
                pltpu.SMEM((1,), jnp.int32),
                pltpu.SemaphoreType.DMA((7,)),
                pltpu.SemaphoreType.DMA((4,)),
                pltpu.SemaphoreType.DMA((4,)),
            ],
        ),
        out_shape=[jax.ShapeDtypeStruct((count, height, span, width), bf16)]
        + [jax.ShapeDtypeStruct(s, f32) for s in sum_shapes + bias_shapes],
        input_output_aliases={first + 6: 0} if carried else {},
        compiler_params=pltpu.CompilerParams(vmem_limit_bytes=VMEM_LIMIT),
        cost_estimate=cost(20),
        name="whole",
    )(here, *pieces, aug, cols, *wqkv, *weights, *carried, *after)
    return out[1:], out[0]


def layer_kernel(index_ref, *refs, pieces, carried, after, parts, inner):
    take = Taker(refs)
    piece_refs = take(pieces)
    aug_ref, cols, wq, wk, wv = take(5)
    weights_hbm = take(6)
    sums_hbm = take(3 if carried else 0)
    bias_in = take(1 if carried else 0)
    take((1 if carried else 0) + after)
    (out_ref,) = take(1)
    saved_hbm, p_hbm, og_ref, delta_ref, gres_ref = take(5)
    part_refs = take(parts)
    saved, p_buf, att_ref, stat_ref = take(4)
    weights = take(6)
    sums = take(3)
    packed, small_ref, weight_sem, sum_sem, p_sem, saved_sem = take(6)
    group = pl.program_id(0)
    width = att_ref.shape[0]
    weight_copies = copies_of(weights_hbm, weights, weight_sem)
    sum_copies = copies_of(sums_hbm, sums, sum_sem)
    saved_copy = pltpu.make_async_copy(saved, saved_hbm, saved_sem)
    slot = lax.rem(group, 2)

    def p_copy(number):
        start = number * PER_GROUP
        return pltpu.make_async_copy(
            p_buf.at[lax.rem(number, 2)], p_hbm.at[pl.ds(start, PER_GROUP)], p_sem.at[lax.rem(number, 2)]
        )

    @pl.when(group == 0)
    def _():
        for copy in weight_copies + sum_copies:
            copy.start()
        project_row(piece_refs, cols, wq, wk, wv, saved, small_ref)
        saved_copy.start()

    @pl.when(group >= 2)
    def _():
        p_copy(group - 2).wait()

    attend_heads(group, saved, aug_ref, lambda h: p_buf.at[slot, h], att_ref, stat_ref, small_ref)
    p_copy(group).start()

    @pl.when(group == GROUPS - 1)
    def _():
        for copy in weight_copies + sum_copies:
            copy.wait()
        total = dense_row(
            piece_refs, cols, saved, att_ref, stat_ref, weights, sums, carried,
            lambda values: write_pieces(values, out_ref, index_ref[1]), lambda number: None, og_ref, delta_ref, gres_ref,
        )
        if carried:
            total = total + bias_in[0][...]
        acc_dn, acc_up, acc_out = sums
        ff = acc_dn.shape[0]
        packed[:ff] = acc_dn[...].astype(bf16)
        for index in range(ff // width):
            packed[ff + index * width : ff + (index + 1) * width] = acc_up[
                :, index * width : (index + 1) * width
            ].astype(bf16)
        packed[2 * ff : 2 * ff + width] = acc_out[...].astype(bf16)
        packed[2 * ff + width : 2 * ff + width + 16] = total.astype(bf16)
        rest = packed.shape[0] - 2 * ff - width - 16
        if rest:
            packed[2 * ff + width + 16 :] = jnp.zeros((rest, width), bf16)
        emit(packed, index_ref[0], part_refs, inner)
        saved_copy.wait()
        for number in range(max(GROUPS - 2, 0), GROUPS):
            p_copy(number).wait()


def layer(pieces, row, height, aug, cols, wqkv, weights, sums, packed_rows, parts, inner, index, after):
    _, span, width = pieces[0].shape
    count = len(pieces)
    length = span * count
    ff = weights[3].shape[1]
    full = lambda shape: pl.BlockSpec(shape, lambda g, i: (0,) * len(shape))
    sum_shapes = [(ff, width), (width, ff), (width, width)]
    part = (packed_rows // parts, width)
    out = pl.pallas_call(
        functools.partial(
            layer_kernel, pieces=count, carried=bool(sums), after=len(after), parts=parts, inner=inner
        ),
        grid_spec=pltpu.PrefetchScalarGridSpec(
            num_scalar_prefetch=1,
            grid=(GROUPS,),
            in_specs=[full((2, span, width))] * count
            + [pl.BlockSpec((1, 2 * AUG, length), lambda g, i: (row, 0, 0)), full(cols.shape)]
            + [full(w.shape) for w in wqkv]
            + [ANY] * 6
            + ([ANY] * 3 + [full((16, width)), ANY] if sums else [])
            + [ANY] * len(after),
            out_specs=[pl.BlockSpec((count, 1, span, width), lambda g, i: (0, height - 1, 0, 0))]
            + [ANY, ANY, full((width, length)), full((16, length)), full((width, length))]
            + [full(part)] * parts,
            scratch_shapes=[
                pltpu.VMEM((4, width, length), bf16),
                pltpu.VMEM((2, PER_GROUP, length, length), bf16),
                pltpu.VMEM((width, length), f32),
                pltpu.VMEM((16, length), f32),
            ]
            + [pltpu.VMEM(w.shape, bf16) for w in weights]
            + [pltpu.VMEM(shape, f32) for shape in sum_shapes]
            + [
                pltpu.VMEM((packed_rows, width), bf16),
                pltpu.SMEM((1,), jnp.int32),
                pltpu.SemaphoreType.DMA((6,)),
                pltpu.SemaphoreType.DMA((3,)),
                pltpu.SemaphoreType.DMA((2,)),
                pltpu.SemaphoreType.DMA,
            ],
        ),
        out_shape=[jax.ShapeDtypeStruct((count, height, span, width), bf16)]
        + [
            jax.ShapeDtypeStruct((4, width, length), bf16),
            jax.ShapeDtypeStruct((HEADS, length, length), bf16),
            jax.ShapeDtypeStruct((width, length), bf16),
            jax.ShapeDtypeStruct((16, length), f32),
            jax.ShapeDtypeStruct((width, length), f32),
        ]
        + [jax.ShapeDtypeStruct(part, bf16)] * parts,
        input_output_aliases={1 + count + 5 + 6 + 4: 0} if sums else {},
        compiler_params=pltpu.CompilerParams(vmem_limit_bytes=VMEM_LIMIT),
        cost_estimate=cost(14),
        name="layer",
    )(index, *pieces, aug, cols, *wqkv, *weights, *sums, *after)
    return out[0], out[1:6], out[6:]


def back_kernel(index_ref, *refs, carried, after, parts, inner):
    take = Taker(refs)
    saved, og_ref, delta_ref, p_ref, saved_hbm, gres_hbm, w_hbm = take(7)
    sum_hbm = take(1 if carried else 0)
    bias_in = take(1 if carried else 0)
    take(after)
    (out_ref,) = take(1)
    part_refs = take(parts)
    grads, held, xt, gres, w_all = take(5)
    sum_in = take(1 if carried else 0)
    packed, sem = take(2)
    group = pl.program_id(0)
    width = og_ref.shape[0]
    copies = copies_of([saved_hbm.at[3], gres_hbm, w_hbm] + sum_hbm, [xt, gres, w_all] + sum_in, sem)

    @pl.when(group == 0)
    def _():
        for copy in copies:
            copy.start()

    back_heads(group, saved, og_ref, delta_ref, lambda h: p_ref.at[h], grads, held)

    @pl.when(group == GROUPS - 1)
    def _():
        for copy in copies:
            copy.wait()
        total = grads[...]
        acc = dot(xt[...], total, NT)
        bias = back_biases(total, width)
        if carried:
            acc = acc + sum_in[0][...]
            bias = bias + bias_in[0][...]
        per = width // 128
        for index in range(3 * per):
            packed[index * width : (index + 1) * width] = acc[:, index * 128 : (index + 1) * 128].astype(bf16)
        bias_rows = [bias[n : n + 1, i * 128 : (i + 1) * 128] for n in range(2) for i in range(per)]
        tail = packed.shape[0] - 3 * per * width
        bias_rows.append(jnp.zeros((tail - len(bias_rows), 128), f32))
        packed[3 * per * width :] = jnp.concatenate(bias_rows, axis=0).astype(bf16)
        emit(packed, index_ref[0], part_refs, inner)
        write_pieces((gres[...] + dot(w_all[...], total)).astype(bf16), out_ref, index_ref[1])


def back(count, saved, probs, og, delta, gres, w_all, sums, packed_rows, parts, inner, index, after):
    _, width, length = saved.shape
    span = length // count
    full = lambda shape: pl.BlockSpec(shape, lambda g, i: (0,) * len(shape))
    part = (packed_rows // parts, 128)
    out = pl.pallas_call(
        functools.partial(back_kernel, carried=bool(sums), after=len(after), parts=parts, inner=inner),
        grid_spec=pltpu.PrefetchScalarGridSpec(
            num_scalar_prefetch=1,
            grid=(GROUPS,),
            in_specs=[
                full((3, width, length)),
                full((width, length)),
                full((16, length)),
                pl.BlockSpec((PER_GROUP, length, length), lambda g, i: (g, 0, 0)),
            ]
            + [ANY] * 3
            + ([ANY, full((8, width))] if sums else [])
            + [ANY] * len(after),
            out_specs=[full((count, 1, span, width))] + [full(part)] * parts,
            scratch_shapes=[
                pltpu.VMEM((3 * width, length), bf16),
                pltpu.VMEM((PER_GROUP, length, length), bf16),
                pltpu.VMEM((width, length), bf16),
                pltpu.VMEM((width, length), f32),
                pltpu.VMEM(w_all.shape, bf16),
            ]
            + ([pltpu.VMEM((width, 3 * width), f32)] if sums else [])
            + [pltpu.VMEM((packed_rows, 128), bf16), pltpu.SemaphoreType.DMA((4,))],
        ),
        out_shape=[jax.ShapeDtypeStruct((count, 1, span, width), bf16)] + [jax.ShapeDtypeStruct(part, bf16)] * parts,
        compiler_params=pltpu.CompilerParams(vmem_limit_bytes=VMEM_LIMIT),
        cost_estimate=cost(9),
        name="back",
    )(index, saved, og, delta, probs, saved, gres, w_all, *sums, *after)
    return out[0], out[1:]


def exchange(pieces, axis, devices, unit=1):
    moved = [pieces[0]]
    for shift in range(1, len(pieces)):
        moved.append(lax.ppermute(pieces[shift], axis, [(i, i ^ (shift * unit)) for i in range(devices)]))
    return moved


def tree_sum(blocks):
    while len(blocks) > 1:
        blocks = [left + right for left, right in zip(blocks[::2], blocks[1::2])]
    return blocks[0]


def combine_kernel(index_ref, *refs, inputs, after, inner):
    total = tree_sum([ref[...].astype(f32) for ref in refs[:inputs]]).astype(bf16)
    outs = refs[inputs + after :]
    if len(outs) == 1:
        outs[0][...] = total
    else:
        packed = outs[-1]
        packed[...] = total
        emit(packed, index_ref[0], outs[:-1], inner)


def combine(blocks, parts, inner, index, after=()):
    rows, width = blocks[0].shape
    part = (rows // parts, width)
    full = lambda s: pl.BlockSpec(s, lambda i, j: (0, 0))
    return pl.pallas_call(
        functools.partial(combine_kernel, inputs=len(blocks), after=len(after), inner=inner),
        grid_spec=pltpu.PrefetchScalarGridSpec(
            num_scalar_prefetch=1,
            grid=(1,),
            in_specs=[full((rows, width))] * len(blocks) + [pl.BlockSpec(memory_space=pl.ANY)] * len(after),
            out_specs=[full(part)] * parts,
            scratch_shapes=[pltpu.VMEM((rows, width), bf16)] if parts > 1 else [],
        ),
        out_shape=[jax.ShapeDtypeStruct(part, bf16)] * parts,
        compiler_params=pltpu.CompilerParams(vmem_limit_bytes=VMEM_LIMIT),
        cost_estimate=cost(1),
        name="combine",
    )(index, *blocks, *after)


def merge_kernel(index_ref, *refs, count, after, parts, inner):
    left = tree_sum([ref[...].astype(f32) for ref in refs[:count]])
    right = tree_sum([ref[...].astype(f32) for ref in refs[count : 2 * count]])
    packed = refs[-1]
    packed[...] = jnp.concatenate([left, right], axis=1).astype(bf16)
    emit(packed, index_ref[0], refs[2 * count + after : -1], inner)


def merge(lefts, rights, stage, after=()):
    rows, left = lefts[0].shape
    width = left + rights[0].shape[1]
    parts = stage[3]
    full = lambda s: pl.BlockSpec(s, lambda i, j: (0, 0))
    return pl.pallas_call(
        functools.partial(merge_kernel, count=len(lefts), after=len(after), parts=parts, inner=stage[4]),
        grid_spec=pltpu.PrefetchScalarGridSpec(
            num_scalar_prefetch=1,
            grid=(1,),
            in_specs=[full(b.shape) for b in list(lefts) + list(rights)] + [ANY] * len(after),
            out_specs=[full((rows // parts, width))] * parts,
            scratch_shapes=[pltpu.VMEM((rows, width), bf16)],
        ),
        out_shape=[jax.ShapeDtypeStruct((rows // parts, width), bf16)] * parts,
        compiler_params=pltpu.CompilerParams(vmem_limit_bytes=VMEM_LIMIT),
        cost_estimate=cost(2),
        name="merge",
    )(place_of(stage), *lefts, *rights, *after)


def put_together(refs, out, index, inner):
    size = refs[0].shape[0] // inner
    for shift, ref in enumerate(refs):
        for block in range(inner):
            start = pl.multiple_of((block * len(refs) + (index ^ shift)) * size, 16)
            out[pl.ds(start, size), :] = ref[block * size : (block + 1) * size]


def assemble_kernel(index_ref, *refs, inputs, after, inner):
    put_together(refs[:inputs], refs[inputs + after], index_ref[0], inner)


def assemble(blocks, stage, after=(), through=()):
    rows, width = blocks[0].shape
    full = lambda s: pl.BlockSpec(s, lambda i, j: (0, 0))
    shape = (rows * len(blocks), width)
    first = 1 + len(blocks) + len(after)
    after = list(after) + list(through)
    out = pl.pallas_call(
        functools.partial(assemble_kernel, inputs=len(blocks), after=len(after), inner=stage[4]),
        grid_spec=pltpu.PrefetchScalarGridSpec(
            num_scalar_prefetch=1,
            grid=(1,),
            in_specs=[full((rows, width))] * len(blocks) + [ANY] * len(after),
            out_specs=[full(shape)] + [ANY] * len(through),
        ),
        out_shape=[jax.ShapeDtypeStruct(shape, bf16)] + [jax.ShapeDtypeStruct(a.shape, a.dtype) for a in through],
        input_output_aliases={first + i: 1 + i for i in range(len(through))},
        compiler_params=pltpu.CompilerParams(vmem_limit_bytes=VMEM_LIMIT),
        cost_estimate=cost(1),
        name="assemble",
    )(place_of(stage), *blocks, *after)
    return out[0], out[1:]


def place_kernel(*refs, rows):
    outs = refs[-2:]
    row = pl.program_id(0)
    for number in range(rows):

        @pl.when(row == number)
        def _(number=number):
            for which in range(2):
                outs[which][...] = refs[2 * number + which][...].astype(outs[which].dtype)


def place(sources):
    rows = len(sources)
    count, _, span, width = sources[0][0][0].shape
    shape = (count, rows, span, width)
    in_specs = []
    arrays = []
    for row in sources:
        for sent, at in row:
            in_specs.append(pl.BlockSpec((count, 1, span, width), lambda r, at=at: (0, at, 0, 0)))
            arrays.append(sent)
    out_spec = pl.BlockSpec((count, 1, span, width), lambda r: (0, r, 0, 0))
    layer_out, grad = pl.pallas_call(
        functools.partial(place_kernel, rows=rows),
        grid=(rows,),
        in_specs=in_specs,
        out_specs=[out_spec, out_spec],
        out_shape=[jax.ShapeDtypeStruct(shape, bf16), jax.ShapeDtypeStruct(shape, f32)],
        compiler_params=pltpu.CompilerParams(vmem_limit_bytes=VMEM_LIMIT),
        cost_estimate=cost(5),
        name="place",
    )(*arrays)
    return layer_out.reshape(count * rows, span, width), grad.reshape(count * rows, span, width)


def sum_stages(sizes):
    stages = []
    for axis in ("rows", "seq"):
        devices = sizes[axis]
        unit = 1
        while unit < devices:
            size = 2 if unit == 1 and devices.bit_length() % 2 == 0 else 4
            stages.append((axis, devices, unit, size, devices // (unit * size)))
            unit *= size
    return stages


def place_of(stage):
    axis, _, unit, size, _ = stage
    return ((lax.axis_index(axis) // unit) % size).astype(jnp.int32).reshape(1)


def send_parts(parts, stage):
    axis, devices, unit, _, _ = stage
    return exchange(parts, axis, devices, unit)


def cut_for(taken, stage, after=()):
    return combine(taken, stage[3], stage[4], place_of(stage), after)


def add(taken, after=()):
    return combine(taken, 1, 1, jnp.zeros((1,), jnp.int32), after)[0]


def unpack_kernel(index_ref, *refs, inputs, after, inner):
    down, up, out, *biases = refs[inputs + after : inputs + after + 10]
    query, key, value, bias_q, bias_v = refs[inputs + after + 10 : -1]
    block = refs[-1]
    put_together(refs[:inputs], block, index_ref[0], inner)
    ff, width = down.shape
    per = ff // width
    down[...] = block[:ff, :width].astype(f32)
    for index in range(per):
        rows = slice(ff + index * width, ff + (index + 1) * width)
        up[:, index * width : (index + 1) * width] = block[rows, :width].astype(f32)
    out[...] = block[2 * ff : 2 * ff + width, :width].astype(f32)
    rows = block[2 * ff + width : 2 * ff + width + 16, :width].astype(f32)
    for index, ref in enumerate(biases[:-1]):
        ref[...] = rows[index]
    biases[-1][...] = jnp.concatenate([rows[len(biases) - 1 + i] for i in range(per)], axis=0)
    per = width // 128
    for number, ref in enumerate((query, key, value)):
        for index in range(per):
            start = (number * per + index) * width
            ref[:, index * 128 : (index + 1) * 128] = block[start : start + width, width:].astype(f32)
    rows = block[3 * per * width : 3 * per * width + 16, width:].astype(f32)
    for number, ref in enumerate((bias_q, bias_v)):
        ref[...] = jnp.concatenate([rows[number * per + i] for i in range(per)], axis=0)


def unpack(blocks, stage, shapes, after=()):
    rows, width = blocks[0].shape
    full = lambda s: pl.BlockSpec(s, lambda i, j: (0,) * len(s))
    return pl.pallas_call(
        functools.partial(unpack_kernel, inputs=len(blocks), after=len(after), inner=stage[4]),
        grid_spec=pltpu.PrefetchScalarGridSpec(
            num_scalar_prefetch=1,
            grid=(1,),
            in_specs=[full((rows, width))] * len(blocks) + [ANY] * len(after),
            out_specs=[full(s) for s in shapes],
            scratch_shapes=[pltpu.VMEM((rows * len(blocks), width), bf16)],
        ),
        out_shape=[jax.ShapeDtypeStruct(s, f32) for s in shapes],
        compiler_params=pltpu.CompilerParams(vmem_limit_bytes=VMEM_LIMIT),
        cost_estimate=cost(4),
        name="unpack",
    )(place_of(stage), *blocks, *after)


def round_up(value, unit):
    return -(-value // unit) * unit


def body(
    tokens, lengths, w_query, b_query, w_key, w_value, b_value, w_out, b_out, gain_attn, shift_attn,
    w_up, b_up, w_down, b_down, gain_ffn, shift_ffn, cotangent, *, sizes,
):
    count = sizes["seq"]
    devices = count * sizes["rows"]
    row_count, span, width = tokens.shape
    ff = w_up.shape[1]
    length = span * count
    rows = row_count // count
    me = lax.axis_index("seq")
    here = me.astype(jnp.int32).reshape(1)
    order = me ^ jnp.arange(count, dtype=jnp.int32)
    stages = sum_stages(sizes)
    row_stages, seq_stages = [[stage for stage in stages if stage[0] == axis] for axis in ("rows", "seq")]
    first = stages[0]
    index = place_of(first)
    later_rows = round_up(2 * ff + width + 16, 16 * devices)
    first_rows = later_rows

    picked = {0: pick(tokens, cotangent, count, rows, 0, here, [])}
    given = {0: exchange(picked[0], "seq", count)}

    bounds = lax.dynamic_slice_in_dim(jnp.cumsum(lengths, axis=1), me * rows, rows, 0)
    places = (order[:, None] * span + jnp.arange(span, dtype=jnp.int32)[None, :]).reshape(length)
    segment = jnp.sum((places[None, None, :] >= bounds[:, :, None]).astype(jnp.int32), axis=1)
    ids = jnp.arange(2 * AUG, dtype=jnp.int32)[None, :, None]
    same = segment[:, None, :] == ids % AUG
    aug = jnp.where(ids < AUG, jnp.where(same, 1.0, 0.0), jnp.where(same | (ids % AUG >= lengths.shape[1]), 0.0, -BIG))
    aug = aug.astype(bf16)

    vectors = [b_query, b_value, b_out, gain_attn, shift_attn, b_down, gain_ffn, shift_ffn]
    vectors = jnp.concatenate([jnp.stack(vectors), b_up.reshape(-1, width)], axis=0)
    wq_t, wk_t, wv_t, wo_t, wup_t, wdn_t, cols = prepare((w_query, w_key, w_value, w_out, w_up, w_down), vectors)
    dense_weights = (wo_t, w_out, wup_t, w_up, wdn_t, w_down)
    w_all = jnp.concatenate([w_query, w_key, w_value], axis=1)

    wqkv = (wq_t, wk_t, wv_t)
    last = rows - 1

    def send_row(row, after):
        if row > last:
            return []
        picked[row] = pick(tokens, cotangent, count, rows, row, here, list(given[row - 1][1:]) + after)
        given[row] = exchange(picked[row], "seq", count)
        return picked[row][:1]

    both = jnp.concatenate([index, here])
    carried, shared = [], None
    for row in range(last):
        after = send_row(row + 1, [] if shared is None else [shared])
        sums, shared = whole(here, given[row], row, 2 * last + 1, aug, cols, wqkv, dense_weights + (w_all,), carried, after)
        carried = list(sums) + [shared]

    def return_pieces(array):
        return lax.all_to_all(array, "seq", 0, 0, tiled=True)

    shared, saved, later = layer(
        given[last], last, 2 * last + 1, aug, cols, wqkv, dense_weights,
        (carried[:3] + carried[4:5] + carried[6:]) if carried else [], later_rows,
        first[3], first[4], both, [],
    )
    keys, probs, og, delta, gres = saved
    taken = send_parts(later, first)
    moved = return_pieces(shared)
    ends, early = back(
        count, keys, probs, og, delta, gres, w_all, (carried[3:4] + carried[5:6]) if carried else [], first_rows,
        first[3], first[4], both, [],
    )
    parts = early
    after = list(early[:1])
    for stage in row_stages[1:]:
        cut = cut_for(taken, stage, after)
        taken = send_parts(cut, stage)
        after = list(cut[:1])
    given_early = send_parts(early, first)
    for number, stage in enumerate(row_stages[1:]):
        parts = cut_for(given_early, stage, after)
        given_early = send_parts(parts, stage)
    parts = merge(taken, given_early, seq_stages[0], [moved])
    for number, stage in enumerate(seq_stages):
        taken = send_parts(parts, stage)
        if number + 1 < len(seq_stages):
            parts = cut_for(taken, seq_stages[number + 1])
    block = add(taken)
    for number, stage in enumerate(reversed(stages[1:])):
        taken = send_parts([block] * stage[3], stage)
        at_end = number == len(stages) - 2
        if at_end:
            ends = return_pieces(ends)
        block, passed = assemble(taken, stage, [ends] if at_end else [], [] if at_end else [ends])
        ends = passed[0] if passed else ends
    shapes = [(ff, width), (width, ff), (width, width)] + [(width,)] * 6 + [(ff,)] + [(width, width)] * 3 + [(width,)] * 2
    (
        grad_down, grad_up, grad_output, grad_gain2, grad_shift2, grad_dnbias, grad_gain1, grad_shift1, grad_obias,
        grad_upbias, grad_query, grad_key, grad_value, grad_qbias, grad_vbias,
    ) = unpack(send_parts([block] * first[3], first), first, shapes)
    layer_out, grad_tokens = place([((moved, 2 * row), (moved, 2 * row + 1)) for row in range(last)] + [((moved, 2 * last), (ends, 0))])
    return (
        layer_out, grad_tokens, grad_query, grad_qbias, grad_key, grad_value, grad_vbias, grad_output, grad_obias,
        grad_gain1, grad_shift1, grad_up, grad_upbias, grad_down, grad_dnbias, grad_gain2, grad_shift2,
    )


def solution(mesh):
    split = P("rows", "seq", None)
    in_specs = (split, P("rows", None)) + (P(),) * 15 + (split,)
    out_specs = (split, split) + (P(),) * 15
    sizes = dict(mesh.shape)
    return jax.shard_map(
        functools.partial(body, sizes=sizes), mesh=mesh, in_specs=in_specs, out_specs=out_specs, check_vma=False
    )
```

time: 286 us -> 229 us (0.80)
  local copies, waits for them, and re-layouts: 51.2 us -> 11.3 us
  Pallas kernels: 72.8 us -> 110 us
  other arithmetic: 30.8 us -> 1.54 us
  waiting for transfers between devices: 68.9 us -> 53.8 us
  starting transfers between devices: 59.7 us -> 49.4 us
    pallas_call x3 -> x16, Pallas kernels: 72.8 us -> 110 us  [the longest x2 45 us: whole(): pl.pallas_call(functools.partial(whole_kernel, pieces=count, carried=bool...]
    concatenate x16 -> x1, other arithmetic: 24.6 us -> 0.58 us  [body(): both = jnp.concatenate([index, here])]
    pallas_call x2 -> x0, local copies, waits for them, and re-layouts: 19.1 us -> none  [attend(): pl.pallas_call(functools.partial(attend_kernel, pieces=count, row_base=0)...]
    ppermute x38 -> x27, starting transfers between devices: 59.7 us -> 41.9 us  [exchange(): lax.ppermute(pieces[shift], axis, [(i, i ^ shift * unit) for i in range(d...]
    ppermute x38 -> x27, waiting for transfers between devices: 68.9 us -> 53.8 us  [exchange(): lax.ppermute(pieces[shift], axis, [(i, i ^ shift * unit) for i in range(d...]
    reshape x10 -> x1, local copies, waits for them, and re-layouts: 8.21 us -> 0.01 us  [body(): b_up.reshape(-1, width)]
    all_to_all x0 -> x2, starting transfers between devices: none -> 7.46 us  [return_pieces(): return lax.all_to_all(array, 'seq', 0, 0, tiled=True)]
    slice x5 -> x0, local copies, waits for them, and re-layouts: 5.05 us -> none  [the longest x1 1.56 us: body(): grad_down = later[:ff]]
  transfers between devices with their start and end apart: 38 -> 29, of which waited for: 17 -> 11; matrix products, arithmetic and copies ran while one was open for 24% -> 1% of each run, Pallas kernels for 3% -> 31%
where the time goes in v3:
time: 229 us; the launch traced here: 227 us
  Pallas kernels  110 us (48%)
  waiting for transfers between devices  53.8 us (23%)
  starting transfers between devices  49.4 us (22%)
  local copies, waits for them, and re-layouts  11.3 us (5%)
    ppermute x27, waiting for transfers between devices, exchange(): lax.ppermute(pieces[shift], axis, [(i, i ^ shift * unit) for i in range(d...  53.8 us
    pallas_call x2, Pallas kernels, whole(): pl.pallas_call(functools.partial(whole_kernel, pieces=count, carried=bool...  45 us
    ppermute x27, starting transfers between devices, exchange(): lax.ppermute(pieces[shift], axis, [(i, i ^ shift * unit) for i in range(d...  41.9 us
    pallas_call x1, Pallas kernels, layer(): pl.pallas_call(functools.partial(layer_kernel, pieces=count, carried=bool...  19.2 us
    pallas_call x1, Pallas kernels, back(): pl.pallas_call(functools.partial(back_kernel, carried=bool(sums), after=l...  11.4 us
    unnamed x86, local copies, waits for them, and re-layouts  9.81 us
    all_to_all x2, starting transfers between devices, return_pieces(): return lax.all_to_all(array, 'seq', 0, 0, tiled=True)  7.46 us
    pallas_call x3, Pallas kernels, combine(): pl.pallas_call(functools.partial(combine_kernel, inputs=len(blocks), afte...  7.39 us
  transfers between devices with their start and end apart: 29, of which 11 were waited for; matrix products, arithmetic and copies ran while one was open for 1% of the time, Pallas kernels for 31%

profile of v3, /device:TPU:0, one launch (start us, length us, event | category | flops | bytes accessed | tf_op | source)
XLA Modules:
  0.0 227.4 jit_solution(3765954380150611155)
XLA Ops:
  0.8 2.2 pick.3
  3.0 3.0 %collective-permute-start = (bf16[2,128,384]{2,1,0:T(8,128)(2,1)}, bf16[2,128,384]{2,1,0:T(8,128)(2,1)S(1)}, u32[]{:S(2)}, u32[]{:S(2)}) collective-permute-start(bf16[2,128,384]{2,1,0:T(8,128)(2,1)} %get-tuple-element.92), channel_id=1, source_target_pairs={{0,1},{1,0},{2,3},{3,2},{4,5},{5,4},{6,7},{7,6},{8,9},{9,8},{10,11... | collective-permute-start | bytes 589832 | tf_op jit(solution)/shard_map/ppermute | solution.py:631
  6.0 2.6 %collective-permute-start.1 = (bf16[2,128,384]{2,1,0:T(8,128)(2,1)}, bf16[2,128,384]{2,1,0:T(8,128)(2,1)S(1)}, u32[]{:S(2)}, u32[]{:S(2)}) collective-permute-start(bf16[2,128,384]{2,1,0:T(8,128)(2,1)} %get-tuple-element.93), channel_id=1, source_target_pairs={{0,2},{1,3},{2,0},{3,1},{4,6},{5,7},{6,4},{7,5},{8,10},{9,11},{10,... | collective-permute-start | bytes 589832 | tf_op jit(solution)/shard_map/ppermute | solution.py:631
  10.5 4.1 %prepare.1 = (bf16[384,384]{1,0:T(8,128)(2,1)}, bf16[384,384]{1,0:T(8,128)(2,1)}, bf16[384,384]{1,0:T(8,128)(2,1)}, bf16[384,384]{1,0:T(8,128)(2,1)}, bf16[1536,...) custom-call(bf16[384,384]{1,0:T(8,128)(2,1)} %wq.1, bf16[384,384]{1,0:T(8,128)(2,1)} %wk.1, ...), custom_call_target="tpu_custom_call" | custom-call | flops 500000 | bytes 5000 | tf_op jit(solution)/shard_map/prepare/pallas_call | solution.py:78
  14.7 8.7 %collective-permute-done.1.refs_9_.refs_2_ = bf16[2,128,384]{2,1,0:T(8,128)(2,1)S(1)} collective-permute-done((bf16[2,128,384]{2,1,0:T(8,128)(2,1)}, bf16[2,128,384]{2,1,0:T(8,128)(2,1)S(1)}, u32[]{:S(2)}, u32[]{:S(2)}) %collective-permute-start.1) | collective-permute-done | bytes 196640 | tf_op jit(solution)/shard_map/ppermute | solution.py:631
  24.7 2.1 pick.4
  26.9 2.7 %collective-permute-start.3 = (bf16[2,128,384]{2,1,0:T(8,128)(2,1)}, bf16[2,128,384]{2,1,0:T(8,128)(2,1)S(1)}, u32[]{:S(2)}, u32[]{:S(2)}) collective-permute-start(bf16[2,128,384]{2,1,0:T(8,128)(2,1)} %get-tuple-element.95), channel_id=1, source_target_pairs={{0,1},{1,0},{2,3},{3,2},{4,5},{5,4},{6,7},{7,6},{8,9},{9,8},{10,11... | collective-permute-start | bytes 589832 | tf_op jit(solution)/shard_map/ppermute | solution.py:631
  32.8 22.4 %whole.2 = (bf16[4,5,128,384]{3,2,1,0:T(8,128)(2,1)}, f32[1536,384]{1,0:T(8,128)}, f32[384,1536]{1,0:T(8,128)}, f32[384,384]{1,0:T(8,128)}, f32[384,1152]{1,0:T(...) custom-call(s32[1]{0:T(128)} %bitcast.1.index_ref.here_ref, bf16[2,128,384]{2,1,0:T(8,128)(2,1)} %get-tuple-element.98.refs_0_, ...), custom_call_target="tpu_custom_call" | custom-call | flops 2000000 | bytes 20000 | tf_op jit(solution)/shard_map/whole/pallas_call | solution.py:375
  56.0 2.1 pick.5
  63.1 22.6 %whole.3 = (bf16[4,5,128,384]{3,2,1,0:T(8,128)(2,1)}, f32[1536,384]{1,0:T(8,128)}, f32[384,1536]{1,0:T(8,128)}, f32[384,384]{1,0:T(8,128)}, f32[384,1152]{1,0:T(...) custom-call(s32[1]{0:T(128)} %bitcast.1.index_ref.here_ref, ...), custom_call_target="tpu_custom_call", output_to_operand_aliasing={{0}: (23, {})} | custom-call | flops 2000000 | bytes 20000 | tf_op jit(solution)/shard_map/whole/pallas_call | solution.py:375
  86.5 19.2 %layer.1 = (bf16[4,5,128,384]{3,2,1,0:T(8,128)(2,1)}, bf16[4,384,512]{2,1,0:T(8,128)(2,1)}, bf16[12,512,512]{2,1,0:T(8,128)(2,1)}, bf16[384,512]{1,0:T(8,128)(2,...) custom-call(s32[2]{0:T(128)} %pad_add_fusion.index_ref, ...), custom_call_target="tpu_custom_call", output_to_operand_aliasing={{0}: (20, {})} | custom-call | flops 1400000 | bytes 14000 | tf_op jit(solution)/shard_map/layer/pallas_call | solution.py:497
  105.7 3.9 %all-to-all-start = ((bf16[4,5,128,384]{3,2,1,0:T(8,128)(2,1)}), bf16[4,5,128,384]{3,2,1,0:T(8,128)(2,1)S(1)}, u32[]{:S(2)}, u32[]{:S(2)}) async-start(bf16[4,5,128,384]{3,2,1,0:T(8,128)(2,1)} %get-tuple-element.123), calls=%async_computation | async-start | bytes 3932160 | tf_op jit(solution)/shard_map/all_to_all | solution.py:905
  109.7 11.4 %back.1 = (bf16[4,1,128,384]{3,2,1,0:T(8,128)(2,1)}, bf16[1792,128]{1,0:T(8,128)(2,1)}, bf16[1792,128]{1,0:T(8,128)(2,1)}) custom-call(s32[2]{0:T(128)} %pad_add_fusion.index_ref, bf16[4,384,512]{2,1,0:T(8,128)(2,1)} %get-tuple-element.126.refs_0_.refs_4_, bf16[384,512]{1,0:T(8,128)(2,1)} %get-tuple-element.127.refs_1_, ...), custom_call_target="tpu_custom_call" | custom-call | flops 900000 | bytes 9000 | tf_op jit(solution)/shard_map/back/pallas_call | solution.py:595
  122.7 3.5 %combine.3 = (bf16[448,384]{1,0:T(8,128)(2,1)}, bf16[448,384]{1,0:T(8,128)(2,1)}, bf16[448,384]{1,0:T(8,128)(2,1)}, bf16[448,384]{1,0:T(8,128)(2,1)}) custom-call(s32[1]{0:T(128)} %bitcast.4.index_ref, bf16[1792,384]{1,0:T(8,128)(2,1)} %get-tuple-element.124.refs_0_, bf16[1792,384]{1,0:T(8,128)(2,1)} %copy-done.4, ...), custom_call_target="tpu_custom_call" | custom-call | flops 100000 | bytes 1000 | tf_op jit(solution)/shard_map/combine/pallas_call | solution.py:656
  127.7 4.0 %collective-permute-start.11 = (bf16[448,384]{1,0:T(8,128)(2,1)}, bf16[448,384]{1,0:T(8,128)(2,1)S(1)}, u32[]{:S(2)}, u32[]{:S(2)}) collective-permute-start(bf16[448,384]{1,0:T(8,128)(2,1)} %get-tuple-element.136), channel_id=1, source_target_pairs={{0,16},{4,20},{8,24},{12,28},{16,0},{20,4},{24,8},{28,12},{1,17},{... | collective-permute-start | bytes 1032200 | tf_op jit(solution)/shard_map/ppermute | solution.py:631
  131.7 2.1 combine.4
  137.3 9.0 %collective-permute-done.14.refs_5_ = bf16[448,128]{1,0:T(8,128)(2,1)S(1)} collective-permute-done((bf16[448,128]{1,0:T(8,128)(2,1)}, bf16[448,128]{1,0:T(8,128)(2,1)S(1)}, u32[]{:S(2)}, u32[]{:S(2)}) %collective-permute-start.14) | collective-permute-done | bytes 114720 | tf_op jit(solution)/shard_map/ppermute | solution.py:631
  146.3 4.9 %collective-permute-start.16 = (bf16[448,128]{1,0:T(8,128)(2,1)}, bf16[448,128]{1,0:T(8,128)(2,1)S(1)}, u32[]{:S(2)}, u32[]{:S(2)}) collective-permute-start(bf16[448,128]{1,0:T(8,128)(2,1)} %get-tuple-element.142), channel_id=1, source_target_pairs={{0,24},{4,28},{8,16},{12,20},{16,8},{20,12},{24,0},{28,4},{1,25},{... | collective-permute-start | bytes 344072 | tf_op jit(solution)/shard_map/ppermute | solution.py:631
  151.2 3.0 %collective-permute-done.16.refs_7_ = bf16[448,128]{1,0:T(8,128)(2,1)S(1)} collective-permute-done((bf16[448,128]{1,0:T(8,128)(2,1)}, bf16[448,128]{1,0:T(8,128)(2,1)S(1)}, u32[]{:S(2)}, u32[]{:S(2)}) %collective-permute-start.16) | collective-permute-done | bytes 114720 | tf_op jit(solution)/shard_map/ppermute | solution.py:631
  155.8 2.6 %merge.1 = (bf16[112,512]{1,0:T(8,128)(2,1)}, bf16[112,512]{1,0:T(8,128)(2,1)}, bf16[112,512]{1,0:T(8,128)(2,1)}, bf16[112,512]{1,0:T(8,128)(2,1)}) custom-call(s32[1]{0:T(128)} %bitcast.3.index_ref, bf16[448,384]{1,0:T(8,128)(2,1)} %get-tuple-element.134.refs_2_.refs_0_, bf16[448,384]{1,0:T(8,128)(2,1)} %copy-done.17, bf16[448,384]{1,0:T(8,128)(2,1)} %copy-done.18, ...), custom_call_target="tpu_custom_call" | custom-call | flops 200000 | bytes 2000 | tf_op jit(solution)/shard_map/merge/pallas_call | solution.py:685
  160.4 2.4 %collective-permute-start.18 = (bf16[112,512]{1,0:T(8,128)(2,1)}, bf16[112,512]{1,0:T(8,128)(2,1)S(1)}, u32[]{:S(2)}, u32[]{:S(2)}) collective-permute-start(bf16[112,512]{1,0:T(8,128)(2,1)} %get-tuple-element.145), channel_id=1, source_target_pairs={{0,2},{1,3},{2,0},{3,1},{4,6},{5,7},{6,4},{7,5},{8,10},{9,11},{10,... | collective-permute-start | bytes 344072 | tf_op jit(solution)/shard_map/ppermute | solution.py:631
  164.5 6.3 %collective-permute-done.18.refs_2_ = bf16[112,512]{1,0:T(8,128)(2,1)S(1)} collective-permute-done((bf16[112,512]{1,0:T(8,128)(2,1)}, bf16[112,512]{1,0:T(8,128)(2,1)S(1)}, u32[]{:S(2)}, u32[]{:S(2)}) %collective-permute-start.18) | collective-permute-done | bytes 114720 | tf_op jit(solution)/shard_map/ppermute | solution.py:631
  173.3 2.3 %collective-permute-start.22 = (bf16[112,512]{1,0:T(8,128)(2,1)}, bf16[112,512]{1,0:T(8,128)(2,1)S(1)}, u32[]{:S(2)}, u32[]{:S(2)}) collective-permute-start(bf16[112,512]{1,0:T(8,128)(2,1)} %combine.5.refs_0_), channel_id=1, source_target_pairs={{0,3},{1,2},{2,1},{3,0},{4,7},{5,6},{6,5},{7,4},{8,11},{9,10},{10,... | collective-permute-start | bytes 344072 | tf_op jit(solution)/shard_map/ppermute | solution.py:631
  177.7 3.5 %collective-permute-done.22.refs_3_ = bf16[112,512]{1,0:T(8,128)(2,1)S(1)} collective-permute-done((bf16[112,512]{1,0:T(8,128)(2,1)}, bf16[112,512]{1,0:T(8,128)(2,1)S(1)}, u32[]{:S(2)}, u32[]{:S(2)}) %collective-permute-start.22) | collective-permute-done | bytes 114720 | tf_op jit(solution)/shard_map/ppermute | solution.py:631
  181.2 3.1 %collective-permute-done.21.refs_2_ = bf16[112,512]{1,0:T(8,128)(2,1)S(1)} collective-permute-done((bf16[112,512]{1,0:T(8,128)(2,1)}, bf16[112,512]{1,0:T(8,128)(2,1)S(1)}, u32[]{:S(2)}, u32[]{:S(2)}) %collective-permute-start.21) | collective-permute-done | bytes 114720 | tf_op jit(solution)/shard_map/ppermute | solution.py:631
  186.8 3.6 %all-to-all-start.1 = ((bf16[4,1,128,384]{3,2,1,0:T(8,128)(2,1)}), bf16[4,1,128,384]{3,2,1,0:T(8,128)(2,1)S(1)}, u32[]{:S(2)}, u32[]{:S(2)}) async-start(bf16[4,1,128,384]{3,2,1,0:T(8,128)(2,1)} %get-tuple-element.148), calls=%async_computation.1 | async-start | bytes 786432 | tf_op jit(solution)/shard_map/all_to_all | solution.py:905
  190.4 2.6 %collective-permute-start.25 = (bf16[448,512]{1,0:T(8,128)(2,1)}, bf16[448,512]{1,0:T(8,128)(2,1)S(1)}, u32[]{:S(2)}, u32[]{:S(2)}) collective-permute-start(bf16[448,512]{1,0:T(8,128)(2,1)} %get-tuple-element.151.refs_0_), channel_id=1, source_target_pairs={{0,24},{4,28},{8,16},{12,20},{16,8},{20,12},{24,0},{28,4},{1,25},{... | collective-permute-start | bytes 1376264 | tf_op jit(solution)/shard_map/ppermute | solution.py:631
  193.9 11.1 %collective-permute-done.25.refs_3_ = bf16[448,512]{1,0:T(8,128)(2,1)S(1)} collective-permute-done((bf16[448,512]{1,0:T(8,128)(2,1)}, bf16[448,512]{1,0:T(8,128)(2,1)S(1)}, u32[]{:S(2)}, u32[]{:S(2)}) %collective-permute-start.25) | collective-permute-done | bytes 458784 | tf_op jit(solution)/shard_map/ppermute | solution.py:631
  205.0 6.8 %collective-permute-done.24.refs_2_ = bf16[448,512]{1,0:T(8,128)(2,1)S(1)} collective-permute-done((bf16[448,512]{1,0:T(8,128)(2,1)}, bf16[448,512]{1,0:T(8,128)(2,1)S(1)}, u32[]{:S(2)}, u32[]{:S(2)}) %collective-permute-start.24) | collective-permute-done | bytes 458784 | tf_op jit(solution)/shard_map/ppermute | solution.py:631
  213.8 2.8 %assemble.3.refs_0_ = bf16[1792,512]{1,0:T(8,128)(2,1)} custom-call(s32[1]{0:T(128)} %bitcast.4.index_ref, bf16[448,512]{1,0:T(8,128)(2,1)} %get-tuple-element.151.refs_0_, bf16[448,512]{1,0:T(8,128)(2,1)} %copy-done.16, bf16[448,512]{1,0:T(8,128)(2,1)} %copy-done.15, bf16[448,512]{1,0:T(8,128)(2,1)} %copy-done.14, bf16[4,1,128,384]{3,2,1,0:T(8,128)(2,1)} %copy-done.2), custom_call_target="tpu_custom_call" | custom-call | flops 100000 | bytes 1000 | tf_op jit(solution)/shard_map/assemble/pallas_call | solution.py:719
  216.6 3.8 %place.1 = (bf16[4,3,128,384]{3,2,1,0:T(8,128)(2,1)}, f32[4,3,128,384]{3,2,1,0:T(8,128)}) custom-call(bf16[4,5,128,384]{3,2,1,0:T(8,128)(2,1)} %copy-done, bf16[4,5,128,384]{3,2,1,0:T(8,128)(2,1)} %copy-done, bf16[4,5,128,384]{3,2,1,0:T(8,128)(2,1)} %copy-done, bf16[4,5,128,384]{3,2,1,0:T(8,128)(2,1)} %copy-done, bf16[4,5,128,384]{3,2,1,0:T(8,128)(2,1)} %copy-done, ...), custom_call_target="tpu_custom_call" | custom-call | flops 500000 | bytes 5000 | tf_op jit(solution)/shard_map/place/pallas_call | solution.py:758
  221.8 5.4 %unpack.1 = (f32[1536,384]{1,0:T(8,128)}, f32[384,1536]{1,0:T(8,128)}, f32[384,384]{1,0:T(8,128)}, f32[384]{0:T(512)}, f32[384]{0:T(512)}, /*index=5*/f32[384]{0...) custom-call(s32[1]{0:T(128)} %bitcast.index_ref, ...), custom_call_target="tpu_custom_call" | custom-call | flops 400000 | bytes 4000 | tf_op jit(solution)/shard_map/unpack/pallas_call | solution.py:830
  (149 shorter events, 36.2 us)
Async XLA Ops:
  0.8 8.4 %copy-start.6 = (bf16[384,384]{1,0:T(8,128)(2,1)S(1)}, bf16[384,384]{1,0:T(8,128)(2,1)}, u32[]{:S(2)}) copy-start(bf16[384,384]{1,0:T(8,128)(2,1)} %wk.1) | copy-start | bytes 884740
  3.0 11.7 %collective-permute-start = (bf16[2,128,384]{2,1,0:T(8,128)(2,1)}, bf16[2,128,384]{2,1,0:T(8,128)(2,1)S(1)}, u32[]{:S(2)}, u32[]{:S(2)}) collective-permute-start(bf16[2,128,384]{2,1,0:T(8,128)(2,1)} %get-tuple-element.92), channel_id=1, source_target_pairs={{0,1},{1,0},{2,3},{3,2},{4,5},{5,4},{6,7},{7,6},{8,9},{9,8},{10,11... | collective-permute-start | bytes 589832 | tf_op jit(solution)/shard_map/ppermute | solution.py:631
  6.0 17.4 %collective-permute-start.1 = (bf16[2,128,384]{2,1,0:T(8,128)(2,1)}, bf16[2,128,384]{2,1,0:T(8,128)(2,1)S(1)}, u32[]{:S(2)}, u32[]{:S(2)}) collective-permute-start(bf16[2,128,384]{2,1,0:T(8,128)(2,1)} %get-tuple-element.93), channel_id=1, source_target_pairs={{0,2},{1,3},{2,0},{3,1},{4,6},{5,7},{6,4},{7,5},{8,10},{9,11},{10,... | collective-permute-start | bytes 589832 | tf_op jit(solution)/shard_map/ppermute | solution.py:631
  8.6 14.8 %collective-permute-start.2 = (bf16[2,128,384]{2,1,0:T(8,128)(2,1)}, bf16[2,128,384]{2,1,0:T(8,128)(2,1)S(1)}, u32[]{:S(2)}, u32[]{:S(2)}) collective-permute-start(bf16[2,128,384]{2,1,0:T(8,128)(2,1)} %get-tuple-element.94), channel_id=1, source_target_pairs={{0,3},{1,2},{2,1},{3,0},{4,7},{5,6},{6,5},{7,4},{8,11},{9,10},{10,... | collective-permute-start | bytes 589832 | tf_op jit(solution)/shard_map/ppermute | solution.py:631
  14.7 12.2 %copy-start.1 = (bf16[384,1152]{1,0:T(8,128)(2,1)}, bf16[384,1152]{1,0:T(8,128)(2,1)S(1)}, u32[]{:S(2)}) copy-start(bf16[384,1152]{1,0:T(8,128)(2,1)S(1)} %constant_dynamic-update-slice_fusion.refs_15_.refs_6_) | copy-start | bytes 2654212
  14.7 8.7 %copy-start.11 = (bf16[2,128,384]{2,1,0:T(8,128)(2,1)}, bf16[2,128,384]{2,1,0:T(8,128)(2,1)S(1)}, u32[]{:S(2)}) copy-start(bf16[2,128,384]{2,1,0:T(8,128)(2,1)S(1)} %collective-permute-done.refs_8_.refs_1_) | copy-start | bytes 589828
  26.9 28.3 %collective-permute-start.3 = (bf16[2,128,384]{2,1,0:T(8,128)(2,1)}, bf16[2,128,384]{2,1,0:T(8,128)(2,1)S(1)}, u32[]{:S(2)}, u32[]{:S(2)}) collective-permute-start(bf16[2,128,384]{2,1,0:T(8,128)(2,1)} %get-tuple-element.95), channel_id=1, source_target_pairs={{0,1},{1,0},{2,3},{3,2},{4,5},{5,4},{6,7},{7,6},{8,9},{9,8},{10,11... | collective-permute-start | bytes 589832 | tf_op jit(solution)/shard_map/ppermute | solution.py:631
  29.5 25.7 %collective-permute-start.4 = (bf16[2,128,384]{2,1,0:T(8,128)(2,1)}, bf16[2,128,384]{2,1,0:T(8,128)(2,1)S(1)}, u32[]{:S(2)}, u32[]{:S(2)}) collective-permute-start(bf16[2,128,384]{2,1,0:T(8,128)(2,1)} %get-tuple-element.96), channel_id=1, source_target_pairs={{0,2},{1,3},{2,0},{3,1},{4,6},{5,7},{6,4},{7,5},{8,10},{9,11},{10,... | collective-permute-start | bytes 589832 | tf_op jit(solution)/shard_map/ppermute | solution.py:631
  30.6 24.6 %collective-permute-start.5 = (bf16[2,128,384]{2,1,0:T(8,128)(2,1)}, bf16[2,128,384]{2,1,0:T(8,128)(2,1)S(1)}, u32[]{:S(2)}, u32[]{:S(2)}) collective-permute-start(bf16[2,128,384]{2,1,0:T(8,128)(2,1)} %get-tuple-element.97), channel_id=1, source_target_pairs={{0,3},{1,2},{2,1},{3,0},{4,7},{5,6},{6,5},{7,4},{8,11},{9,10},{10,... | collective-permute-start | bytes 589832 | tf_op jit(solution)/shard_map/ppermute | solution.py:631
  58.1 27.6 %collective-permute-start.6 = (bf16[2,128,384]{2,1,0:T(8,128)(2,1)}, bf16[2,128,384]{2,1,0:T(8,128)(2,1)S(1)}, u32[]{:S(2)}, u32[]{:S(2)}) collective-permute-start(bf16[2,128,384]{2,1,0:T(8,128)(2,1)} %get-tuple-element.109), channel_id=1, source_target_pairs={{0,1},{1,0},{2,3},{3,2},{4,5},{5,4},{6,7},{7,6},{8,9},{9,8},{10,11... | collective-permute-start | bytes 589832 | tf_op jit(solution)/shard_map/ppermute | solution.py:631
  59.1 26.6 %collective-permute-start.7 = (bf16[2,128,384]{2,1,0:T(8,128)(2,1)}, bf16[2,128,384]{2,1,0:T(8,128)(2,1)S(1)}, u32[]{:S(2)}, u32[]{:S(2)}) collective-permute-start(bf16[2,128,384]{2,1,0:T(8,128)(2,1)} %get-tuple-element.110), channel_id=1, source_target_pairs={{0,2},{1,3},{2,0},{3,1},{4,6},{5,7},{6,4},{7,5},{8,10},{9,11},{10,... | collective-permute-start | bytes 589832 | tf_op jit(solution)/shard_map/ppermute | solution.py:631
  61.1 24.6 %collective-permute-start.8 = (bf16[2,128,384]{2,1,0:T(8,128)(2,1)}, bf16[2,128,384]{2,1,0:T(8,128)(2,1)S(1)}, u32[]{:S(2)}, u32[]{:S(2)}) collective-permute-start(bf16[2,128,384]{2,1,0:T(8,128)(2,1)} %get-tuple-element.111), channel_id=1, source_target_pairs={{0,3},{1,2},{2,1},{3,0},{4,7},{5,6},{6,5},{7,4},{8,11},{9,10},{10,... | collective-permute-start | bytes 589832 | tf_op jit(solution)/shard_map/ppermute | solution.py:631
  105.7 48.5 %all-to-all-start = ((bf16[4,5,128,384]{3,2,1,0:T(8,128)(2,1)}), bf16[4,5,128,384]{3,2,1,0:T(8,128)(2,1)S(1)}, u32[]{:S(2)}, u32[]{:S(2)}) async-start(bf16[4,5,128,384]{3,2,1,0:T(8,128)(2,1)} %get-tuple-element.123), calls=%async_computation | async-start | bytes 3932160 | tf_op jit(solution)/shard_map/all_to_all | solution.py:905
  109.6 12.1 %collective-permute-start.9 = (bf16[1792,384]{1,0:T(8,128)(2,1)}, bf16[1792,384]{1,0:T(8,128)(2,1)S(1)}, u32[]{:S(2)}, u32[]{:S(2)}) collective-permute-start(bf16[1792,384]{1,0:T(8,128)(2,1)} %get-tuple-element.125), channel_id=1, source_target_pairs={{0,4},{4,0},{8,12},{12,8},{16,20},{20,16},{24,28},{28,24},{1,5},{5... | collective-permute-start | bytes 4128776 | tf_op jit(solution)/shard_map/ppermute | solution.py:631
  121.1 10.6 %collective-permute-start.13 = (bf16[1792,128]{1,0:T(8,128)(2,1)}, bf16[1792,128]{1,0:T(8,128)(2,1)}, u32[]{:S(2)}, u32[]{:S(2)}) collective-permute-start(bf16[1792,128]{1,0:T(8,128)(2,1)} %get-tuple-element.138), channel_id=1, source_target_pairs={{0,4},{4,0},{8,12},{12,8},{16,20},{20,16},{24,28},{28,24},{1,5},{5... | collective-permute-start | bytes 1376264 | tf_op jit(solution)/shard_map/ppermute | solution.py:631
  126.2 28.0 %collective-permute-start.10 = (bf16[448,384]{1,0:T(8,128)(2,1)}, bf16[448,384]{1,0:T(8,128)(2,1)S(1)}, u32[]{:S(2)}, u32[]{:S(2)}) collective-permute-start(bf16[448,384]{1,0:T(8,128)(2,1)} %get-tuple-element.135), channel_id=1, source_target_pairs={{0,8},{4,12},{8,0},{12,4},{16,24},{20,28},{24,16},{28,20},{1,9},{5... | collective-permute-start | bytes 1032200 | tf_op jit(solution)/shard_map/ppermute | solution.py:631
  127.7 26.5 %collective-permute-start.11 = (bf16[448,384]{1,0:T(8,128)(2,1)}, bf16[448,384]{1,0:T(8,128)(2,1)S(1)}, u32[]{:S(2)}, u32[]{:S(2)}) collective-permute-start(bf16[448,384]{1,0:T(8,128)(2,1)} %get-tuple-element.136), channel_id=1, source_target_pairs={{0,16},{4,20},{8,24},{12,28},{16,0},{20,4},{24,8},{28,12},{1,17},{... | collective-permute-start | bytes 1032200 | tf_op jit(solution)/shard_map/ppermute | solution.py:631
  131.7 22.6 %collective-permute-start.12 = (bf16[448,384]{1,0:T(8,128)(2,1)}, bf16[448,384]{1,0:T(8,128)(2,1)S(1)}, u32[]{:S(2)}, u32[]{:S(2)}) collective-permute-start(bf16[448,384]{1,0:T(8,128)(2,1)} %get-tuple-element.137), channel_id=1, source_target_pairs={{0,24},{4,28},{8,16},{12,20},{16,8},{20,12},{24,0},{28,4},{1,25},{... | collective-permute-start | bytes 1032200 | tf_op jit(solution)/shard_map/ppermute | solution.py:631
  133.8 12.5 %collective-permute-start.14 = (bf16[448,128]{1,0:T(8,128)(2,1)}, bf16[448,128]{1,0:T(8,128)(2,1)S(1)}, u32[]{:S(2)}, u32[]{:S(2)}) collective-permute-start(bf16[448,128]{1,0:T(8,128)(2,1)} %get-tuple-element.140), channel_id=1, source_target_pairs={{0,8},{4,12},{8,0},{12,4},{16,24},{20,28},{24,16},{28,20},{1,9},{5... | collective-permute-start | bytes 344072 | tf_op jit(solution)/shard_map/ppermute | solution.py:631
  135.3 15.9 %collective-permute-start.15 = (bf16[448,128]{1,0:T(8,128)(2,1)}, bf16[448,128]{1,0:T(8,128)(2,1)S(1)}, u32[]{:S(2)}, u32[]{:S(2)}) collective-permute-start(bf16[448,128]{1,0:T(8,128)(2,1)} %get-tuple-element.141), channel_id=1, source_target_pairs={{0,16},{4,20},{8,24},{12,28},{16,0},{20,4},{24,8},{28,12},{1,17},{... | collective-permute-start | bytes 344072 | tf_op jit(solution)/shard_map/ppermute | solution.py:631
  146.3 7.9 %collective-permute-start.16 = (bf16[448,128]{1,0:T(8,128)(2,1)}, bf16[448,128]{1,0:T(8,128)(2,1)S(1)}, u32[]{:S(2)}, u32[]{:S(2)}) collective-permute-start(bf16[448,128]{1,0:T(8,128)(2,1)} %get-tuple-element.142), channel_id=1, source_target_pairs={{0,24},{4,28},{8,16},{12,20},{16,8},{20,12},{24,0},{28,4},{1,25},{... | collective-permute-start | bytes 344072 | tf_op jit(solution)/shard_map/ppermute | solution.py:631
  158.4 6.0 %collective-permute-start.17 = (bf16[112,512]{1,0:T(8,128)(2,1)}, bf16[112,512]{1,0:T(8,128)(2,1)S(1)}, u32[]{:S(2)}, u32[]{:S(2)}) collective-permute-start(bf16[112,512]{1,0:T(8,128)(2,1)} %get-tuple-element.144), channel_id=1, source_target_pairs={{0,1},{1,0},{2,3},{3,2},{4,5},{5,4},{6,7},{7,6},{8,9},{9,8},{10,11... | collective-permute-start | bytes 344072 | tf_op jit(solution)/shard_map/ppermute | solution.py:631
  160.4 10.4 %collective-permute-start.18 = (bf16[112,512]{1,0:T(8,128)(2,1)}, bf16[112,512]{1,0:T(8,128)(2,1)S(1)}, u32[]{:S(2)}, u32[]{:S(2)}) collective-permute-start(bf16[112,512]{1,0:T(8,128)(2,1)} %get-tuple-element.145), channel_id=1, source_target_pairs={{0,2},{1,3},{2,0},{3,1},{4,6},{5,7},{6,4},{7,5},{8,10},{9,11},{10,... | collective-permute-start | bytes 344072 | tf_op jit(solution)/shard_map/ppermute | solution.py:631
  162.8 8.0 %collective-permute-start.19 = (bf16[112,512]{1,0:T(8,128)(2,1)}, bf16[112,512]{1,0:T(8,128)(2,1)S(1)}, u32[]{:S(2)}, u32[]{:S(2)}) collective-permute-start(bf16[112,512]{1,0:T(8,128)(2,1)} %get-tuple-element.146), channel_id=1, source_target_pairs={{0,3},{1,2},{2,1},{3,0},{4,7},{5,6},{6,5},{7,4},{8,11},{9,10},{10,... | collective-permute-start | bytes 344072 | tf_op jit(solution)/shard_map/ppermute | solution.py:631
  173.3 7.9 %collective-permute-start.22 = (bf16[112,512]{1,0:T(8,128)(2,1)}, bf16[112,512]{1,0:T(8,128)(2,1)S(1)}, u32[]{:S(2)}, u32[]{:S(2)}) collective-permute-start(bf16[112,512]{1,0:T(8,128)(2,1)} %combine.5.refs_0_), channel_id=1, source_target_pairs={{0,3},{1,2},{2,1},{3,0},{4,7},{5,6},{6,5},{7,4},{8,11},{9,10},{10,... | collective-permute-start | bytes 344072 | tf_op jit(solution)/shard_map/ppermute | solution.py:631
  175.6 8.6 %collective-permute-start.21 = (bf16[112,512]{1,0:T(8,128)(2,1)}, bf16[112,512]{1,0:T(8,128)(2,1)S(1)}, u32[]{:S(2)}, u32[]{:S(2)}) collective-permute-start(bf16[112,512]{1,0:T(8,128)(2,1)} %combine.5.refs_0_), channel_id=1, source_target_pairs={{0,2},{1,3},{2,0},{3,1},{4,6},{5,7},{6,4},{7,5},{8,10},{9,11},{10,... | collective-permute-start | bytes 344072 | tf_op jit(solution)/shard_map/ppermute | solution.py:631
  176.5 7.8 %collective-permute-start.20 = (bf16[112,512]{1,0:T(8,128)(2,1)}, bf16[112,512]{1,0:T(8,128)(2,1)S(1)}, u32[]{:S(2)}, u32[]{:S(2)}) collective-permute-start(bf16[112,512]{1,0:T(8,128)(2,1)} %combine.5.refs_0_), channel_id=1, source_target_pairs={{0,1},{1,0},{2,3},{3,2},{4,5},{5,4},{6,7},{7,6},{8,9},{9,8},{10,11... | collective-permute-start | bytes 344072 | tf_op jit(solution)/shard_map/ppermute | solution.py:631
  186.8 25.5 %all-to-all-start.1 = ((bf16[4,1,128,384]{3,2,1,0:T(8,128)(2,1)}), bf16[4,1,128,384]{3,2,1,0:T(8,128)(2,1)S(1)}, u32[]{:S(2)}, u32[]{:S(2)}) async-start(bf16[4,1,128,384]{3,2,1,0:T(8,128)(2,1)} %get-tuple-element.148), calls=%async_computation.1 | async-start | bytes 786432 | tf_op jit(solution)/shard_map/all_to_all | solution.py:905
  190.4 14.6 %collective-permute-start.25 = (bf16[448,512]{1,0:T(8,128)(2,1)}, bf16[448,512]{1,0:T(8,128)(2,1)S(1)}, u32[]{:S(2)}, u32[]{:S(2)}) collective-permute-start(bf16[448,512]{1,0:T(8,128)(2,1)} %get-tuple-element.151.refs_0_), channel_id=1, source_target_pairs={{0,24},{4,28},{8,16},{12,20},{16,8},{20,12},{24,0},{28,4},{1,25},{... | collective-permute-start | bytes 1376264 | tf_op jit(solution)/shard_map/ppermute | solution.py:631
  192.9 18.9 %collective-permute-start.24 = (bf16[448,512]{1,0:T(8,128)(2,1)}, bf16[448,512]{1,0:T(8,128)(2,1)S(1)}, u32[]{:S(2)}, u32[]{:S(2)}) collective-permute-start(bf16[448,512]{1,0:T(8,128)(2,1)} %get-tuple-element.151.refs_0_), channel_id=1, source_target_pairs={{0,16},{4,20},{8,24},{12,28},{16,0},{20,4},{24,8},{28,12},{1,17},{... | collective-permute-start | bytes 1376264 | tf_op jit(solution)/shard_map/ppermute | solution.py:631
  193.6 18.7 %collective-permute-start.23 = (bf16[448,512]{1,0:T(8,128)(2,1)}, bf16[448,512]{1,0:T(8,128)(2,1)S(1)}, u32[]{:S(2)}, u32[]{:S(2)}) collective-permute-start(bf16[448,512]{1,0:T(8,128)(2,1)} %get-tuple-element.151.refs_0_), channel_id=1, source_target_pairs={{0,8},{4,12},{8,0},{12,4},{16,24},{20,28},{24,16},{28,20},{1,9},{5... | collective-permute-start | bytes 1376264 | tf_op jit(solution)/shard_map/ppermute | solution.py:631
  216.6 4.0 %collective-permute-start.26 = (bf16[1792,512]{1,0:T(8,128)(2,1)}, bf16[1792,512]{1,0:T(8,128)(2,1)S(1)}, u32[]{:S(2)}, u32[]{:S(2)}) collective-permute-start(bf16[1792,512]{1,0:T(8,128)(2,1)} %assemble.3.refs_0_), channel_id=1, source_target_pairs={{0,4},{4,0},{8,12},{12,8},{16,20},{20,16},{24,28},{28,24},{1,5},{5... | collective-permute-start | bytes 5505032 | tf_op jit(solution)/shard_map/ppermute | solution.py:631
  (39 other events, 139.7 us)
